TPU v7x, 32 devices: a whole 2x2x4 slice. The times are simulated.
32 devices in a mesh: row: 8 (over z, core), col: 4 (over y, x).
Axes of the slice: x: 2, y: 2, z: 4, core: 2. Of those that a mesh axis runs over, the one named last changes fastest.
Arguments:
- eigvec: float32 [16384, 8192], P('row', 'col'), may hold values from -6 to 6
- slots: float32 [4, 16384, 256], P('col', 'row'), may hold values from -0.046875 to 0.046875
- roots: int32 [3], replicated, may hold values from 0 to 3, as said below
- tfac: float32 [3, 256, 256], replicated, as said below
Outputs:
- transformed: float32 [16384, 8192], P('row', 'col')
Inputs may be any that keep to these rules, and one draw needn't show every extreme that they name: The panels lie in consecutive grid columns, roots[k] = (roots[0] + k) mod 4; roots[0] is one of the last two grid columns, so the panels always wrap past the last grid column. tfac[k] is upper triangular with a diagonal between 1 and 2.
All inputs are finite; a program needn't handle non-finite values.
Results may differ from a plain program's by a relative error of at most 0.00013.
Values sent between devices are 32-bit elements; how exact they have to be, the bound alone decides.
No kernel may reach another device: no remote copies, remote signals or barrier semaphores. Data moves between devices by JAX's collectives and lax.ppermute only.
A program may use at most 128 MiB of HBM per device.

v0:
```python
import functools

import jax
import jax.numpy as jnp
from jax import lax
from jax.experimental import pallas as pl
from jax.experimental.pallas import tpu as pltpu
from jax.sharding import PartitionSpec as P

PANELS = 3
BLOCK = 512
LAG = 1
PIECE = 512
MIB = 1024 * 1024
F32 = jnp.float32
BF16 = jnp.bfloat16
ANYWHERE = pl.BlockSpec(memory_space=pl.ANY)
IN_HBM = pl.BlockSpec(memory_space=pltpu.HBM)


def split(value):
    high = value.astype(BF16)
    return high, (value - high.astype(F32)).astype(BF16)


def dot(left, right):
    return jnp.dot(left, right, preferred_element_type=F32)


def dot_three(left, right):
    left_high, left_low = split(left)
    right_high, right_low = split(right)
    return dot(
        jnp.concatenate([left_high, left_low, left_high], axis=1),
        jnp.concatenate([right_high, right_high, right_low], axis=0),
    )


def params(mib):
    return pltpu.CompilerParams(vmem_limit_bytes=mib * MIB)


def cost(flops, count):
    return pl.CostEstimate(flops=flops // 64, bytes_accessed=count // 64, transcendentals=0)


def pinned(value):
    return pltpu.with_memory_space_constraint(value, memory_space=pltpu.HBM)


def split_kernel(x_ref, both_ref):
    blocks, _, _, width = both_ref.shape
    for index in range(blocks):
        both_ref[index, 0], both_ref[index, 1] = split(x_ref[:, index * width : (index + 1) * width])


def split_array(x, width):
    rows, columns = x.shape
    step, blocks = min(rows, 256), columns // width
    return pl.pallas_call(
        split_kernel,
        grid=(rows // step,),
        in_specs=[pl.BlockSpec((step, columns), lambda i: (i, 0))],
        out_specs=pl.BlockSpec((blocks, 2, step, width), lambda i: (0, 0, i, 0)),
        out_shape=pltpu.HBM((blocks, 2, rows, width), BF16),
        compiler_params=params(49),
        cost_estimate=cost(rows * columns * 4, rows * columns * 8),
        name="split_x",
    )(x)


def choose_kernel(outputs, count, which_ref, *refs):
    cases, (panel_ref, split_ref, sem) = refs[:count], refs[-3:]
    use = dict(zip(outputs, refs[-3 - len(outputs) :]))
    half = cases[0].shape[1]
    for side in range(2):
        for index, case in enumerate(cases):

            @pl.when(which_ref[side] == index)
            def _(case=case, side=side):
                copy = pltpu.make_async_copy(case, panel_ref.at[:, side * half : (side + 1) * half], sem)
                copy.start()
                copy.wait()

    rows, width = panel_ref.shape
    step = min(rows, 256)
    for start in range(0, rows, step):
        here = slice(start, start + step)
        value = panel_ref[here, :]
        if "both" in use:
            split_ref[0, 0, here, :], split_ref[0, 1, here, :] = split(value)
        if "flipped" in use:
            high, low = split(value.T)
            use["flipped"][:width, here] = high
            use["flipped"][width:, here] = low
    if "both" in use:
        copy = pltpu.make_async_copy(split_ref, use["both"], sem)
        copy.start()
        copy.wait()


def choose(cases, which, outputs, after=()):
    rows, half = cases[0].shape
    shapes = {"both": (1, 2, rows, 2 * half), "flipped": (4 * half, rows)}
    spaces = {"both": pltpu.HBM, "flipped": pltpu.VMEM}
    return pl.pallas_call(
        functools.partial(choose_kernel, outputs, len(cases)),
        in_specs=[pl.BlockSpec(memory_space=pltpu.SMEM)] + [ANYWHERE] * (len(cases) + len(after)),
        out_specs=[pl.BlockSpec(memory_space=spaces[name]) for name in outputs],
        out_shape=[spaces[name](shapes[name], BF16) for name in outputs],
        scratch_shapes=[
            pltpu.VMEM((rows, 2 * half), F32),
            pltpu.VMEM(shapes["both"], BF16),
            pltpu.SemaphoreType.DMA,
        ],
        compiler_params=params(14),
        cost_estimate=cost(rows * half * 8, rows * half * 24),
        name="choose_panel",
    )(which, *cases, *after)


def products_kernel(block, flipped_ref, both_ref, *refs):
    keep_ref, send_ref, block_ref, sems = refs[-4:]
    half = keep_ref.shape[0]
    rows = block_ref.shape[1] // 2
    copies = []
    for index in range(2):
        here = slice(index * rows, (index + 1) * rows)
        for side in range(2):
            source, target = both_ref.at[block, side, here], block_ref.at[side, here]
            copies.append(pltpu.make_async_copy(source, target, sems.at[index, side]))
            copies[-1].start()
    total = None
    for index in range(2):
        here = slice(index * rows, (index + 1) * rows)
        copies[2 * index].wait()
        with_high = dot(flipped_ref[:, here], block_ref[0, here, :])
        copies[2 * index + 1].wait()
        with_low = dot(flipped_ref[: 2 * half, here], block_ref[1, here, :])
        part = with_high[: 2 * half] + (with_high[2 * half :] + with_low)
        total = part if total is None else total + part
    keep_ref[...] = total[:half]
    send_ref[...] = total[half:]


def products(flipped, both, block, after=()):
    rows, width = both.shape[2:]
    half = flipped.shape[0] // 4
    in_vmem = pl.BlockSpec(memory_space=pltpu.VMEM)
    return pl.pallas_call(
        functools.partial(products_kernel, block),
        in_specs=[in_vmem, IN_HBM] + [ANYWHERE] * len(after),
        out_specs=[in_vmem] * 2,
        out_shape=[jax.ShapeDtypeStruct((half, width), F32)] * 2,
        scratch_shapes=[pltpu.VMEM((2, rows, width), BF16), pltpu.SemaphoreType.DMA((2, 2))],
        compiler_params=params(16),
        cost_estimate=cost(2 * 6 * half * rows * width, rows * width * 4 + 8 * half * rows),
        name="products",
    )(flipped, pinned(both), *after)


def update_kernel(place_ref, *refs):
    sums = refs[:6]
    tfac_ref, gram_ref = refs[6:8]
    panel_refs, x_ref = refs[8:11], refs[11]
    out_ref, done_ref, w_ref, y_ref, y_split_ref = refs[-5:]
    half = sums[0].shape[0]
    width = 2 * half

    @pl.when(pl.program_id(0) == 0)
    def _():
        for index, piece in enumerate(sums):
            start = pl.multiple_of(place_ref[index] * half, half)
            w_ref[pl.ds(start, half), :] = piece[:, : w_ref.shape[1]]
        first = dot_three(tfac_ref[0], w_ref[:width, :])
        y_ref[:width, :] = first
        second = dot_three(tfac_ref[1], w_ref[width : 2 * width, :] - dot_three(gram_ref[0], first))
        y_ref[width : 2 * width, :] = second
        third = w_ref[2 * width :, :] - dot_three(gram_ref[1], first) - dot_three(gram_ref[2], second)
        y_ref[2 * width :, :] = dot_three(tfac_ref[2], third)
        for index in range(6):
            start = pl.multiple_of(place_ref[index] * half, half)
            high, low = split(y_ref[pl.ds(start, half), :])
            for number, value in enumerate((high, high, low)):
                y_split_ref[(6 * number + index) * half : (6 * number + index + 1) * half, :] = value

    sides = [ref[0, side] for side in (0, 1, 0) for ref in panel_refs]
    out_ref[...] = x_ref[...] - dot(jnp.concatenate(sides, axis=1), y_split_ref[...])
    done_ref[...] = jnp.zeros(done_ref.shape, F32)


def update(place, sums, tfac, grams, panels, x, out, block, width):
    rows, columns = x.shape
    half = sums[0].shape[0]
    step = min(rows, 512)
    panel_spec = pl.BlockSpec((1, 2, step, 2 * half), lambda i, place: (0, 0, i, 0))
    block_spec = pl.BlockSpec((step, width), lambda i, place: (i, block))
    operands = [place, *sums, tfac, grams, *map(pinned, panels), x]
    in_specs = (
        [pl.BlockSpec(memory_space=pltpu.VMEM)] * 8
        + [panel_spec] * 3
        + [block_spec]
    )
    aliases = {}
    if out is not None:
        aliases = {len(operands): 0}
        operands.append(out)
        in_specs.append(IN_HBM)
    return pl.pallas_call(
        update_kernel,
        grid_spec=pltpu.PrefetchScalarGridSpec(
            num_scalar_prefetch=1,
            grid=(rows // step,),
            in_specs=in_specs,
            out_specs=[block_spec, pl.BlockSpec((8, 128), lambda i, place: (0, 0))],
            scratch_shapes=[
                pltpu.VMEM((6 * half, width), F32),
                pltpu.VMEM((6 * half, width), F32),
                pltpu.VMEM((18 * half, width), BF16),
            ],
        ),
        out_shape=[jax.ShapeDtypeStruct(x.shape, F32), jax.ShapeDtypeStruct((8, 128), F32)],
        input_output_aliases=aliases,
        compiler_params=params(40),
        cost_estimate=cost(2 * 18 * half * rows * width, rows * width * 8 + rows * half * 24),
        name="update",
    )(*operands)


def pairs_of(count, step):
    return [(index, index ^ step) for index in range(count)]


def swap_cores(value):
    return lax.ppermute(value, "row", pairs_of(lax.axis_size("row"), 1))


def both_cores(chip_pairs):
    return [(2 * a + core, 2 * b + core) for a, b in chip_pairs for core in range(2)]


def sum_over_rows(keep, send):
    chips = lax.axis_size("row") // 2
    chip = lax.axis_index("row") // 2
    total = keep + swap_cores(send)
    for hop in range(chips // 2 - 1):
        pairs = [(hop, hop + 1), (chips - 1 - hop, chips - 2 - hop)]
        total = total + lax.ppermute(total, "row", both_cores(pairs))
    middle = [(chips // 2 - 1, chips // 2), (chips // 2, chips // 2 - 1)]
    total = total + lax.ppermute(total, "row", both_cores(middle))
    for hop in reversed(range(chips // 2 - 1)):
        pairs = [(hop + 1, hop), (chips - 2 - hop, chips - 1 - hop)]
        arrived = lax.ppermute(total, "row", both_cores(pairs))
        total = jnp.where((chip == hop) | (chip == chips - 1 - hop), arrived, total)
    return total, swap_cores(total)


def pick(index, *cases):
    return lax.select_n(index, *cases)


def fetch_square(slot, roots):
    half = slot.shape[1] // 2
    me = lax.axis_index("col")
    along = lambda value, step: lax.ppermute(value, "col", pairs_of(4, step))
    own = [slot[:, :half], slot[:, half:]]
    near, far = [], []
    for piece in own:
        near.append(along(piece, 1))
        far.append(along(piece, 2))
    cross = [along(far[0], 1), along(near[1], 2)]
    spare = (roots[0] + 3) % 4
    case = me ^ spare
    rounds = [
        ((*own, near[0], far[0]), jnp.array([[2, 3], [0, 1], [0, 1], [0, 1]], jnp.int32)[case]),
        ((*near, *far), jnp.array([[1, 3], [2, 3], [0, 1], [0, 2]], jnp.int32)[case]),
        ((*cross, near[1], far[1]), jnp.array([[0, 1], [0, 1], [0, 1], [2, 3]], jnp.int32)[case]),
    ]
    slots = jnp.array([[1, 2, 1, 2, 3, 3], [0, 0, 2, 2, 3, 3], [0, 0, 1, 1, 3, 3], [0, 0, 1, 2, 1, 2]], jnp.int32)
    halves = jnp.array([[0, 0, 1, 1, 0, 1], [0, 1, 0, 1, 0, 1], [0, 1, 0, 1, 0, 1], [0, 1, 0, 0, 1, 1]], jnp.int32)
    panel = ((slots[case] ^ me) - roots[0]) % 4
    places = panel * 2 + halves[case]
    later_of = jnp.array([[0, 1, 0, 0], [1, 0, 2, 2]], jnp.int32)[roots[0] - 2, me]
    earlier_of = jnp.array([[2, 2, 0, 1], [0, 0, 1, 0]], jnp.int32)[roots[0] - 2, me]
    both = jnp.arange(2, dtype=jnp.int32)
    later = ((*own, *near, *far), 2 * later_of + both)
    earlier = ((*own, *near, *far), 2 * earlier_of + both)
    holders = jnp.array([[3, 0, 1], [2, 3, 0]], jnp.int32)[roots[0] - 2]
    return rounds, places, later, earlier, holders


def fetch_any(slot, roots):
    half = slot.shape[1] // 2
    me = lax.axis_index("col")
    panels = [lax.psum(jnp.where(me == roots[index], slot, jnp.zeros_like(slot)), "col") for index in range(PANELS)]
    rounds = [(panel[:, :half], panel[:, half:]) for panel in panels]
    return rounds, jnp.arange(2 * PANELS, dtype=jnp.int32), panels


def gram(left, right):
    return lax.dot_general(
        left, right, (((0,), (0,)), ((), ())), precision=lax.Precision.HIGH, preferred_element_type=F32
    )


def exchange_kernel(names, pieces, ends_ref, *refs):
    use = dict(zip(names, refs))
    end = ends_ref[0] == 1
    if "acc" in use:
        start = 0
        for index in range(pieces):
            keep, swapped = use["keep", index], use["swapped", index]
            columns = slice(start, start + keep.shape[1])
            use["acc"][:, columns] = keep[...] + swapped[...]
            start = columns.stop
    if "part" in use:
        columns = use["part"].shape[1]
        use["part"][...] = use["acc_before"][...] + use["outer"][:, :columns]
    if "total" in use:
        use["total"][...] = use["part_before"][...] + use["inner"][...]
    if "final" in use:
        columns = use["final"].shape[1]
        use["final"][...] = jnp.where(end, use["outer"][:, :columns], use["total_before"][...])
    if "out" in use:
        sources = [use[name] for name in ("acc", "total") if name in use]
        if len(sources) == 1:
            use["out"][...] = sources[0][...]
        else:
            both = min(source.shape[1] for source in sources)
            use["out"][:, :both] = jnp.where(end, sources[0][:, :both], sources[1][:, :both])
            for source in sources:
                if source.shape[1] > both:
                    use["out"][:, both:] = source[:, both:]


def exchange(ends, operands, shapes, after):
    names = list(operands) + [None] * len(after) + list(shapes)
    pieces = sum(name[0] == "keep" for name in operands)
    in_vmem = pl.BlockSpec(memory_space=pltpu.VMEM)
    results = pl.pallas_call(
        functools.partial(exchange_kernel, names, pieces),
        in_specs=[pl.BlockSpec(memory_space=pltpu.SMEM)] + [in_vmem] * len(operands)
        + [ANYWHERE] * len(after),
        out_specs=[in_vmem] * len(shapes),
        out_shape=[jax.ShapeDtypeStruct(shape, F32) for shape in shapes.values()],
        compiler_params=params(14),
        cost_estimate=cost(0, 0),
        name="exchange",
    )(ends, *operands.values(), *after)
    return dict(zip(shapes, results))


def shards_square(eigvec, slot, roots, tfac):
    columns = eigvec.shape[1]
    width, half = columns // 2, slot.shape[1] // 2
    rounds, places, later, earlier, holders = fetch_square(slot, roots)
    chip, core = lax.axis_index("row") // 2, lax.axis_index("row") % 2
    ends = jnp.where((chip == 0) | (chip == 3), 1, 0).astype(jnp.int32).reshape(1)
    places = jnp.where(core == 0, places, places.reshape(PANELS, 2)[:, ::-1].reshape(-1))
    ordered = lambda pair: jnp.where(core == 0, pair, pair[::-1])
    x_both = split_array(eigvec, PIECE)
    chunks = [(index, block) for index in range(PANELS) for block in range(columns // width)]
    count = len(chunks)
    gram_chunk = 2
    prepared, arrived, sizes, gram_sides = {}, {}, {}, []

    def start(number, after):
        index, block = chunks[number]
        pieces = []
        if index not in prepared:
            cases, which = rounds[index]
            prepared[index] = choose(cases, ordered(which), ("both", "flipped"), after)
        for part in range(width // PIECE):
            pieces.append(products(prepared[index][1], x_both, block * (width // PIECE) + part, after))
        if number == gram_chunk - 1:
            gram_sides.append(choose(later[0], ordered(later[1]), ("flipped",), after)[0])
            gram_sides.append(choose(*earlier, ("both",), after)[0])
        if number == gram_chunk:
            pieces.append(products(*gram_sides, 0, after))
        arrived[number] = [(mine, swap_cores(other)) for mine, other in pieces]
        sizes[number] = (half, sum(mine.shape[1] for mine, other in pieces))

    outer_pairs = both_cores([(0, 1), (1, 0), (2, 3), (3, 2)])
    inner_pairs = both_cores([(1, 2), (2, 1)])
    acc, part, total, outer, inner, sums = {}, {}, {}, {}, {}, {}
    grams, out = None, None
    start(0, ())
    for step in range(count + 3 * LAG):
        operands, shapes = {}, {}
        inward, middle, outward = step - LAG, step - 2 * LAG, step - 3 * LAG
        if step < count:
            for number, (mine, other) in enumerate(arrived[step]):
                operands["keep", number], operands["swapped", number] = mine, other
            shapes["acc"] = sizes[step]
        if step - LAG in outer:
            operands["outer"] = outer[step - LAG]
        if 0 <= inward < count:
            operands["acc_before"] = acc[inward]
            shapes["part"] = sizes[inward]
        if 0 <= middle < count:
            operands["part_before"], operands["inner"] = part[middle], inner[step - LAG]
            shapes["total"] = sizes[middle]
        if 0 <= outward < count:
            operands["total_before"] = total[outward]
            shapes["final"] = sizes[outward]
        sent = [shapes[name] for name in ("acc", "total") if name in shapes]
        if sent:
            shapes["out"] = max(sent, key=lambda shape: shape[1])
        ahead = [] if out is None else [finished]
        if step + 1 == chunks.index((PANELS - 1, 0)):
            ahead.extend(rounds[-1][0][:2])
        if step == gram_chunk - 1:
            ahead.extend(gram_sides)
        if step == count + 1:
            ahead.append(grams)
        if 0 <= outward - 1 < count - 2:
            ahead.append(sums[chunks[outward - 1]][1])
        results = exchange(ends, operands, shapes, ahead)
        if "out" in results:
            outer[step] = lax.ppermute(results["out"], "row", outer_pairs)
        if "acc" in results:
            acc[step] = results["acc"]
        if "part" in results:
            part[inward] = results["part"]
            inner[step] = lax.ppermute(results["part"], "row", inner_pairs)
        if "total" in results:
            total[middle] = results["total"]
        if step + 1 < count:
            start(step + 1, [next(iter(results.values()))])
        if "final" in results:
            done = outward
            own, other = results["final"], swap_cores(results["final"])
            if done == gram_chunk:
                pair = own[:, width:], other[:, width:]
                block = jnp.where(core == 0, jnp.concatenate(pair, axis=0), jnp.concatenate(pair[::-1], axis=0))
                spread = [block] + [lax.ppermute(block, "col", pairs_of(4, shift)) for shift in range(1, 4)]
                places_of = holders ^ lax.axis_index("col")
                grams = jnp.stack([pick(places_of[number], *spread) for number in range(PANELS)])
            sums[chunks[done]] = (own, other)
            index, block = chunks[done]
            if index == PANELS - 1:
                pieces = [piece for panel in range(PANELS) for piece in sums[panel, block]]
                panels = [prepared[panel][0] for panel in range(PANELS)]
                out, finished = update(places, pieces, tfac, grams, panels, eigvec, out, block, width)
    return out


def shards(eigvec, slots, roots, tfac):
    if lax.axis_size("col") == 4 and lax.axis_size("row") == 8:
        return shards_square(eigvec, slots[0], roots, tfac)
    columns = eigvec.shape[1]
    width = min(columns, BLOCK)
    rounds, places, panels = fetch_any(slots[0], roots)
    core = lax.axis_index("row") % 2
    places = jnp.where(core == 0, places, places.reshape(PANELS, 2)[:, ::-1].reshape(-1))
    x_both = split_array(eigvec, width)
    prepared, sums = [], []
    for pair in rounds:
        which = jnp.where(core == 0, jnp.arange(2), jnp.arange(1, -1, -1)).astype(jnp.int32)
        prepared.append(choose(pair, which, ("both", "flipped")))
        sums.append([
            sum_over_rows(*products(prepared[-1][1], x_both, block)) for block in range(columns // width)
        ])
    grams = jnp.stack([gram(panels[1], panels[0]), gram(panels[2], panels[0]), gram(panels[2], panels[1])])
    grams = lax.psum(grams, "row")
    out = None
    for block in range(columns // width):
        pieces = [piece for index in range(PANELS) for piece in sums[index][block]]
        out, _ = update(places, pieces, tfac, grams, [both for both, _ in prepared], eigvec, out, block, width)
    return out


def solution(mesh):
    in_specs = (P("row", "col"), P("col", "row", None), P(), P())
    out_specs = P("row", "col")
    return jax.shard_map(shards, mesh=mesh, in_specs=in_specs, out_specs=out_specs, check_vma=False)
```

profile of v0, /device:TPU:0, one launch (start us, length us, event | category | flops | bytes accessed | tf_op | source)
XLA Modules:
  0.0 231.8 jit_solution(9256212952754301153)
XLA Ops:
  0.0 3.0 %fusion.14 = (f32[2048,128]{1,0:T(8,128)}, f32[2048,128]{1,0:T(8,128)}) fusion(f32[2048,256]{1,0:T(8,128)} %bitcast.37), kind=kLoop, calls=%fused_computation.37 | loop fusion | bytes 4194304 | tf_op jit(solution)/shard_map/slice | solution.py:266
  3.0 2.9 %collective-permute-start.5 = (f32[2048,128]{1,0:T(8,128)}, f32[2048,128]{1,0:T(8,128)S(1)}, u32[]{:S(2)}, u32[]{:S(2)}) collective-permute-start(f32[2048,128]{1,0:T(8,128)} %get-tuple-element.138.refs_0_), channel_id=1, source_target_pairs={{0,1},{1,0},{2,3},{3,2},{4,5},{5,4},{6,7},{7,6},{8,9},{9,8},{10,11... | collective-permute-start | bytes 3145736 | tf_op jit(solution)/shard_map/ppermute | solution.py:265
  5.9 1.5 collective-permute-start
  8.0 14.6 %split_x.1.both_ref = bf16[4,2,2048,512]{3,2,1,0:T(8,128)(2,1)} custom-call(f32[2048,2048]{1,0:T(8,128)} %refs_11_.3), custom_call_target="tpu_custom_call" | custom-call | flops 262144 | bytes 524288 | tf_op jit(solution)/shard_map/split_x/pallas_call | solution.py:60
  22.8 7.3 %collective-permute-done.5.refs_2_.refs_0_ = f32[2048,128]{1,0:T(8,128)S(1)} collective-permute-done((f32[2048,128]{1,0:T(8,128)}, f32[2048,128]{1,0:T(8,128)S(1)}, u32[]{:S(2)}, u32[]{:S(2)}) %collective-permute-start.5) | collective-permute-done | bytes 1048608 | tf_op jit(solution)/shard_map/ppermute | solution.py:265
  30.1 1.0 copy-done.4
  31.1 1.1 collective-permute-done.refs_3_.refs_4_.refs_2_
  32.2 1.0 copy-done.1
  33.2 1.2 copy-done.2
  34.4 1.2 copy-done.5
  35.7 4.9 %choose_panel.5 = (bf16[1,2,2048,256]{3,2,1,0:T(8,128)(2,1)}, bf16[512,2048]{1,0:T(8,128)(2,1)S(1)}) custom-call(s32[2]{0:T(128)S(1)} %broadcast_select_fusion.1.which_ref, f32[2048,128]{1,0:T(8,128)} %get-tuple-element.138.refs_0_, f32[2048,128]{1,0:T(8,128)} %get-tuple-element.137.refs_1_, f32[2048,128]{1,0:T(8,128)S(1)} %copy-done.5, ...), custom_call_target="tpu_custom_call" | custom-call | flops 32768 | bytes 98304 | tf_op jit(solution)/shard_map/choose_panel/pallas_call | solution.py:106
  40.5 3.9 %products.14 = (f32[128,512]{1,0:T(8,128)S(1)}, f32[128,512]{1,0:T(8,128)}) custom-call(bf16[512,2048]{1,0:T(8,128)(2,1)S(1)} %get-tuple-element.71.flipped_ref, bf16[4,2,2048,512]{3,2,1,0:T(8,128)(2,1)} %split_x.1.both_ref), custom_call_target="tpu_custom_call" | custom-call | flops 25165824 | bytes 98304 | tf_op jit(solution)/shard_map/products/pallas_call | solution.py:150
  44.5 3.9 %products.13 = (f32[128,512]{1,0:T(8,128)S(1)}, f32[128,512]{1,0:T(8,128)}) custom-call(bf16[512,2048]{1,0:T(8,128)(2,1)S(1)} %get-tuple-element.71.flipped_ref, bf16[4,2,2048,512]{3,2,1,0:T(8,128)(2,1)} %split_x.1.both_ref), custom_call_target="tpu_custom_call" | custom-call | flops 25165824 | bytes 98304 | tf_op jit(solution)/shard_map/products/pallas_call | solution.py:150
  51.3 0.9 copy-done.25
  52.2 1.1 exchange.9
  53.4 1.6 collective-permute-start.10
  55.1 3.2 %products.16 = (f32[128,512]{1,0:T(8,128)S(1)}, f32[128,512]{1,0:T(8,128)S(1)}) custom-call(bf16[512,2048]{1,0:T(8,128)(2,1)S(1)} %get-tuple-element.71.flipped_ref, bf16[4,2,2048,512]{3,2,1,0:T(8,128)(2,1)} %split_x.1.both_ref, f32[128,1024]{1,0:T(8,128)S(1)} %get-tuple-element.76.refs_0_.refs_6_.refs_5_), custom_call_target="tpu_custom_call" | custom-call | flops 25165824 | bytes 98304 | tf_op jit(solution)/shard_map/products/pallas_call | solution.py:150
  58.4 3.3 %products.15 = (f32[128,512]{1,0:T(8,128)S(1)}, f32[128,512]{1,0:T(8,128)S(1)}) custom-call(bf16[512,2048]{1,0:T(8,128)(2,1)S(1)} %get-tuple-element.71.flipped_ref, bf16[4,2,2048,512]{3,2,1,0:T(8,128)(2,1)} %split_x.1.both_ref, f32[128,1024]{1,0:T(8,128)S(1)} %get-tuple-element.76.refs_0_.refs_6_.refs_5_), custom_call_target="tpu_custom_call" | custom-call | flops 25165824 | bytes 98304 | tf_op jit(solution)/shard_map/products/pallas_call | solution.py:150
  63.3 4.6 %choose_panel.7.refs_7_.both_ref = bf16[1,2,2048,256]{3,2,1,0:T(8,128)(2,1)} custom-call(s32[2]{0:T(128)S(1)} %iota_add_fusion.which_ref, f32[2048,128]{1,0:T(8,128)} %get-tuple-element.138.refs_0_, f32[2048,128]{1,0:T(8,128)} %get-tuple-element.137.refs_1_, f32[2048,128]{1,0:T(8,128)S(1)} %copy-done.6, ...), custom_call_target="tpu_custom_call" | custom-call | flops 32768 | bytes 98304 | tf_op jit(solution)/shard_map/choose_panel/pallas_call | solution.py:106
  67.9 1.5 choose_panel.6.refs_6_.flipped_ref
  69.6 2.6 %choose_panel.8 = (bf16[1,2,2048,256]{3,2,1,0:T(8,128)(2,1)}, bf16[512,2048]{1,0:T(8,128)(2,1)S(1)}) custom-call(s32[2]{0:T(128)S(1)} %broadcast_select_fusion.2.which_ref, f32[2048,128]{1,0:T(8,128)S(1)} %copy-done.6, f32[2048,128]{1,0:T(8,128)S(1)} %collective-permute-done.2.refs_3_.refs_1_.refs_2_, f32[2048,128]{1,0:T(8,128)S(1)} %copy-done.3, ...), custom_call_target="tpu_custom_call" | custom-call | flops 32768 | bytes 98304 | tf_op jit(solution)/shard_map/choose_panel/pallas_call | solution.py:106
  72.3 3.2 %products.18 = (f32[128,512]{1,0:T(8,128)S(1)}, f32[128,512]{1,0:T(8,128)S(1)}) custom-call(bf16[512,2048]{1,0:T(8,128)(2,1)S(1)} %get-tuple-element.83.flipped_ref, bf16[4,2,2048,512]{3,2,1,0:T(8,128)(2,1)} %split_x.1.both_ref, f32[128,1024]{1,0:T(8,128)S(1)} %get-tuple-element.82.refs_4_.refs_0_.refs_7_), custom_call_target="tpu_custom_call" | custom-call | flops 25165824 | bytes 98304 | tf_op jit(solution)/shard_map/products/pallas_call | solution.py:150
  75.7 3.0 %products.19 = (f32[128,256]{1,0:T(8,128)S(1)}, f32[128,256]{1,0:T(8,128)S(1)}) custom-call(bf16[512,2048]{1,0:T(8,128)(2,1)S(1)} %choose_panel.6.refs_6_.flipped_ref, bf16[1,2,2048,256]{3,2,1,0:T(8,128)(2,1)} %choose_panel.7.refs_7_.both_ref, f32[128,1024]{1,0:T(8,128)S(1)} %get-tuple-element.82.refs_4_.refs_0_.refs_7_), custom_call_target="tpu_custom_call" | custom-call | flops 12582912 | bytes 65536 | tf_op jit(solution)/shard_map/products/pallas_call | solution.py:150
  79.3 0.9 collective-permute-start.15
  80.3 1.3 collective-permute-done.13.refs_5_
  81.6 4.7 %collective-permute-start.1 = (f32[2048,128]{1,0:T(8,128)S(1)}, f32[2048,128]{1,0:T(8,128)S(1)}, u32[]{:S(2)}, u32[]{:S(2)}) collective-permute-start(f32[2048,128]{1,0:T(8,128)S(1)} %copy-done.3), channel_id=1, source_target_pairs={{0,1},{1,0},{2,3},{3,2},{4,5},{5,4},{6,7},{7,6},{8,9},{9,8},{10,11... | collective-permute-start | bytes 3145736 | tf_op jit(solution)/shard_map/ppermute | solution.py:265
  86.3 3.2 %products.17 = (f32[128,512]{1,0:T(8,128)S(1)}, f32[128,512]{1,0:T(8,128)S(1)}) custom-call(bf16[512,2048]{1,0:T(8,128)(2,1)S(1)} %get-tuple-element.83.flipped_ref, bf16[4,2,2048,512]{3,2,1,0:T(8,128)(2,1)} %split_x.1.both_ref, f32[128,1024]{1,0:T(8,128)S(1)} %get-tuple-element.82.refs_4_.refs_0_.refs_7_), custom_call_target="tpu_custom_call" | custom-call | flops 25165824 | bytes 98304 | tf_op jit(solution)/shard_map/products/pallas_call | solution.py:150
  89.6 1.5 collective-permute-done.11.refs_1_
  91.1 1.9 collective-permute-done.14.refs_6_
  93.3 3.7 %collective-permute-start.18 = (f32[128,1280]{1,0:T(8,128)S(1)}, f32[128,1280]{1,0:T(8,128)S(1)}, u32[]{:S(2)}, u32[]{:S(2)}) collective-permute-start(f32[128,1280]{1,0:T(8,128)S(1)} %get-tuple-element.97), channel_id=1, source_target_pairs={{0,8},{4,12},{8,0},{12,4},{16,24},{20,28},{24,16},{28,20},{1,9},{5... | collective-permute-start | bytes 1966088 | tf_op jit(solution)/shard_map/ppermute | solution.py:420
  97.7 3.2 %products.21 = (f32[128,512]{1,0:T(8,128)S(1)}, f32[128,512]{1,0:T(8,128)S(1)}) custom-call(bf16[512,2048]{1,0:T(8,128)(2,1)S(1)} %get-tuple-element.83.flipped_ref, bf16[4,2,2048,512]{3,2,1,0:T(8,128)(2,1)} %split_x.1.both_ref, f32[128,1280]{1,0:T(8,128)S(1)} %get-tuple-element.92.refs_0_.refs_5_), custom_call_target="tpu_custom_call" | custom-call | flops 25165824 | bytes 98304 | tf_op jit(solution)/shard_map/products/pallas_call | solution.py:150
  101.0 3.2 %products.20 = (f32[128,512]{1,0:T(8,128)S(1)}, f32[128,512]{1,0:T(8,128)S(1)}) custom-call(bf16[512,2048]{1,0:T(8,128)(2,1)S(1)} %get-tuple-element.83.flipped_ref, bf16[4,2,2048,512]{3,2,1,0:T(8,128)(2,1)} %split_x.1.both_ref, f32[128,1280]{1,0:T(8,128)S(1)} %get-tuple-element.92.refs_0_.refs_5_), custom_call_target="tpu_custom_call" | custom-call | flops 25165824 | bytes 98304 | tf_op jit(solution)/shard_map/products/pallas_call | solution.py:150
  104.8 5.0 %collective-permute-done.1.refs_9_.refs_0_ = f32[2048,128]{1,0:T(8,128)S(1)} collective-permute-done((f32[2048,128]{1,0:T(8,128)S(1)}, f32[2048,128]{1,0:T(8,128)S(1)}, u32[]{:S(2)}, u32[]{:S(2)}) %collective-permute-start.1) | collective-permute-done | bytes 1048608 | tf_op jit(solution)/shard_map/ppermute | solution.py:265
  109.8 1.3 collective-permute-done.18.refs_4_
  111.1 1.3 exchange.12
  113.2 1.5 collective-permute-start.23
  114.7 4.2 %collective-permute-start.22 = (f32[128,1024]{1,0:T(8,128)}, f32[128,1024]{1,0:T(8,128)}, u32[]{:S(2)}, u32[]{:S(2)}) collective-permute-start(f32[128,1024]{1,0:T(8,128)} %get-tuple-element.106), channel_id=1, source_target_pairs={{0,8},{4,12},{8,0},{12,4},{16,24},{20,28},{24,16},{28,20},{1,9},{5... | collective-permute-start | bytes 1572872 | tf_op jit(solution)/shard_map/ppermute | solution.py:420
  119.0 1.2 copy-done.8
  120.3 1.2 copy-done.10
  121.5 2.6 %choose_panel.9 = (bf16[1,2,2048,256]{3,2,1,0:T(8,128)(2,1)}, bf16[512,2048]{1,0:T(8,128)(2,1)S(1)}) custom-call(s32[2]{0:T(128)S(1)} %broadcast_select_fusion.3.which_ref, f32[2048,128]{1,0:T(8,128)S(1)} %copy-done.10, f32[2048,128]{1,0:T(8,128)S(1)} %copy-done.8, f32[2048,128]{1,0:T(8,128)S(1)} %collective-permute-done.2.refs_3_.refs_1_.refs_2_, ...), custom_call_target="tpu_custom_call" | custom-call | flops 32768 | bytes 98304 | tf_op jit(solution)/shard_map/choose_panel/pallas_call | solution.py:106
  124.1 3.2 %products.23 = (f32[128,512]{1,0:T(8,128)S(1)}, f32[128,512]{1,0:T(8,128)S(1)}) custom-call(bf16[512,2048]{1,0:T(8,128)(2,1)S(1)} %get-tuple-element.101.flipped_ref, bf16[4,2,2048,512]{3,2,1,0:T(8,128)(2,1)} %split_x.1.both_ref, f32[128,1024]{1,0:T(8,128)S(1)} %get-tuple-element.100.refs_4_.refs_0_.refs_5_), custom_call_target="tpu_custom_call" | custom-call | flops 25165824 | bytes 98304 | tf_op jit(solution)/shard_map/products/pallas_call | solution.py:150
  127.9 3.2 %products.22 = (f32[128,512]{1,0:T(8,128)S(1)}, f32[128,512]{1,0:T(8,128)S(1)}) custom-call(bf16[512,2048]{1,0:T(8,128)(2,1)S(1)} %get-tuple-element.101.flipped_ref, bf16[4,2,2048,512]{3,2,1,0:T(8,128)(2,1)} %split_x.1.both_ref, f32[128,1024]{1,0:T(8,128)S(1)} %get-tuple-element.100.refs_4_.refs_0_.refs_5_), custom_call_target="tpu_custom_call" | custom-call | flops 25165824 | bytes 98304 | tf_op jit(solution)/shard_map/products/pallas_call | solution.py:150
  131.3 1.5 collective-permute-done.20.refs_1_
  132.8 1.9 exchange.13
  134.8 2.0 collective-permute-start.28
  137.5 3.2 %products.25 = (f32[128,512]{1,0:T(8,128)S(1)}, f32[128,512]{1,0:T(8,128)S(1)}) custom-call(bf16[512,2048]{1,0:T(8,128)(2,1)S(1)} %get-tuple-element.101.flipped_ref, bf16[4,2,2048,512]{3,2,1,0:T(8,128)(2,1)} %split_x.1.both_ref, f32[128,1024]{1,0:T(8,128)S(1)} %get-tuple-element.111.refs_0_.refs_5_), custom_call_target="tpu_custom_call" | custom-call | flops 25165824 | bytes 98304 | tf_op jit(solution)/shard_map/products/pallas_call | solution.py:150
  141.3 3.2 %products.24 = (f32[128,512]{1,0:T(8,128)S(1)}, f32[128,512]{1,0:T(8,128)S(1)}) custom-call(bf16[512,2048]{1,0:T(8,128)(2,1)S(1)} %get-tuple-element.101.flipped_ref, bf16[4,2,2048,512]{3,2,1,0:T(8,128)(2,1)} %split_x.1.both_ref, f32[128,1024]{1,0:T(8,128)S(1)} %get-tuple-element.111.refs_0_.refs_5_), custom_call_target="tpu_custom_call" | custom-call | flops 25165824 | bytes 98304 | tf_op jit(solution)/shard_map/products/pallas_call | solution.py:150
  144.7 1.5 collective-permute-done.26.refs_1_
  146.2 5.4 %collective-permute-done.28.refs_4_ = f32[128,1280]{1,0:T(8,128)S(1)} collective-permute-done((f32[128,1280]{1,0:T(8,128)S(1)}, f32[128,1280]{1,0:T(8,128)S(1)}, u32[]{:S(2)}, u32[]{:S(2)}) %collective-permute-start.28) | collective-permute-done | bytes 655392 | tf_op jit(solution)/shard_map/ppermute | solution.py:420
  152.0 1.6 collective-permute-start.30
  154.3 4.3 %collective-permute-start.38 = (f32[256,256]{1,0:T(8,128)S(1)}, f32[256,256]{1,0:T(8,128)S(1)}, u32[]{:S(2)}, u32[]{:S(2)}) collective-permute-start(f32[256,256]{1,0:T(8,128)S(1)} %maximum_select_fusion), channel_id=1, source_target_pairs={{0,3},{1,2},{2,1},{3,0},{4,7},{5,6},{6,5},{7,4},{8,11},{9,10},{10,... | collective-permute-start | bytes 786440 | tf_op jit(solution)/shard_map/ppermute | solution.py:436
  158.6 2.6 %collective-permute-start.37 = (f32[256,256]{1,0:T(8,128)S(1)}, f32[256,256]{1,0:T(8,128)S(1)}, u32[]{:S(2)}, u32[]{:S(2)}) collective-permute-start(f32[256,256]{1,0:T(8,128)S(1)} %maximum_select_fusion), channel_id=1, source_target_pairs={{0,2},{1,3},{2,0},{3,1},{4,6},{5,7},{6,4},{7,5},{8,10},{9,11},{10,... | collective-permute-start | bytes 786440 | tf_op jit(solution)/shard_map/ppermute | solution.py:436
  161.2 5.1 %collective-permute-done.30.refs_0_ = f32[128,1024]{1,0:T(8,128)S(1)} collective-permute-done((f32[128,1024]{1,0:T(8,128)S(1)}, f32[128,1024]{1,0:T(8,128)S(1)}, u32[]{:S(2)}, u32[]{:S(2)}) %collective-permute-start.30) | collective-permute-done | bytes 524320 | tf_op jit(solution)/shard_map/ppermute | solution.py:420
  166.6 3.7 %collective-permute-start.34 = (f32[128,1024]{1,0:T(8,128)S(1)}, f32[128,1024]{1,0:T(8,128)S(1)}, u32[]{:S(2)}, u32[]{:S(2)}) collective-permute-start(f32[128,1024]{1,0:T(8,128)S(1)} %get-tuple-element.125), channel_id=1, source_target_pairs={{0,8},{4,12},{8,0},{12,4},{16,24},{20,28},{24,16},{28,20},{1,9},{5... | collective-permute-start | bytes 1572872 | tf_op jit(solution)/shard_map/ppermute | solution.py:420
  170.3 0.9 collective-permute-start.35
  177.6 4.1 %collective-permute-done.34.refs_0_ = f32[128,1024]{1,0:T(8,128)S(1)} collective-permute-done((f32[128,1024]{1,0:T(8,128)S(1)}, f32[128,1024]{1,0:T(8,128)S(1)}, u32[]{:S(2)}, u32[]{:S(2)}) %collective-permute-start.34) | collective-permute-done | bytes 524320 | tf_op jit(solution)/shard_map/ppermute | solution.py:420
  181.7 1.1 exchange.16
  183.6 4.9 %collective-permute-start.39 = (f32[128,1024]{1,0:T(8,128)}, f32[128,1024]{1,0:T(8,128)}, u32[]{:S(2)}, u32[]{:S(2)}) collective-permute-start(f32[128,1024]{1,0:T(8,128)} %get-tuple-element.128), channel_id=1, source_target_pairs={{0,8},{4,12},{8,0},{12,4},{16,24},{20,28},{24,16},{28,20},{1,9},{5... | collective-permute-start | bytes 1572872 | tf_op jit(solution)/shard_map/ppermute | solution.py:420
  189.0 1.0 copy-done.13
  190.0 1.1 copy-done.15
  191.1 19.0 %update.2 = (f32[2048,2048]{1,0:T(8,128)}, f32[8,128]{1,0:T(8,128)S(1)}) custom-call(s32[6]{0:T(128)S(1)} %broadcast_select_fusion.4.place_ref, f32[128,1024]{1,0:T(8,128)} %get-tuple-element.109.refs_0_, f32[128,1024]{1,0:T(8,128)S(1)} %copy-done.13, f32[128,1280]{1,0:T(8,128)S(1)} %copy-done.15, f32[128,1280]{1,0:T(8,128)S(1)} %collective-permute-done.32.refs_5_.refs_3_, ...), custom_call_target="tpu_custom_call" | custom-call | flops 150994944 | bytes 360448 | tf_op jit(solution)/shard_map/update/pallas_call | solution.py:209
  210.1 1.1 exchange.17.refs_4_
  211.5 1.7 collective-permute-done.41.refs_5_
  213.2 18.6 %update.3 = (f32[2048,2048]{1,0:T(8,128)}, f32[8,128]{1,0:T(8,128)}) custom-call(s32[6]{0:T(128)S(1)} %broadcast_select_fusion.4.place_ref, f32[128,1024]{1,0:T(8,128)S(1)} %copy-done.17, f32[128,1024]{1,0:T(8,128)S(1)} %collective-permute-done.25.refs_9_.refs_1_, f32[128,1024]{1,0:T(8,128)S(1)} %copy-done.19, ...), custom_call_target="tpu_custom_call", output_to_operand_aliasing={{0}: (13, {})} | custom-call | flops 150994944 | bytes 360448 | tf_op jit(solution)/shard_map/update/pallas_call | solution.py:209
  (149 shorter events, 13.4 us)
Async XLA Ops:
  3.0 27.1 %collective-permute-start.5 = (f32[2048,128]{1,0:T(8,128)}, f32[2048,128]{1,0:T(8,128)S(1)}, u32[]{:S(2)}, u32[]{:S(2)}) collective-permute-start(f32[2048,128]{1,0:T(8,128)} %get-tuple-element.138.refs_0_), channel_id=1, source_target_pairs={{0,1},{1,0},{2,3},{3,2},{4,5},{5,4},{6,7},{7,6},{8,9},{9,8},{10,11... | collective-permute-start | bytes 3145736 | tf_op jit(solution)/shard_map/ppermute | solution.py:265
  5.9 26.3 %collective-permute-start = (f32[2048,128]{1,0:T(8,128)}, f32[2048,128]{1,0:T(8,128)S(1)}, u32[]{:S(2)}, u32[]{:S(2)}) collective-permute-start(f32[2048,128]{1,0:T(8,128)} %get-tuple-element.138.refs_0_), channel_id=1, source_target_pairs={{0,2},{1,3},{2,0},{3,1},{4,6},{5,7},{6,4},{7,5},{8,10},{9,11},{10,... | collective-permute-start | bytes 3145736 | tf_op jit(solution)/shard_map/ppermute | solution.py:265
  7.5 15.2 %copy-start.26 = (s32[3]{0:T(128)S(1)}, s32[3]{0:T(128)}, u32[]{:S(2)}) copy-start(s32[3]{0:T(128)} %param.14) | copy-start | bytes 40
  7.5 15.2 %copy-start.34 = (s32[4,2]{1,0:T(4,128)S(1)}, s32[4,2]{1,0:T(4,128)}, u32[]{:S(2)}) copy-start(s32[4,2]{1,0:T(4,128)} %constant.99.clone) | copy-start | bytes 100
  7.5 47.5 %collective-permute-start.2 = (f32[2048,128]{1,0:T(8,128)}, f32[2048,128]{1,0:T(8,128)S(1)}, u32[]{:S(2)}, u32[]{:S(2)}) collective-permute-start(f32[2048,128]{1,0:T(8,128)} %get-tuple-element.137.refs_1_), channel_id=1, source_target_pairs={{0,1},{1,0},{2,3},{3,2},{4,5},{5,4},{6,7},{7,6},{8,9},{9,8},{10,11... | collective-permute-start | bytes 3145736 | tf_op jit(solution)/shard_map/ppermute | solution.py:265
  8.0 55.3 %collective-permute-start.4 = (f32[2048,128]{1,0:T(8,128)}, f32[2048,128]{1,0:T(8,128)}, u32[]{:S(2)}, u32[]{:S(2)}) collective-permute-start(f32[2048,128]{1,0:T(8,128)} %get-tuple-element.137.refs_1_), channel_id=1, source_target_pairs={{0,2},{1,3},{2,0},{3,1},{4,6},{5,7},{6,4},{7,5},{8,10},{9,11},{10,... | collective-permute-start | bytes 3145736 | tf_op jit(solution)/shard_map/ppermute | solution.py:265
  44.4 5.4 %copy-start.27 = (s32[4,2]{1,0:T(4,128)S(1)}, s32[4,2]{1,0:T(4,128)}, u32[]{:S(2)}) copy-start(s32[4,2]{1,0:T(4,128)} %constant.101.clone) | copy-start | bytes 100
  44.4 5.4 %copy-start.28 = (s32[4,2]{1,0:T(4,128)S(1)}, s32[4,2]{1,0:T(4,128)}, u32[]{:S(2)}) copy-start(s32[4,2]{1,0:T(4,128)} %constant.100.clone) | copy-start | bytes 100
  44.4 5.5 %copy-start.33 = (s32[2,4]{1,0:T(2,128)S(1)}, s32[2,4]{1,0:T(2,128)}, u32[]{:S(2)}) copy-start(s32[2,4]{1,0:T(2,128)} %constant.104.clone) | copy-start | bytes 100
  44.4 6.8 %collective-permute-start.7 = (f32[128,512]{1,0:T(8,128)}, f32[128,512]{1,0:T(8,128)}, u32[]{:S(2)}, u32[]{:S(2)}) collective-permute-start(f32[128,512]{1,0:T(8,128)} %get-tuple-element.75), channel_id=1, source_target_pairs={{0,4},{4,0},{8,12},{12,8},{16,20},{20,16},{24,28},{28,24},{1,5},{5... | collective-permute-start | bytes 786440 | tf_op jit(solution)/shard_map/ppermute | solution.py:235
  49.1 2.2 collective-permute-start.6
  53.4 16.1 %collective-permute-start.10 = (f32[128,1024]{1,0:T(8,128)S(1)}, f32[128,1024]{1,0:T(8,128)S(1)}, u32[]{:S(2)}, u32[]{:S(2)}) collective-permute-start(f32[128,1024]{1,0:T(8,128)S(1)} %get-tuple-element.81), channel_id=1, source_target_pairs={{0,8},{4,12},{8,0},{12,4},{16,24},{20,28},{24,16},{28,20},{1,9},{5... | collective-permute-start | bytes 1572872 | tf_op jit(solution)/shard_map/ppermute | solution.py:420
  55.0 49.2 %collective-permute-start.3 = (f32[2048,128]{1,0:T(8,128)S(1)}, f32[2048,128]{1,0:T(8,128)S(1)}, u32[]{:S(2)}, u32[]{:S(2)}) collective-permute-start(f32[2048,128]{1,0:T(8,128)S(1)} %collective-permute-done.2.refs_3_.refs_1_.refs_2_), channel_id=1, source_target_pairs={{0,2},{1,3},{2,0},{3,1},{4,6},{5,7},{6,4},{7,5},{8,10},{9,11},{10,... | collective-permute-start | bytes 3145736 | tf_op jit(solution)/shard_map/ppermute | solution.py:265
  58.3 3.9 %copy-start.32 = (s32[2,4]{1,0:T(2,128)S(1)}, s32[2,4]{1,0:T(2,128)}, u32[]{:S(2)}) copy-start(s32[2,4]{1,0:T(2,128)} %constant.105.clone) | copy-start | bytes 100
  58.3 5.0 %copy-start.3 = (f32[2048,128]{1,0:T(8,128)S(1)}, f32[2048,128]{1,0:T(8,128)}, u32[]{:S(2)}) copy-start(f32[2048,128]{1,0:T(8,128)} %copy-done.1) | copy-start | bytes 3145732
  58.3 5.0 %copy-start.6 = (f32[2048,128]{1,0:T(8,128)S(1)}, f32[2048,128]{1,0:T(8,128)}, u32[]{:S(2)}) copy-start(f32[2048,128]{1,0:T(8,128)} %copy-done.4) | copy-start | bytes 3145732
  58.3 11.1 %collective-permute-start.9 = (f32[128,512]{1,0:T(8,128)S(1)}, f32[128,512]{1,0:T(8,128)S(1)}, u32[]{:S(2)}, u32[]{:S(2)}) collective-permute-start(f32[128,512]{1,0:T(8,128)S(1)} %get-tuple-element.80), channel_id=1, source_target_pairs={{0,4},{4,0},{8,12},{12,8},{16,20},{20,16},{24,28},{28,24},{1,5},{5... | collective-permute-start | bytes 786440 | tf_op jit(solution)/shard_map/ppermute | solution.py:235
  61.8 7.6 %collective-permute-start.8 = (f32[128,512]{1,0:T(8,128)S(1)}, f32[128,512]{1,0:T(8,128)S(1)}, u32[]{:S(2)}, u32[]{:S(2)}) collective-permute-start(f32[128,512]{1,0:T(8,128)S(1)} %get-tuple-element.78), channel_id=1, source_target_pairs={{0,4},{4,0},{8,12},{12,8},{16,20},{20,16},{24,28},{28,24},{1,5},{5... | collective-permute-start | bytes 786440 | tf_op jit(solution)/shard_map/ppermute | solution.py:235
  75.5 14.0 %collective-permute-start.12 = (f32[128,512]{1,0:T(8,128)S(1)}, f32[128,512]{1,0:T(8,128)S(1)}, u32[]{:S(2)}, u32[]{:S(2)}) collective-permute-start(f32[128,512]{1,0:T(8,128)S(1)} %get-tuple-element.87), channel_id=1, source_target_pairs={{0,4},{4,0},{8,12},{12,8},{16,20},{20,16},{24,28},{28,24},{1,5},{5... | collective-permute-start | bytes 786440 | tf_op jit(solution)/shard_map/ppermute | solution.py:235
  78.8 14.3 %collective-permute-start.14 = (f32[128,1024]{1,0:T(8,128)S(1)}, f32[128,1024]{1,0:T(8,128)S(1)}, u32[]{:S(2)}, u32[]{:S(2)}) collective-permute-start(f32[128,1024]{1,0:T(8,128)S(1)} %get-tuple-element.90), channel_id=1, source_target_pairs={{0,8},{4,12},{8,0},{12,4},{16,24},{20,28},{24,16},{28,20},{1,9},{5... | collective-permute-start | bytes 1572872 | tf_op jit(solution)/shard_map/ppermute | solution.py:420
  79.3 13.7 %collective-permute-start.15 = (f32[128,1024]{1,0:T(8,128)S(1)}, f32[128,1024]{1,0:T(8,128)S(1)}, u32[]{:S(2)}, u32[]{:S(2)}) collective-permute-start(f32[128,1024]{1,0:T(8,128)S(1)} %get-tuple-element.91.refs_8_), channel_id=1, source_target_pairs={{8,16},{12,20},{16,8},{20,12},{9,17},{13,21},{17,9},{21,13},{10,18... | collective-permute-start | bytes 1572872 | tf_op jit(solution)/shard_map/ppermute | solution.py:425
  80.2 1.4 collective-permute-start.13
  81.6 28.2 %collective-permute-start.1 = (f32[2048,128]{1,0:T(8,128)S(1)}, f32[2048,128]{1,0:T(8,128)S(1)}, u32[]{:S(2)}, u32[]{:S(2)}) collective-permute-start(f32[2048,128]{1,0:T(8,128)S(1)} %copy-done.3), channel_id=1, source_target_pairs={{0,1},{1,0},{2,3},{3,2},{4,5},{5,4},{6,7},{7,6},{8,9},{9,8},{10,11... | collective-permute-start | bytes 3145736 | tf_op jit(solution)/shard_map/ppermute | solution.py:265
  89.5 1.6 collective-permute-start.11
  93.3 17.8 %collective-permute-start.18 = (f32[128,1280]{1,0:T(8,128)S(1)}, f32[128,1280]{1,0:T(8,128)S(1)}, u32[]{:S(2)}, u32[]{:S(2)}) collective-permute-start(f32[128,1280]{1,0:T(8,128)S(1)} %get-tuple-element.97), channel_id=1, source_target_pairs={{0,8},{4,12},{8,0},{12,4},{16,24},{20,28},{24,16},{28,20},{1,9},{5... | collective-permute-start | bytes 1966088 | tf_op jit(solution)/shard_map/ppermute | solution.py:420
  97.0 12.8 %collective-permute-start.19 = (f32[128,1024]{1,0:T(8,128)S(1)}, f32[128,1024]{1,0:T(8,128)S(1)}, u32[]{:S(2)}, u32[]{:S(2)}) collective-permute-start(f32[128,1024]{1,0:T(8,128)S(1)} %get-tuple-element.98.refs_6_), channel_id=1, source_target_pairs={{8,16},{12,20},{16,8},{20,12},{9,17},{13,21},{17,9},{21,13},{10,18... | collective-permute-start | bytes 1572872 | tf_op jit(solution)/shard_map/ppermute | solution.py:425
  100.9 8.9 %collective-permute-start.17 = (f32[128,512]{1,0:T(8,128)S(1)}, f32[128,512]{1,0:T(8,128)S(1)}, u32[]{:S(2)}, u32[]{:S(2)}) collective-permute-start(f32[128,512]{1,0:T(8,128)S(1)} %get-tuple-element.96), channel_id=1, source_target_pairs={{0,4},{4,0},{8,12},{12,8},{16,20},{20,16},{24,28},{28,24},{1,5},{5... | collective-permute-start | bytes 786440 | tf_op jit(solution)/shard_map/ppermute | solution.py:235
  104.2 8.2 %copy-start.7 = (f32[2048,128]{1,0:T(8,128)}, f32[2048,128]{1,0:T(8,128)S(1)}, u32[]{:S(2)}) copy-start(f32[2048,128]{1,0:T(8,128)S(1)} %collective-permute-done.3.refs_10_.refs_1_) | copy-start | bytes 3145732
  104.3 5.5 %collective-permute-start.16 = (f32[128,512]{1,0:T(8,128)S(1)}, f32[128,512]{1,0:T(8,128)S(1)}, u32[]{:S(2)}, u32[]{:S(2)}) collective-permute-start(f32[128,512]{1,0:T(8,128)S(1)} %get-tuple-element.94), channel_id=1, source_target_pairs={{0,4},{4,0},{8,12},{12,8},{16,20},{20,16},{24,28},{28,24},{1,5},{5... | collective-permute-start | bytes 786440 | tf_op jit(solution)/shard_map/ppermute | solution.py:235
  109.8 2.7 %copy-start.9 = (f32[2048,128]{1,0:T(8,128)}, f32[2048,128]{1,0:T(8,128)S(1)}, u32[]{:S(2)}) copy-start(f32[2048,128]{1,0:T(8,128)S(1)} %collective-permute-done.1.refs_9_.refs_0_) | copy-start | bytes 3145732
  113.2 19.6 %collective-permute-start.23 = (f32[128,1280]{1,0:T(8,128)}, f32[128,1280]{1,0:T(8,128)}, u32[]{:S(2)}, u32[]{:S(2)}) collective-permute-start(f32[128,1280]{1,0:T(8,128)} %get-tuple-element.107.refs_6_), channel_id=1, source_target_pairs={{8,16},{12,20},{16,8},{20,12},{9,17},{13,21},{17,9},{21,13},{10,18... | collective-permute-start | bytes 1966088 | tf_op jit(solution)/shard_map/ppermute | solution.py:425
  114.7 18.1 %collective-permute-start.22 = (f32[128,1024]{1,0:T(8,128)}, f32[128,1024]{1,0:T(8,128)}, u32[]{:S(2)}, u32[]{:S(2)}) collective-permute-start(f32[128,1024]{1,0:T(8,128)} %get-tuple-element.106), channel_id=1, source_target_pairs={{0,8},{4,12},{8,0},{12,4},{16,24},{20,28},{24,16},{28,20},{1,9},{5... | collective-permute-start | bytes 1572872 | tf_op jit(solution)/shard_map/ppermute | solution.py:420
  118.9 13.9 %collective-permute-start.24 = (f32[128,1024]{1,0:T(8,128)}, f32[128,1024]{1,0:T(8,128)S(1)}, u32[]{:S(2)}, u32[]{:S(2)}) collective-permute-start(f32[128,1024]{1,0:T(8,128)} %get-tuple-element.109.refs_0_), channel_id=1, source_target_pairs={{0,4},{4,0},{8,12},{12,8},{16,20},{20,16},{24,28},{28,24},{1,5},{5... | collective-permute-start | bytes 1572872 | tf_op jit(solution)/shard_map/ppermute | solution.py:235
  127.3 5.5 %copy-start.21 = (f32[128,1024]{1,0:T(8,128)S(1)}, f32[128,1024]{1,0:T(8,128)}, u32[]{:S(2)}) copy-start(f32[128,1024]{1,0:T(8,128)} %copy-done.20) | copy-start | bytes 1572868
  127.4 4.0 %collective-permute-start.21 = (f32[128,512]{1,0:T(8,128)S(1)}, f32[128,512]{1,0:T(8,128)S(1)}, u32[]{:S(2)}, u32[]{:S(2)}) collective-permute-start(f32[128,512]{1,0:T(8,128)S(1)} %get-tuple-element.105), channel_id=1, source_target_pairs={{0,4},{4,0},{8,12},{12,8},{16,20},{20,16},{24,28},{28,24},{1,5},{5... | collective-permute-start | bytes 786440 | tf_op jit(solution)/shard_map/ppermute | solution.py:235
  131.2 1.6 collective-permute-start.20
  132.8 2.0 copy-start.12
  134.8 6.0 %copy-start.16 = (f32[128,1024]{1,0:T(8,128)}, f32[128,1024]{1,0:T(8,128)S(1)}, u32[]{:S(2)}) copy-start(f32[128,1024]{1,0:T(8,128)S(1)} %get-tuple-element.110.refs_0_) | copy-start | bytes 1572868
  134.8 16.8 %collective-permute-start.28 = (f32[128,1280]{1,0:T(8,128)S(1)}, f32[128,1280]{1,0:T(8,128)S(1)}, u32[]{:S(2)}, u32[]{:S(2)}) collective-permute-start(f32[128,1280]{1,0:T(8,128)S(1)} %get-tuple-element.116), channel_id=1, source_target_pairs={{0,8},{4,12},{8,0},{12,4},{16,24},{20,28},{24,16},{28,20},{1,9},{5... | collective-permute-start | bytes 1966088 | tf_op jit(solution)/shard_map/ppermute | solution.py:420
  136.8 9.4 %collective-permute-start.25 = (f32[128,1024]{1,0:T(8,128)S(1)}, f32[128,1024]{1,0:T(8,128)S(1)}, u32[]{:S(2)}, u32[]{:S(2)}) collective-permute-start(f32[128,1024]{1,0:T(8,128)S(1)} %get-tuple-element.110.refs_0_), channel_id=1, source_target_pairs={{0,4},{4,0},{8,12},{12,8},{16,20},{20,16},{24,28},{28,24},{1,5},{5... | collective-permute-start | bytes 1572872 | tf_op jit(solution)/shard_map/ppermute | solution.py:235
  136.8 9.4 %collective-permute-start.29 = (f32[128,1024]{1,0:T(8,128)S(1)}, f32[128,1024]{1,0:T(8,128)S(1)}, u32[]{:S(2)}, u32[]{:S(2)}) collective-permute-start(f32[128,1024]{1,0:T(8,128)S(1)} %get-tuple-element.117.refs_6_), channel_id=1, source_target_pairs={{8,16},{12,20},{16,8},{20,12},{9,17},{13,21},{17,9},{21,13},{10,18... | collective-permute-start | bytes 1572872 | tf_op jit(solution)/shard_map/ppermute | solution.py:425
  140.8 3.9 %collective-permute-start.27 = (f32[128,512]{1,0:T(8,128)S(1)}, f32[128,512]{1,0:T(8,128)S(1)}, u32[]{:S(2)}, u32[]{:S(2)}) collective-permute-start(f32[128,512]{1,0:T(8,128)S(1)} %get-tuple-element.115), channel_id=1, source_target_pairs={{0,4},{4,0},{8,12},{12,8},{16,20},{20,16},{24,28},{28,24},{1,5},{5... | collective-permute-start | bytes 786440 | tf_op jit(solution)/shard_map/ppermute | solution.py:235
  144.6 1.6 collective-permute-start.26
  151.9 14.6 %copy-start.14 = (f32[128,1280]{1,0:T(8,128)}, f32[128,1280]{1,0:T(8,128)S(1)}, u32[]{:S(2)}) copy-start(f32[128,1280]{1,0:T(8,128)S(1)} %get-tuple-element.123.refs_2_) | copy-start | bytes 1966084
  151.9 2.4 %collective-permute-start.32 = (f32[128,1280]{1,0:T(8,128)S(1)}, f32[128,1280]{1,0:T(8,128)S(1)}, u32[]{:S(2)}, u32[]{:S(2)}) collective-permute-start(f32[128,1280]{1,0:T(8,128)S(1)} %get-tuple-element.123.refs_2_), channel_id=1, source_target_pairs={{0,4},{4,0},{8,12},{12,8},{16,20},{20,16},{24,28},{28,24},{1,5},{5... | collective-permute-start | bytes 1966088 | tf_op jit(solution)/shard_map/ppermute | solution.py:235
  152.0 14.3 %collective-permute-start.30 = (f32[128,1024]{1,0:T(8,128)S(1)}, f32[128,1024]{1,0:T(8,128)S(1)}, u32[]{:S(2)}, u32[]{:S(2)}) collective-permute-start(f32[128,1024]{1,0:T(8,128)S(1)} %get-tuple-element.119), channel_id=1, source_target_pairs={{0,8},{4,12},{8,0},{12,4},{16,24},{20,28},{24,16},{28,20},{1,9},{5... | collective-permute-start | bytes 1572872 | tf_op jit(solution)/shard_map/ppermute | solution.py:420
  153.6 12.8 %collective-permute-start.31 = (f32[128,1024]{1,0:T(8,128)S(1)}, f32[128,1024]{1,0:T(8,128)S(1)}, u32[]{:S(2)}, u32[]{:S(2)}) collective-permute-start(f32[128,1024]{1,0:T(8,128)S(1)} %get-tuple-element.121.refs_2_), channel_id=1, source_target_pairs={{8,16},{12,20},{16,8},{20,12},{9,17},{13,21},{17,9},{21,13},{10,18... | collective-permute-start | bytes 1572872 | tf_op jit(solution)/shard_map/ppermute | solution.py:425
  154.3 16.9 %copy-start.31 = (s32[2,3]{1,0:T(2,128)S(1)}, s32[2,3]{1,0:T(2,128)}, u32[]{:S(2)}) copy-start(s32[2,3]{1,0:T(2,128)} %constant.106.clone) | copy-start | bytes 76
  154.3 15.9 %collective-permute-start.38 = (f32[256,256]{1,0:T(8,128)S(1)}, f32[256,256]{1,0:T(8,128)S(1)}, u32[]{:S(2)}, u32[]{:S(2)}) collective-permute-start(f32[256,256]{1,0:T(8,128)S(1)} %maximum_select_fusion), channel_id=1, source_target_pairs={{0,3},{1,2},{2,1},{3,0},{4,7},{5,6},{6,5},{7,4},{8,11},{9,10},{10,... | collective-permute-start | bytes 786440 | tf_op jit(solution)/shard_map/ppermute | solution.py:436
  158.6 18.8 %collective-permute-start.37 = (f32[256,256]{1,0:T(8,128)S(1)}, f32[256,256]{1,0:T(8,128)S(1)}, u32[]{:S(2)}, u32[]{:S(2)}) collective-permute-start(f32[256,256]{1,0:T(8,128)S(1)} %maximum_select_fusion), channel_id=1, source_target_pairs={{0,2},{1,3},{2,0},{3,1},{4,6},{5,7},{6,4},{7,5},{8,10},{9,11},{10,... | collective-permute-start | bytes 786440 | tf_op jit(solution)/shard_map/ppermute | solution.py:436
  161.2 16.2 %collective-permute-start.36 = (f32[256,256]{1,0:T(8,128)S(1)}, f32[256,256]{1,0:T(8,128)S(1)}, u32[]{:S(2)}, u32[]{:S(2)}) collective-permute-start(f32[256,256]{1,0:T(8,128)S(1)} %maximum_select_fusion), channel_id=1, source_target_pairs={{0,1},{1,0},{2,3},{3,2},{4,5},{5,4},{6,7},{7,6},{8,9},{9,8},{10,11... | collective-permute-start | bytes 786440 | tf_op jit(solution)/shard_map/ppermute | solution.py:436
  166.6 15.1 %copy-start.18 = (f32[128,1024]{1,0:T(8,128)}, f32[128,1024]{1,0:T(8,128)S(1)}, u32[]{:S(2)}) copy-start(f32[128,1024]{1,0:T(8,128)S(1)} %get-tuple-element.124.refs_2_) | copy-start | bytes 1572868
  166.6 15.1 %collective-permute-start.34 = (f32[128,1024]{1,0:T(8,128)S(1)}, f32[128,1024]{1,0:T(8,128)S(1)}, u32[]{:S(2)}, u32[]{:S(2)}) collective-permute-start(f32[128,1024]{1,0:T(8,128)S(1)} %get-tuple-element.125), channel_id=1, source_target_pairs={{0,8},{4,12},{8,0},{12,4},{16,24},{20,28},{24,16},{28,20},{1,9},{5... | collective-permute-start | bytes 1572872 | tf_op jit(solution)/shard_map/ppermute | solution.py:420
  170.3 11.4 %collective-permute-start.33 = (f32[128,1024]{1,0:T(8,128)S(1)}, f32[128,1024]{1,0:T(8,128)S(1)}, u32[]{:S(2)}, u32[]{:S(2)}) collective-permute-start(f32[128,1024]{1,0:T(8,128)S(1)} %get-tuple-element.124.refs_2_), channel_id=1, source_target_pairs={{0,4},{4,0},{8,12},{12,8},{16,20},{20,16},{24,28},{28,24},{1,5},{5... | collective-permute-start | bytes 1572872 | tf_op jit(solution)/shard_map/ppermute | solution.py:235
  170.3 11.4 %collective-permute-start.35 = (f32[128,1024]{1,0:T(8,128)S(1)}, f32[128,1024]{1,0:T(8,128)S(1)}, u32[]{:S(2)}, u32[]{:S(2)}) collective-permute-start(f32[128,1024]{1,0:T(8,128)S(1)} %get-tuple-element.126.refs_1_), channel_id=1, source_target_pairs={{8,16},{12,20},{16,8},{20,12},{9,17},{13,21},{17,9},{21,13},{10,18... | collective-permute-start | bytes 1572872 | tf_op jit(solution)/shard_map/ppermute | solution.py:425
  177.6 10.9 %copy-start.29 = (s32[4,6]{1,0:T(4,128)S(1)}, s32[4,6]{1,0:T(4,128)}, u32[]{:S(2)}) copy-start(s32[4,6]{1,0:T(4,128)} %constant.103.clone) | copy-start | bytes 292
  177.6 10.9 %copy-start.30 = (s32[4,6]{1,0:T(4,128)S(1)}, s32[4,6]{1,0:T(4,128)}, u32[]{:S(2)}) copy-start(s32[4,6]{1,0:T(4,128)} %constant.102.clone) | copy-start | bytes 292
  177.6 11.3 %copy-start.11 = (f32[3,256,256]{2,1,0:T(8,128)S(1)}, f32[3,256,256]{2,1,0:T(8,128)}, u32[]{:S(2)}) copy-start(f32[3,256,256]{2,1,0:T(8,128)} %refs_6_.3) | copy-start | bytes 2359300
  183.6 5.4 %collective-permute-start.40 = (f32[128,1024]{1,0:T(8,128)}, f32[128,1024]{1,0:T(8,128)}, u32[]{:S(2)}, u32[]{:S(2)}) collective-permute-start(f32[128,1024]{1,0:T(8,128)} %get-tuple-element.130.refs_4_), channel_id=1, source_target_pairs={{0,4},{4,0},{8,12},{12,8},{16,20},{20,16},{24,28},{28,24},{1,5},{5... | collective-permute-start | bytes 1572872 | tf_op jit(solution)/shard_map/ppermute | solution.py:235
  183.6 26.5 %collective-permute-start.39 = (f32[128,1024]{1,0:T(8,128)}, f32[128,1024]{1,0:T(8,128)}, u32[]{:S(2)}, u32[]{:S(2)}) collective-permute-start(f32[128,1024]{1,0:T(8,128)} %get-tuple-element.128), channel_id=1, source_target_pairs={{0,8},{4,12},{8,0},{12,4},{16,24},{20,28},{24,16},{28,20},{1,9},{5... | collective-permute-start | bytes 1572872 | tf_op jit(solution)/shard_map/ppermute | solution.py:420
  191.1 19.0 %copy-start.23 = (f32[128,1024]{1,0:T(8,128)S(1)}, f32[128,1024]{1,0:T(8,128)}, u32[]{:S(2)}) copy-start(f32[128,1024]{1,0:T(8,128)} %copy-done.22) | copy-start | bytes 1572868
  191.1 22.1 %copy-start.17 = (f32[128,1024]{1,0:T(8,128)S(1)}, f32[128,1024]{1,0:T(8,128)}, u32[]{:S(2)}) copy-start(f32[128,1024]{1,0:T(8,128)} %copy-done.16) | copy-start | bytes 1572868
  191.1 22.1 %copy-start.19 = (f32[128,1024]{1,0:T(8,128)S(1)}, f32[128,1024]{1,0:T(8,128)}, u32[]{:S(2)}) copy-start(f32[128,1024]{1,0:T(8,128)} %copy-done.18) | copy-start | bytes 1572868
  211.2 2.0 collective-permute-start.41
  (13 other events, 13.8 us)
where the time goes:
time: 236 us; the launch traced here: 232 us
  Pallas kernels  119 us (50%)
  starting transfers between devices  48.1 us (20%)
  waiting for transfers between devices  38.7 us (16%)
  local copies, waits for them, and re-layouts  18 us (8%)
  between operations  7.67 us (3%)
    pallas_call x13, Pallas kernels, products(): pl.pallas_call(functools.partial(products_kernel, block), in_specs=[in_vm...  43.2 us
    pallas_call x2, Pallas kernels, update(): pl.pallas_call(update_kernel, grid_spec=pltpu.PrefetchScalarGridSpec(num_...  37.6 us
    ppermute x8, starting transfers between devices, shards_square(): outer[step] = lax.ppermute(results['out'], 'row', outer_pairs)  22.2 us
    ppermute x8, waiting for transfers between devices, shards_square(): outer[step] = lax.ppermute(results['out'], 'row', outer_pairs)  17.8 us
    pallas_call x5, Pallas kernels, choose(): pl.pallas_call(functools.partial(choose_kernel, outputs, len(cases)), in_...  16.1 us
    pallas_call x1, Pallas kernels, split_array(): pl.pallas_call(split_kernel, grid=(rows // step,), in_specs=[pl.BlockSpec...  14.6 us
    ppermute x6, waiting for transfers between devices, fetch_square(): along = lambda value, step: lax.ppermute(value, 'col', pairs_of(4, step))  13.4 us
    unnamed x70, local copies, waits for them, and re-layouts  12.4 us
  transfers between devices with their start and end apart: 42, of which 13 were waited for; matrix products, arithmetic and copies ran while one was open for 1% of the time, Pallas kernels for 41%

commit v1 on v0

--- a/solution.py
+++ b/solution.py
@@ -159,7 +159,7 @@
     )(flipped, pinned(both), *after)
 
 
-def update_kernel(place_ref, *refs):
+def update_kernel(offset, place_ref, *refs):
     sums = refs[:6]
     tfac_ref, gram_ref = refs[6:8]
     panel_refs, x_ref = refs[8:11], refs[11]
@@ -171,7 +171,7 @@
     def _():
         for index, piece in enumerate(sums):
             start = pl.multiple_of(place_ref[index] * half, half)
-            w_ref[pl.ds(start, half), :] = piece[:, : w_ref.shape[1]]
+            w_ref[pl.ds(start, half), :] = piece[:, offset : offset + w_ref.shape[1]]
         first = dot_three(tfac_ref[0], w_ref[:width, :])
         y_ref[:width, :] = first
         second = dot_three(tfac_ref[1], w_ref[width : 2 * width, :] - dot_three(gram_ref[0], first))
@@ -189,7 +189,7 @@
     done_ref[...] = jnp.zeros(done_ref.shape, F32)
 
 
-def update(place, sums, tfac, grams, panels, x, out, block, width):
+def update(place, sums, tfac, grams, panels, x, out, block, width, offset=0):
     rows, columns = x.shape
     half = sums[0].shape[0]
     step = min(rows, 512)
@@ -207,7 +207,7 @@
         operands.append(out)
         in_specs.append(IN_HBM)
     return pl.pallas_call(
-        update_kernel,
+        functools.partial(update_kernel, offset),
         grid_spec=pltpu.PrefetchScalarGridSpec(
             num_scalar_prefetch=1,
             grid=(rows // step,),
@@ -359,7 +359,7 @@
     places = jnp.where(core == 0, places, places.reshape(PANELS, 2)[:, ::-1].reshape(-1))
     ordered = lambda pair: jnp.where(core == 0, pair, pair[::-1])
     x_both = split_array(eigvec, PIECE)
-    chunks = [(index, block) for index in range(PANELS) for block in range(columns // width)]
+    chunks = [(0, 0), (0, 1), (1, 0), (2, 0), (1, 1), (2, 1)]
     count = len(chunks)
     gram_chunk = 2
     prepared, arrived, sizes, gram_sides = {}, {}, {}, []
@@ -411,8 +411,6 @@
             ahead.extend(rounds[-1][0][:2])
         if step == gram_chunk - 1:
             ahead.extend(gram_sides)
-        if step == count + 1:
-            ahead.append(grams)
         if 0 <= outward - 1 < count - 2:
             ahead.append(sums[chunks[outward - 1]][1])
         results = exchange(ends, operands, shapes, ahead)
@@ -438,10 +436,15 @@
                 grams = jnp.stack([pick(places_of[number], *spread) for number in range(PANELS)])
             sums[chunks[done]] = (own, other)
             index, block = chunks[done]
-            if index == PANELS - 1:
-                pieces = [piece for panel in range(PANELS) for piece in sums[panel, block]]
+            ready = block if index == PANELS - 1 else 0
+            if step >= count:
+                pieces = [piece for panel in range(PANELS) for piece in sums[panel, ready]]
                 panels = [prepared[panel][0] for panel in range(PANELS)]
-                out, finished = update(places, pieces, tfac, grams, panels, eigvec, out, block, width)
+                if ready == 0:
+                    place, size, offset = step - count, width // 2, (step - count) * (width // 2)
+                else:
+                    place, size, offset = 1, width, 0
+                out, finished = update(places, pieces, tfac, grams, panels, eigvec, out, place, size, offset)
     return out
 
 

time: 236 us -> 242 us (1.025); the launches traced: 232 us -> 241 us
  Pallas kernels: 119 us -> 134 us
  waiting for transfers between devices: 38.7 us -> 29.7 us
  local copies, waits for them, and re-layouts: 18 us -> 26.3 us
  starting transfers between devices: 48.1 us -> 41.7 us
    unnamed x70 -> x92, local copies, waits for them, and re-layouts: 12.4 us -> 20.7 us
    ppermute x8, waiting for transfers between devices: 17.8 us -> 9.88 us  [shards_square(): outer[step] = lax.ppermute(results['out'], 'row', outer_pairs)]
    pallas_call x5, Pallas kernels: 16.1 us -> 21.1 us  [choose(): pl.pallas_call(functools.partial(choose_kernel, outputs, len(cases)), in_...]
    pallas_call x2 -> x3, Pallas kernels: 37.6 us -> 42.6 us  [update(): pl.pallas_call(functools.partial(update_kernel, offset), grid_spec=pltpu....]
    pallas_call x9, Pallas kernels: 7.44 us -> 11.1 us  [exchange(): pl.pallas_call(functools.partial(exchange_kernel, names, pieces), in_spec...]
    ppermute x3, starting transfers between devices: 6.9 us -> 3.55 us  [shards_square(): lax.ppermute(block, 'col', pairs_of(4, shift))]
    ppermute x6, starting transfers between devices: 9.77 us -> 6.82 us  [fetch_square(): along = lambda value, step: lax.ppermute(value, 'col', pairs_of(4, step))]
  transfers between devices with their start and end apart: 42 -> 42, of which waited for: 13 -> 14; matrix products, arithmetic and copies ran while one was open for 1% -> 2% of each run, Pallas kernels for 41% -> 46%
where the time goes in v1:
time: 242 us; the launch traced here: 241 us
  Pallas kernels  134 us (55%)
  starting transfers between devices  41.7 us (17%)
  waiting for transfers between devices  29.7 us (12%)
  local copies, waits for them, and re-layouts  26.3 us (11%)
  between operations  7.45 us (3%)
    pallas_call x13, Pallas kernels, products(): pl.pallas_call(functools.partial(products_kernel, block), in_specs=[in_vm...  44.5 us
    pallas_call x3, Pallas kernels, update(): pl.pallas_call(functools.partial(update_kernel, offset), grid_spec=pltpu....  42.6 us
    pallas_call x5, Pallas kernels, choose(): pl.pallas_call(functools.partial(choose_kernel, outputs, len(cases)), in_...  21.1 us
    ppermute x8, starting transfers between devices, shards_square(): outer[step] = lax.ppermute(results['out'], 'row', outer_pairs)  20.7 us
    unnamed x92, local copies, waits for them, and re-layouts  20.7 us
    pallas_call x1, Pallas kernels, split_array(): pl.pallas_call(split_kernel, grid=(rows // step,), in_specs=[pl.BlockSpec...  14.6 us
    ppermute x6, waiting for transfers between devices, fetch_square(): along = lambda value, step: lax.ppermute(value, 'col', pairs_of(4, step))  12 us
    pallas_call x9, Pallas kernels, exchange(): pl.pallas_call(functools.partial(exchange_kernel, names, pieces), in_spec...  11.1 us
  transfers between devices with their start and end apart: 42, of which 14 were waited for; matrix products, arithmetic and copies ran while one was open for 2% of the time, Pallas kernels for 46%

profile of v1, /device:TPU:0, one launch (start us, length us, event | category | flops | bytes accessed | tf_op | source)
XLA Modules:
  0.0 241.3 jit_solution(8588591791689796297)
XLA Ops:
  0.0 3.0 %fusion.14 = (f32[2048,128]{1,0:T(8,128)}, f32[2048,128]{1,0:T(8,128)}) fusion(f32[2048,256]{1,0:T(8,128)} %bitcast.37), kind=kLoop, calls=%fused_computation.37 | loop fusion | bytes 4194304 | tf_op jit(solution)/shard_map/slice | solution.py:266
  3.0 3.0 %collective-permute-start.2 = (f32[2048,128]{1,0:T(8,128)}, f32[2048,128]{1,0:T(8,128)S(1)}, u32[]{:S(2)}, u32[]{:S(2)}) collective-permute-start(f32[2048,128]{1,0:T(8,128)} %get-tuple-element.142.refs_0_), channel_id=1, source_target_pairs={{0,2},{1,3},{2,0},{3,1},{4,6},{5,7},{6,4},{7,5},{8,10},{9,11},{10,... | collective-permute-start | bytes 3145736 | tf_op jit(solution)/shard_map/ppermute | solution.py:265
  6.0 1.5 collective-permute-start
  8.0 14.6 %split_x.1.both_ref = bf16[4,2,2048,512]{3,2,1,0:T(8,128)(2,1)} custom-call(f32[2048,2048]{1,0:T(8,128)} %refs_11_.5), custom_call_target="tpu_custom_call" | custom-call | flops 262144 | bytes 524288 | tf_op jit(solution)/shard_map/split_x/pallas_call | solution.py:60
  22.9 7.3 %collective-permute-done.2.refs_3_.refs_4_.refs_2_ = f32[2048,128]{1,0:T(8,128)S(1)} collective-permute-done((f32[2048,128]{1,0:T(8,128)}, f32[2048,128]{1,0:T(8,128)S(1)}, u32[]{:S(2)}, u32[]{:S(2)}) %collective-permute-start.2) | collective-permute-done | bytes 1048608 | tf_op jit(solution)/shard_map/ppermute | solution.py:265
  30.2 1.0 copy-done.3
  31.1 1.1 collective-permute-done.refs_2_.refs_0_
  33.2 1.2 copy-done.4
  34.5 1.2 copy-done.9
  35.7 4.8 %choose_panel.5 = (bf16[1,2,2048,256]{3,2,1,0:T(8,128)(2,1)}, bf16[512,2048]{1,0:T(8,128)(2,1)S(1)}) custom-call(s32[2]{0:T(128)S(1)} %broadcast_select_fusion.2.which_ref, f32[2048,128]{1,0:T(8,128)} %get-tuple-element.142.refs_0_, f32[2048,128]{1,0:T(8,128)} %get-tuple-element.141.refs_1_, f32[2048,128]{1,0:T(8,128)S(1)} %copy-done.9, ...), custom_call_target="tpu_custom_call" | custom-call | flops 32768 | bytes 98304 | tf_op jit(solution)/shard_map/choose_panel/pallas_call | solution.py:106
  40.5 3.9 %products.14 = (f32[128,512]{1,0:T(8,128)S(1)}, f32[128,512]{1,0:T(8,128)}) custom-call(bf16[512,2048]{1,0:T(8,128)(2,1)S(1)} %get-tuple-element.73.flipped_ref, bf16[4,2,2048,512]{3,2,1,0:T(8,128)(2,1)} %split_x.1.both_ref), custom_call_target="tpu_custom_call" | custom-call | flops 25165824 | bytes 98304 | tf_op jit(solution)/shard_map/products/pallas_call | solution.py:150
  44.5 3.9 %products.13 = (f32[128,512]{1,0:T(8,128)S(1)}, f32[128,512]{1,0:T(8,128)}) custom-call(bf16[512,2048]{1,0:T(8,128)(2,1)S(1)} %get-tuple-element.73.flipped_ref, bf16[4,2,2048,512]{3,2,1,0:T(8,128)(2,1)} %split_x.1.both_ref), custom_call_target="tpu_custom_call" | custom-call | flops 25165824 | bytes 98304 | tf_op jit(solution)/shard_map/products/pallas_call | solution.py:150
  49.6 3.6 %collective-permute-done.1.refs_3_.refs_1_.refs_2_ = f32[2048,128]{1,0:T(8,128)S(1)} collective-permute-done((f32[2048,128]{1,0:T(8,128)}, f32[2048,128]{1,0:T(8,128)S(1)}, u32[]{:S(2)}, u32[]{:S(2)}) %collective-permute-start.1) | collective-permute-done | bytes 1048608 | tf_op jit(solution)/shard_map/ppermute | solution.py:265
  54.5 1.9 exchange.9
  57.2 1.8 collective-permute-start.8
  59.0 1.5 collective-permute-start.9
  61.9 1.0 copy-done.14
  62.9 3.9 %products.16 = (f32[128,512]{1,0:T(8,128)S(1)}, f32[128,512]{1,0:T(8,128)}) custom-call(bf16[512,2048]{1,0:T(8,128)(2,1)S(1)} %get-tuple-element.73.flipped_ref, bf16[4,2,2048,512]{3,2,1,0:T(8,128)(2,1)} %split_x.1.both_ref, f32[128,1024]{1,0:T(8,128)S(1)} %copy-done.14), custom_call_target="tpu_custom_call" | custom-call | flops 25165824 | bytes 98304 | tf_op jit(solution)/shard_map/products/pallas_call | solution.py:150
  66.9 3.9 %products.15 = (f32[128,512]{1,0:T(8,128)S(1)}, f32[128,512]{1,0:T(8,128)}) custom-call(bf16[512,2048]{1,0:T(8,128)(2,1)S(1)} %get-tuple-element.73.flipped_ref, bf16[4,2,2048,512]{3,2,1,0:T(8,128)(2,1)} %split_x.1.both_ref, f32[128,1024]{1,0:T(8,128)S(1)} %copy-done.14), custom_call_target="tpu_custom_call" | custom-call | flops 25165824 | bytes 98304 | tf_op jit(solution)/shard_map/products/pallas_call | solution.py:150
  73.4 1.2 copy-done.5
  74.6 1.2 copy-done.10
  75.8 1.0 copy-done.15
  76.9 3.6 %choose_panel.7.refs_7_.both_ref = bf16[1,2,2048,256]{3,2,1,0:T(8,128)(2,1)} custom-call(s32[2]{0:T(128)S(1)} %iota_add_fusion.which_ref, f32[2048,128]{1,0:T(8,128)} %get-tuple-element.142.refs_0_, f32[2048,128]{1,0:T(8,128)} %get-tuple-element.141.refs_1_, f32[2048,128]{1,0:T(8,128)S(1)} %copy-done.10, ...), custom_call_target="tpu_custom_call" | custom-call | flops 32768 | bytes 98304 | tf_op jit(solution)/shard_map/choose_panel/pallas_call | solution.py:106
  80.5 3.8 %choose_panel.6.refs_6_.flipped_ref = bf16[512,2048]{1,0:T(8,128)(2,1)S(1)} custom-call(s32[2]{0:T(128)S(1)} %broadcast_select_fusion.1.which_ref, f32[2048,128]{1,0:T(8,128)} %get-tuple-element.142.refs_0_, f32[2048,128]{1,0:T(8,128)} %get-tuple-element.141.refs_1_, f32[2048,128]{1,0:T(8,128)S(1)} %copy-done.11, ...), custom_call_target="tpu_custom_call" | custom-call | flops 32768 | bytes 98304 | tf_op jit(solution)/shard_map/choose_panel/pallas_call | solution.py:106
  84.4 2.8 %exchange.10 = (f32[128,1024]{1,0:T(8,128)S(1)}, f32[128,1024]{1,0:T(8,128)}, f32[128,1024]{1,0:T(8,128)}) custom-call(s32[1]{0:T(128)} %bitcast.3.ends_ref, f32[128,512]{1,0:T(8,128)S(1)} %copy-done.33, f32[128,512]{1,0:T(8,128)S(1)} %collective-permute-done.6.refs_1_, f32[128,512]{1,0:T(8,128)S(1)} %get-tuple-element.81.refs_2_, ...), custom_call_target="tpu_custom_call" | custom-call | tf_op jit(solution)/shard_map/exchange/pallas_call | solution.py:340
  87.7 1.5 collective-permute-start.15
  89.3 1.6 copy-done.2
  90.9 3.2 %products.19 = (f32[128,256]{1,0:T(8,128)S(1)}, f32[128,256]{1,0:T(8,128)S(1)}) custom-call(bf16[512,2048]{1,0:T(8,128)(2,1)S(1)} %copy-done.2, bf16[1,2,2048,256]{3,2,1,0:T(8,128)(2,1)} %choose_panel.7.refs_7_.both_ref, f32[128,1024]{1,0:T(8,128)S(1)} %get-tuple-element.84.refs_4_.refs_0_.refs_7_), custom_call_target="tpu_custom_call" | custom-call | flops 12582912 | bytes 65536 | tf_op jit(solution)/shard_map/products/pallas_call | solution.py:150
  94.2 1.0 copy-done.18
  95.2 4.0 %choose_panel.8 = (bf16[1,2,2048,256]{3,2,1,0:T(8,128)(2,1)}, bf16[512,2048]{1,0:T(8,128)(2,1)S(1)}) custom-call(s32[2]{0:T(128)S(1)} %broadcast_select_fusion.3.which_ref, f32[2048,128]{1,0:T(8,128)S(1)} %copy-done.12, f32[2048,128]{1,0:T(8,128)S(1)} %collective-permute-done.1.refs_3_.refs_1_.refs_2_, f32[2048,128]{1,0:T(8,128)S(1)} %copy-done.7, ...), custom_call_target="tpu_custom_call" | custom-call | flops 32768 | bytes 98304 | tf_op jit(solution)/shard_map/choose_panel/pallas_call | solution.py:106
  99.2 3.2 %products.18 = (f32[128,512]{1,0:T(8,128)S(1)}, f32[128,512]{1,0:T(8,128)S(1)}) custom-call(bf16[512,2048]{1,0:T(8,128)(2,1)S(1)} %get-tuple-element.85.flipped_ref, bf16[4,2,2048,512]{3,2,1,0:T(8,128)(2,1)} %split_x.1.both_ref, f32[128,1024]{1,0:T(8,128)S(1)} %copy-done.19), custom_call_target="tpu_custom_call" | custom-call | flops 25165824 | bytes 98304 | tf_op jit(solution)/shard_map/products/pallas_call | solution.py:150
  102.5 3.2 %products.17 = (f32[128,512]{1,0:T(8,128)S(1)}, f32[128,512]{1,0:T(8,128)S(1)}) custom-call(bf16[512,2048]{1,0:T(8,128)(2,1)S(1)} %get-tuple-element.85.flipped_ref, bf16[4,2,2048,512]{3,2,1,0:T(8,128)(2,1)} %split_x.1.both_ref, f32[128,1024]{1,0:T(8,128)S(1)} %copy-done.19), custom_call_target="tpu_custom_call" | custom-call | flops 25165824 | bytes 98304 | tf_op jit(solution)/shard_map/products/pallas_call | solution.py:150
  106.3 1.1 collective-permute-done.12.refs_3_
  107.8 2.5 %exchange.11 = (f32[128,1280]{1,0:T(8,128)S(1)}, f32[128,1024]{1,0:T(8,128)}, f32[128,1024]{1,0:T(8,128)S(1)}, f32[128,1280]{1,0:T(8,128)}) custom-call(s32[1]{0:T(128)} %bitcast.3.ends_ref, f32[128,512]{1,0:T(8,128)S(1)} %get-tuple-element.86.refs_0_, f32[128,512]{1,0:T(8,128)S(1)} %collective-permute-done.11.refs_1_, ...), custom_call_target="tpu_custom_call" | custom-call | tf_op jit(solution)/shard_map/exchange/pallas_call | solution.py:340
  111.9 3.6 %collective-permute-start.18 = (f32[128,1280]{1,0:T(8,128)}, f32[128,1280]{1,0:T(8,128)}, u32[]{:S(2)}, u32[]{:S(2)}) collective-permute-start(f32[128,1280]{1,0:T(8,128)} %get-tuple-element.100), channel_id=1, source_target_pairs={{0,8},{4,12},{8,0},{12,4},{16,24},{20,28},{24,16},{28,20},{1,9},{5... | collective-permute-start | bytes 1966088 | tf_op jit(solution)/shard_map/ppermute | solution.py:418
  115.5 1.5 collective-permute-start.19
  117.1 1.1 copy-done.21
  118.2 4.9 %choose_panel.9 = (bf16[1,2,2048,256]{3,2,1,0:T(8,128)(2,1)}, bf16[512,2048]{1,0:T(8,128)(2,1)S(1)}) custom-call(s32[2]{0:T(128)S(1)} %broadcast_select_fusion.which_ref, f32[2048,128]{1,0:T(8,128)} %collective-permute-done.9.refs_10_.refs_0_, f32[2048,128]{1,0:T(8,128)} %collective-permute-done.10.refs_11_.refs_1_, ...), custom_call_target="tpu_custom_call" | custom-call | flops 32768 | bytes 98304 | tf_op jit(solution)/shard_map/choose_panel/pallas_call | solution.py:106
  123.0 3.2 %products.21 = (f32[128,512]{1,0:T(8,128)S(1)}, f32[128,512]{1,0:T(8,128)S(1)}) custom-call(bf16[512,2048]{1,0:T(8,128)(2,1)S(1)} %get-tuple-element.95.flipped_ref, bf16[4,2,2048,512]{3,2,1,0:T(8,128)(2,1)} %split_x.1.both_ref, f32[128,1280]{1,0:T(8,128)S(1)} %copy-done.22), custom_call_target="tpu_custom_call" | custom-call | flops 25165824 | bytes 98304 | tf_op jit(solution)/shard_map/products/pallas_call | solution.py:150
  126.4 3.2 %products.20 = (f32[128,512]{1,0:T(8,128)S(1)}, f32[128,512]{1,0:T(8,128)S(1)}) custom-call(bf16[512,2048]{1,0:T(8,128)(2,1)S(1)} %get-tuple-element.95.flipped_ref, bf16[4,2,2048,512]{3,2,1,0:T(8,128)(2,1)} %split_x.1.both_ref, f32[128,1280]{1,0:T(8,128)S(1)} %copy-done.22), custom_call_target="tpu_custom_call" | custom-call | flops 25165824 | bytes 98304 | tf_op jit(solution)/shard_map/products/pallas_call | solution.py:150
  130.1 1.2 collective-permute-done.16.refs_1_
  131.3 1.7 exchange.12
  133.7 3.8 %collective-permute-start.22 = (f32[128,1024]{1,0:T(8,128)S(1)}, f32[128,1024]{1,0:T(8,128)S(1)}, u32[]{:S(2)}, u32[]{:S(2)}) collective-permute-start(f32[128,1024]{1,0:T(8,128)S(1)} %get-tuple-element.108), channel_id=1, source_target_pairs={{0,8},{4,12},{8,0},{12,4},{16,24},{20,28},{24,16},{28,20},{1,9},{5... | collective-permute-start | bytes 1572872 | tf_op jit(solution)/shard_map/ppermute | solution.py:418
  137.5 3.2 %products.23 = (f32[128,512]{1,0:T(8,128)S(1)}, f32[128,512]{1,0:T(8,128)S(1)}) custom-call(bf16[512,2048]{1,0:T(8,128)(2,1)S(1)} %get-tuple-element.85.flipped_ref, bf16[4,2,2048,512]{3,2,1,0:T(8,128)(2,1)} %split_x.1.both_ref, f32[128,1024]{1,0:T(8,128)S(1)} %get-tuple-element.103.refs_0_.refs_5_), custom_call_target="tpu_custom_call" | custom-call | flops 25165824 | bytes 98304 | tf_op jit(solution)/shard_map/products/pallas_call | solution.py:150
  141.3 3.2 %products.22 = (f32[128,512]{1,0:T(8,128)S(1)}, f32[128,512]{1,0:T(8,128)S(1)}) custom-call(bf16[512,2048]{1,0:T(8,128)(2,1)S(1)} %get-tuple-element.85.flipped_ref, bf16[4,2,2048,512]{3,2,1,0:T(8,128)(2,1)} %split_x.1.both_ref, f32[128,1024]{1,0:T(8,128)S(1)} %get-tuple-element.103.refs_0_.refs_5_), custom_call_target="tpu_custom_call" | custom-call | flops 25165824 | bytes 98304 | tf_op jit(solution)/shard_map/products/pallas_call | solution.py:150
  144.6 1.5 collective-permute-done.20.refs_1_
  146.1 3.6 %collective-permute-done.22.refs_4_ = f32[128,1024]{1,0:T(8,128)S(1)} collective-permute-done((f32[128,1024]{1,0:T(8,128)S(1)}, f32[128,1024]{1,0:T(8,128)S(1)}, u32[]{:S(2)}, u32[]{:S(2)}) %collective-permute-start.22) | collective-permute-done | bytes 524320 | tf_op jit(solution)/shard_map/ppermute | solution.py:418
  150.5 3.4 %collective-permute-start.28 = (f32[128,1280]{1,0:T(8,128)S(1)}, f32[128,1280]{1,0:T(8,128)S(1)}, u32[]{:S(2)}, u32[]{:S(2)}) collective-permute-start(f32[128,1280]{1,0:T(8,128)S(1)} %get-tuple-element.118), channel_id=1, source_target_pairs={{0,8},{4,12},{8,0},{12,4},{16,24},{20,28},{24,16},{28,20},{1,9},{5... | collective-permute-start | bytes 1966088 | tf_op jit(solution)/shard_map/ppermute | solution.py:418
  154.6 3.2 %products.25 = (f32[128,512]{1,0:T(8,128)S(1)}, f32[128,512]{1,0:T(8,128)S(1)}) custom-call(bf16[512,2048]{1,0:T(8,128)(2,1)S(1)} %get-tuple-element.95.flipped_ref, bf16[4,2,2048,512]{3,2,1,0:T(8,128)(2,1)} %split_x.1.both_ref, f32[128,1024]{1,0:T(8,128)S(1)} %get-tuple-element.113.refs_0_.refs_5_), custom_call_target="tpu_custom_call" | custom-call | flops 25165824 | bytes 98304 | tf_op jit(solution)/shard_map/products/pallas_call | solution.py:150
  158.3 3.2 %products.24 = (f32[128,512]{1,0:T(8,128)S(1)}, f32[128,512]{1,0:T(8,128)S(1)}) custom-call(bf16[512,2048]{1,0:T(8,128)(2,1)S(1)} %get-tuple-element.95.flipped_ref, bf16[4,2,2048,512]{3,2,1,0:T(8,128)(2,1)} %split_x.1.both_ref, f32[128,1024]{1,0:T(8,128)S(1)} %get-tuple-element.113.refs_0_.refs_5_), custom_call_target="tpu_custom_call" | custom-call | flops 25165824 | bytes 98304 | tf_op jit(solution)/shard_map/products/pallas_call | solution.py:150
  161.6 1.5 collective-permute-done.26.refs_1_
  163.2 5.2 %collective-permute-done.28.refs_4_ = f32[128,1280]{1,0:T(8,128)S(1)} collective-permute-done((f32[128,1280]{1,0:T(8,128)S(1)}, f32[128,1280]{1,0:T(8,128)S(1)}, u32[]{:S(2)}, u32[]{:S(2)}) %collective-permute-start.28) | collective-permute-done | bytes 655392 | tf_op jit(solution)/shard_map/ppermute | solution.py:418
  170.5 1.9 collective-permute-start.30
  172.4 1.5 collective-permute-start.31
  175.4 2.8 %collective-permute-start.36 = (f32[256,256]{1,0:T(8,128)}, f32[256,256]{1,0:T(8,128)}, u32[]{:S(2)}, u32[]{:S(2)}) collective-permute-start(f32[256,256]{1,0:T(8,128)} %maximum_select_fusion), channel_id=1, source_target_pairs={{0,1},{1,0},{2,3},{3,2},{4,5},{5,4},{6,7},{7,6},{8,9},{9,8},{10,11... | collective-permute-start | bytes 786440 | tf_op jit(solution)/shard_map/ppermute | solution.py:434
  185.3 1.0 copy-done.31
  186.3 1.4 exchange.15
  187.8 3.5 %collective-permute-start.33 = (f32[128,1024]{1,0:T(8,128)S(1)}, f32[128,1024]{1,0:T(8,128)S(1)}, u32[]{:S(2)}, u32[]{:S(2)}) collective-permute-start(f32[128,1024]{1,0:T(8,128)S(1)} %get-tuple-element.126), channel_id=1, source_target_pairs={{0,8},{4,12},{8,0},{12,4},{16,24},{20,28},{24,16},{28,20},{1,9},{5... | collective-permute-start | bytes 1572872 | tf_op jit(solution)/shard_map/ppermute | solution.py:418
  192.1 1.3 select_bitcast_fusion.2
  194.0 12.0 %update.3 = (f32[2048,2048]{1,0:T(8,128)}, f32[8,128]{1,0:T(8,128)S(1)}) custom-call(s32[6]{0:T(128)S(1)} %broadcast_select_fusion.4.place_ref, f32[128,1024]{1,0:T(8,128)S(1)} %copy-done.27, f32[128,1024]{1,0:T(8,128)S(1)} %copy-done.25, f32[128,1280]{1,0:T(8,128)S(1)} %get-tuple-element.125.refs_2_, ...), custom_call_target="tpu_custom_call" | custom-call | flops 75497472 | bytes 229376 | tf_op jit(solution)/shard_map/update/pallas_call | solution.py:209
  206.1 2.3 collective-permute-start.40
  208.4 12.0 %update.4 = (f32[2048,2048]{1,0:T(8,128)}, f32[8,128]{1,0:T(8,128)S(1)}) custom-call(s32[6]{0:T(128)S(1)} %broadcast_select_fusion.4.place_ref, f32[128,1024]{1,0:T(8,128)S(1)} %copy-done.27, f32[128,1024]{1,0:T(8,128)S(1)} %copy-done.25, f32[128,1280]{1,0:T(8,128)S(1)} %get-tuple-element.125.refs_2_, ...), custom_call_target="tpu_custom_call", output_to_operand_aliasing={{0}: (13, {})} | custom-call | flops 75497472 | bytes 229376 | tf_op jit(solution)/shard_map/update/pallas_call | solution.py:209
  221.0 1.6 collective-permute-done.41.refs_5_
  222.7 18.6 %update.5 = (f32[2048,2048]{1,0:T(8,128)}, f32[8,128]{1,0:T(8,128)}) custom-call(s32[6]{0:T(128)S(1)} %broadcast_select_fusion.4.place_ref, f32[128,1024]{1,0:T(8,128)S(1)} %get-tuple-element.112.refs_0_, f32[128,1024]{1,0:T(8,128)S(1)} %collective-permute-done.25.refs_9_.refs_1_, ...), custom_call_target="tpu_custom_call", output_to_operand_aliasing={{0}: (13, {})} | custom-call | flops 150994944 | bytes 360448 | tf_op jit(solution)/shard_map/update/pallas_call | solution.py:209
  (172 shorter events, 22.7 us)
Async XLA Ops:
  3.0 27.2 %collective-permute-start.2 = (f32[2048,128]{1,0:T(8,128)}, f32[2048,128]{1,0:T(8,128)S(1)}, u32[]{:S(2)}, u32[]{:S(2)}) collective-permute-start(f32[2048,128]{1,0:T(8,128)} %get-tuple-element.142.refs_0_), channel_id=1, source_target_pairs={{0,2},{1,3},{2,0},{3,1},{4,6},{5,7},{6,4},{7,5},{8,10},{9,11},{10,... | collective-permute-start | bytes 3145736 | tf_op jit(solution)/shard_map/ppermute | solution.py:265
  6.0 26.3 %collective-permute-start = (f32[2048,128]{1,0:T(8,128)}, f32[2048,128]{1,0:T(8,128)S(1)}, u32[]{:S(2)}, u32[]{:S(2)}) collective-permute-start(f32[2048,128]{1,0:T(8,128)} %get-tuple-element.142.refs_0_), channel_id=1, source_target_pairs={{0,1},{1,0},{2,3},{3,2},{4,5},{5,4},{6,7},{7,6},{8,9},{9,8},{10,11... | collective-permute-start | bytes 3145736 | tf_op jit(solution)/shard_map/ppermute | solution.py:265
  7.5 15.2 %copy-start.37 = (s32[3]{0:T(128)S(1)}, s32[3]{0:T(128)}, u32[]{:S(2)}) copy-start(s32[3]{0:T(128)} %param.14) | copy-start | bytes 40
  7.5 15.3 %copy-start.38 = (s32[4,2]{1,0:T(4,128)S(1)}, s32[4,2]{1,0:T(4,128)}, u32[]{:S(2)}) copy-start(s32[4,2]{1,0:T(4,128)} %constant.100.clone) | copy-start | bytes 100
  7.5 15.3 %copy-start.39 = (s32[4,2]{1,0:T(4,128)S(1)}, s32[4,2]{1,0:T(4,128)}, u32[]{:S(2)}) copy-start(s32[4,2]{1,0:T(4,128)} %constant.99.clone) | copy-start | bytes 100
  7.5 45.8 %collective-permute-start.1 = (f32[2048,128]{1,0:T(8,128)}, f32[2048,128]{1,0:T(8,128)S(1)}, u32[]{:S(2)}, u32[]{:S(2)}) collective-permute-start(f32[2048,128]{1,0:T(8,128)} %get-tuple-element.141.refs_1_), channel_id=1, source_target_pairs={{0,1},{1,0},{2,3},{3,2},{4,5},{5,4},{6,7},{7,6},{8,9},{9,8},{10,11... | collective-permute-start | bytes 3145736 | tf_op jit(solution)/shard_map/ppermute | solution.py:265
  8.0 63.5 %collective-permute-start.3 = (f32[2048,128]{1,0:T(8,128)}, f32[2048,128]{1,0:T(8,128)}, u32[]{:S(2)}, u32[]{:S(2)}) collective-permute-start(f32[2048,128]{1,0:T(8,128)} %get-tuple-element.141.refs_1_), channel_id=1, source_target_pairs={{0,2},{1,3},{2,0},{3,1},{4,6},{5,7},{6,4},{7,5},{8,10},{9,11},{10,... | collective-permute-start | bytes 3145736 | tf_op jit(solution)/shard_map/ppermute | solution.py:265
  44.5 16.1 %copy-start.44 = (s32[2,4]{1,0:T(2,128)S(1)}, s32[2,4]{1,0:T(2,128)}, u32[]{:S(2)}) copy-start(s32[2,4]{1,0:T(2,128)} %constant.105.clone) | copy-start | bytes 100
  44.5 9.1 %collective-permute-start.5 = (f32[128,512]{1,0:T(8,128)}, f32[128,512]{1,0:T(8,128)}, u32[]{:S(2)}, u32[]{:S(2)}) collective-permute-start(f32[128,512]{1,0:T(8,128)} %get-tuple-element.77), channel_id=1, source_target_pairs={{0,4},{4,0},{8,12},{12,8},{16,20},{20,16},{24,28},{28,24},{1,5},{5... | collective-permute-start | bytes 786440 | tf_op jit(solution)/shard_map/ppermute | solution.py:235
  49.2 4.4 %collective-permute-start.4 = (f32[128,512]{1,0:T(8,128)}, f32[128,512]{1,0:T(8,128)}, u32[]{:S(2)}, u32[]{:S(2)}) collective-permute-start(f32[128,512]{1,0:T(8,128)} %get-tuple-element.75), channel_id=1, source_target_pairs={{0,4},{4,0},{8,12},{12,8},{16,20},{20,16},{24,28},{28,24},{1,5},{5... | collective-permute-start | bytes 786440 | tf_op jit(solution)/shard_map/ppermute | solution.py:235
  53.3 52.9 %collective-permute-start.10 = (f32[2048,128]{1,0:T(8,128)S(1)}, f32[2048,128]{1,0:T(8,128)}, u32[]{:S(2)}, u32[]{:S(2)}) collective-permute-start(f32[2048,128]{1,0:T(8,128)S(1)} %collective-permute-done.1.refs_3_.refs_1_.refs_2_), channel_id=1, source_target_pairs={{0,2},{1,3},{2,0},{3,1},{4,6},{5,7},{6,4},{7,5},{8,10},{9,11},{10,... | collective-permute-start | bytes 3145736 | tf_op jit(solution)/shard_map/ppermute | solution.py:265
  57.2 27.2 %collective-permute-start.8 = (f32[128,1024]{1,0:T(8,128)}, f32[128,1024]{1,0:T(8,128)}, u32[]{:S(2)}, u32[]{:S(2)}) collective-permute-start(f32[128,1024]{1,0:T(8,128)} %get-tuple-element.83), channel_id=1, source_target_pairs={{0,8},{4,12},{8,0},{12,4},{16,24},{20,28},{24,16},{28,20},{1,9},{5... | collective-permute-start | bytes 1572872 | tf_op jit(solution)/shard_map/ppermute | solution.py:418
  59.0 47.3 %collective-permute-start.9 = (f32[2048,128]{1,0:T(8,128)}, f32[2048,128]{1,0:T(8,128)}, u32[]{:S(2)}, u32[]{:S(2)}) collective-permute-start(f32[2048,128]{1,0:T(8,128)} %copy-done.3), channel_id=1, source_target_pairs={{0,1},{1,0},{2,3},{3,2},{4,5},{5,4},{6,7},{7,6},{8,9},{9,8},{10,11... | collective-permute-start | bytes 3145736 | tf_op jit(solution)/shard_map/ppermute | solution.py:265
  66.8 5.2 %copy-start.43 = (s32[2,4]{1,0:T(2,128)S(1)}, s32[2,4]{1,0:T(2,128)}, u32[]{:S(2)}) copy-start(s32[2,4]{1,0:T(2,128)} %constant.104.clone) | copy-start | bytes 100
  66.8 17.6 %collective-permute-start.7 = (f32[128,512]{1,0:T(8,128)}, f32[128,512]{1,0:T(8,128)}, u32[]{:S(2)}, u32[]{:S(2)}) collective-permute-start(f32[128,512]{1,0:T(8,128)} %get-tuple-element.82), channel_id=1, source_target_pairs={{0,4},{4,0},{8,12},{12,8},{16,20},{20,16},{24,28},{28,24},{1,5},{5... | collective-permute-start | bytes 786440 | tf_op jit(solution)/shard_map/ppermute | solution.py:235
  71.5 12.9 %collective-permute-start.6 = (f32[128,512]{1,0:T(8,128)}, f32[128,512]{1,0:T(8,128)S(1)}, u32[]{:S(2)}, u32[]{:S(2)}) collective-permute-start(f32[128,512]{1,0:T(8,128)} %get-tuple-element.80), channel_id=1, source_target_pairs={{0,4},{4,0},{8,12},{12,8},{16,20},{20,16},{24,28},{28,24},{1,5},{5... | collective-permute-start | bytes 786440 | tf_op jit(solution)/shard_map/ppermute | solution.py:235
  76.9 3.6 %copy-start.6 = (f32[2048,128]{1,0:T(8,128)S(1)}, f32[2048,128]{1,0:T(8,128)}, u32[]{:S(2)}) copy-start(f32[2048,128]{1,0:T(8,128)} %copy-done.3) | copy-start | bytes 3145732
  76.9 3.6 %copy-start.11 = (f32[2048,128]{1,0:T(8,128)S(1)}, f32[2048,128]{1,0:T(8,128)}, u32[]{:S(2)}) copy-start(f32[2048,128]{1,0:T(8,128)} %copy-done.8) | copy-start | bytes 3145732
  76.9 3.6 %copy-start.16 = (f32[128,1024]{1,0:T(8,128)S(1)}, f32[128,1024]{1,0:T(8,128)}, u32[]{:S(2)}) copy-start(f32[128,1024]{1,0:T(8,128)} %copy-done.13) | copy-start | bytes 1572868
  80.5 3.9 %copy-start = (bf16[1,2,2048,256]{3,2,1,0:T(8,128)(2,1)S(1)}, bf16[1,2,2048,256]{3,2,1,0:T(8,128)(2,1)}, u32[]{:S(2)}) copy-start(bf16[1,2,2048,256]{3,2,1,0:T(8,128)(2,1)} %choose_panel.7.refs_7_.both_ref) | copy-start | bytes 6291460
  80.5 3.9 %copy-start.33 = (f32[128,512]{1,0:T(8,128)S(1)}, f32[128,512]{1,0:T(8,128)}, u32[]{:S(2)}) copy-start(f32[128,512]{1,0:T(8,128)} %copy-done.32) | copy-start | bytes 786436
  87.3 6.8 %copy-start.17 = (f32[128,1024]{1,0:T(8,128)}, f32[128,1024]{1,0:T(8,128)S(1)}, u32[]{:S(2)}) copy-start(f32[128,1024]{1,0:T(8,128)S(1)} %get-tuple-element.84.refs_4_.refs_0_.refs_7_) | copy-start | bytes 1572868
  87.3 20.5 %collective-permute-start.14 = (f32[128,1024]{1,0:T(8,128)}, f32[128,1024]{1,0:T(8,128)}, u32[]{:S(2)}, u32[]{:S(2)}) collective-permute-start(f32[128,1024]{1,0:T(8,128)} %get-tuple-element.92), channel_id=1, source_target_pairs={{0,8},{4,12},{8,0},{12,4},{16,24},{20,28},{24,16},{28,20},{1,9},{5... | collective-permute-start | bytes 1572872 | tf_op jit(solution)/shard_map/ppermute | solution.py:418
  87.7 20.0 %collective-permute-start.15 = (f32[128,1024]{1,0:T(8,128)}, f32[128,1024]{1,0:T(8,128)}, u32[]{:S(2)}, u32[]{:S(2)}) collective-permute-start(f32[128,1024]{1,0:T(8,128)} %get-tuple-element.93.refs_8_), channel_id=1, source_target_pairs={{8,16},{12,20},{16,8},{20,12},{9,17},{13,21},{17,9},{21,13},{10,18... | collective-permute-start | bytes 1572872 | tf_op jit(solution)/shard_map/ppermute | solution.py:423
  90.9 3.3 %copy-start.7 = (f32[2048,128]{1,0:T(8,128)S(1)}, f32[2048,128]{1,0:T(8,128)}, u32[]{:S(2)}) copy-start(f32[2048,128]{1,0:T(8,128)} %copy-done.3) | copy-start | bytes 3145732
  90.9 3.3 %copy-start.12 = (f32[2048,128]{1,0:T(8,128)S(1)}, f32[2048,128]{1,0:T(8,128)}, u32[]{:S(2)}) copy-start(f32[2048,128]{1,0:T(8,128)} %copy-done.8) | copy-start | bytes 3145732
  94.1 11.6 %collective-permute-start.13 = (f32[128,256]{1,0:T(8,128)S(1)}, f32[128,256]{1,0:T(8,128)S(1)}, u32[]{:S(2)}, u32[]{:S(2)}) collective-permute-start(f32[128,256]{1,0:T(8,128)S(1)} %get-tuple-element.91), channel_id=1, source_target_pairs={{0,4},{4,0},{8,12},{12,8},{16,20},{20,16},{24,28},{28,24},{1,5},{5... | collective-permute-start | bytes 393224 | tf_op jit(solution)/shard_map/ppermute | solution.py:235
  95.2 4.0 %copy-start.19 = (f32[128,1024]{1,0:T(8,128)S(1)}, f32[128,1024]{1,0:T(8,128)}, u32[]{:S(2)}) copy-start(f32[128,1024]{1,0:T(8,128)} %copy-done.17) | copy-start | bytes 1572868
  105.7 1.7 collective-permute-start.12
  106.2 1.5 collective-permute-start.11
  107.7 9.2 %copy-start.45 = (s32[4,2]{1,0:T(4,128)S(1)}, s32[4,2]{1,0:T(4,128)}, u32[]{:S(2)}) copy-start(s32[4,2]{1,0:T(4,128)} %constant.101.clone) | copy-start | bytes 100
  111.9 19.4 %collective-permute-start.18 = (f32[128,1280]{1,0:T(8,128)}, f32[128,1280]{1,0:T(8,128)}, u32[]{:S(2)}, u32[]{:S(2)}) collective-permute-start(f32[128,1280]{1,0:T(8,128)} %get-tuple-element.100), channel_id=1, source_target_pairs={{0,8},{4,12},{8,0},{12,4},{16,24},{20,28},{24,16},{28,20},{1,9},{5... | collective-permute-start | bytes 1966088 | tf_op jit(solution)/shard_map/ppermute | solution.py:418
  115.5 15.8 %collective-permute-start.19 = (f32[128,1024]{1,0:T(8,128)}, f32[128,1024]{1,0:T(8,128)}, u32[]{:S(2)}, u32[]{:S(2)}) collective-permute-start(f32[128,1024]{1,0:T(8,128)} %get-tuple-element.101.refs_6_), channel_id=1, source_target_pairs={{8,16},{12,20},{16,8},{20,12},{9,17},{13,21},{17,9},{21,13},{10,18... | collective-permute-start | bytes 1572872 | tf_op jit(solution)/shard_map/ppermute | solution.py:423
  118.2 4.9 %copy-start.22 = (f32[128,1280]{1,0:T(8,128)S(1)}, f32[128,1280]{1,0:T(8,128)}, u32[]{:S(2)}) copy-start(f32[128,1280]{1,0:T(8,128)} %copy-done.20) | copy-start | bytes 1966084
  126.3 5.0 %copy-start.29 = (f32[128,1024]{1,0:T(8,128)S(1)}, f32[128,1024]{1,0:T(8,128)}, u32[]{:S(2)}) copy-start(f32[128,1024]{1,0:T(8,128)} %copy-done.28) | copy-start | bytes 1572868
  126.3 3.9 %collective-permute-start.17 = (f32[128,512]{1,0:T(8,128)S(1)}, f32[128,512]{1,0:T(8,128)S(1)}, u32[]{:S(2)}, u32[]{:S(2)}) collective-permute-start(f32[128,512]{1,0:T(8,128)S(1)} %get-tuple-element.99), channel_id=1, source_target_pairs={{0,4},{4,0},{8,12},{12,8},{16,20},{20,16},{24,28},{28,24},{1,5},{5... | collective-permute-start | bytes 786440 | tf_op jit(solution)/shard_map/ppermute | solution.py:235
  129.7 1.6 collective-permute-start.16
  133.0 7.7 %copy-start.26 = (f32[128,1024]{1,0:T(8,128)}, f32[128,1024]{1,0:T(8,128)S(1)}, u32[]{:S(2)}) copy-start(f32[128,1024]{1,0:T(8,128)S(1)} %get-tuple-element.111.refs_0_) | copy-start | bytes 1572868
  133.0 16.7 %collective-permute-start.23 = (f32[128,1280]{1,0:T(8,128)S(1)}, f32[128,1280]{1,0:T(8,128)S(1)}, u32[]{:S(2)}, u32[]{:S(2)}) collective-permute-start(f32[128,1280]{1,0:T(8,128)S(1)} %get-tuple-element.109.refs_6_), channel_id=1, source_target_pairs={{8,16},{12,20},{16,8},{20,12},{9,17},{13,21},{17,9},{21,13},{10,18... | collective-permute-start | bytes 1966088 | tf_op jit(solution)/shard_map/ppermute | solution.py:423
  133.7 15.9 %collective-permute-start.22 = (f32[128,1024]{1,0:T(8,128)S(1)}, f32[128,1024]{1,0:T(8,128)S(1)}, u32[]{:S(2)}, u32[]{:S(2)}) collective-permute-start(f32[128,1024]{1,0:T(8,128)S(1)} %get-tuple-element.108), channel_id=1, source_target_pairs={{0,8},{4,12},{8,0},{12,4},{16,24},{20,28},{24,16},{28,20},{1,9},{5... | collective-permute-start | bytes 1572872 | tf_op jit(solution)/shard_map/ppermute | solution.py:418
  137.5 12.2 %collective-permute-start.24 = (f32[128,1024]{1,0:T(8,128)S(1)}, f32[128,1024]{1,0:T(8,128)S(1)}, u32[]{:S(2)}, u32[]{:S(2)}) collective-permute-start(f32[128,1024]{1,0:T(8,128)S(1)} %get-tuple-element.111.refs_0_), channel_id=1, source_target_pairs={{0,4},{4,0},{8,12},{12,8},{16,20},{20,16},{24,28},{28,24},{1,5},{5... | collective-permute-start | bytes 1572872 | tf_op jit(solution)/shard_map/ppermute | solution.py:235
  140.7 3.9 %collective-permute-start.21 = (f32[128,512]{1,0:T(8,128)S(1)}, f32[128,512]{1,0:T(8,128)S(1)}, u32[]{:S(2)}, u32[]{:S(2)}) collective-permute-start(f32[128,512]{1,0:T(8,128)S(1)} %get-tuple-element.107), channel_id=1, source_target_pairs={{0,4},{4,0},{8,12},{12,8},{16,20},{20,16},{24,28},{28,24},{1,5},{5... | collective-permute-start | bytes 786440 | tf_op jit(solution)/shard_map/ppermute | solution.py:235
  144.5 1.6 collective-permute-start.20
  150.5 17.8 %collective-permute-start.28 = (f32[128,1280]{1,0:T(8,128)S(1)}, f32[128,1280]{1,0:T(8,128)S(1)}, u32[]{:S(2)}, u32[]{:S(2)}) collective-permute-start(f32[128,1280]{1,0:T(8,128)S(1)} %get-tuple-element.118), channel_id=1, source_target_pairs={{0,8},{4,12},{8,0},{12,4},{16,24},{20,28},{24,16},{28,20},{1,9},{5... | collective-permute-start | bytes 1966088 | tf_op jit(solution)/shard_map/ppermute | solution.py:418
  153.9 9.3 %collective-permute-start.25 = (f32[128,1024]{1,0:T(8,128)S(1)}, f32[128,1024]{1,0:T(8,128)S(1)}, u32[]{:S(2)}, u32[]{:S(2)}) collective-permute-start(f32[128,1024]{1,0:T(8,128)S(1)} %get-tuple-element.112.refs_0_), channel_id=1, source_target_pairs={{0,4},{4,0},{8,12},{12,8},{16,20},{20,16},{24,28},{28,24},{1,5},{5... | collective-permute-start | bytes 1572872 | tf_op jit(solution)/shard_map/ppermute | solution.py:235
  153.9 9.3 %collective-permute-start.29 = (f32[128,1024]{1,0:T(8,128)S(1)}, f32[128,1024]{1,0:T(8,128)S(1)}, u32[]{:S(2)}, u32[]{:S(2)}) collective-permute-start(f32[128,1024]{1,0:T(8,128)S(1)} %get-tuple-element.119.refs_6_), channel_id=1, source_target_pairs={{8,16},{12,20},{16,8},{20,12},{9,17},{13,21},{17,9},{21,13},{10,18... | collective-permute-start | bytes 1572872 | tf_op jit(solution)/shard_map/ppermute | solution.py:423
  157.8 3.9 %collective-permute-start.27 = (f32[128,512]{1,0:T(8,128)S(1)}, f32[128,512]{1,0:T(8,128)S(1)}, u32[]{:S(2)}, u32[]{:S(2)}) collective-permute-start(f32[128,512]{1,0:T(8,128)S(1)} %get-tuple-element.117), channel_id=1, source_target_pairs={{0,4},{4,0},{8,12},{12,8},{16,20},{20,16},{24,28},{28,24},{1,5},{5... | collective-permute-start | bytes 786440 | tf_op jit(solution)/shard_map/ppermute | solution.py:235
  161.5 1.6 collective-permute-start.26
  168.3 6.3 %copy-start.42 = (s32[2,3]{1,0:T(2,128)S(1)}, s32[2,3]{1,0:T(2,128)}, u32[]{:S(2)}) copy-start(s32[2,3]{1,0:T(2,128)} %constant.106.clone) | copy-start | bytes 76
  170.2 3.7 %collective-permute-start.32 = (f32[128,1280]{1,0:T(8,128)S(1)}, f32[128,1280]{1,0:T(8,128)S(1)}, u32[]{:S(2)}, u32[]{:S(2)}) collective-permute-start(f32[128,1280]{1,0:T(8,128)S(1)} %get-tuple-element.125.refs_2_), channel_id=1, source_target_pairs={{0,4},{4,0},{8,12},{12,8},{16,20},{20,16},{24,28},{28,24},{1,5},{5... | collective-permute-start | bytes 1966088 | tf_op jit(solution)/shard_map/ppermute | solution.py:235
  170.5 14.8 %collective-permute-start.30 = (f32[128,1024]{1,0:T(8,128)}, f32[128,1024]{1,0:T(8,128)}, u32[]{:S(2)}, u32[]{:S(2)}) collective-permute-start(f32[128,1024]{1,0:T(8,128)} %copy-done.36), channel_id=1, source_target_pairs={{0,8},{4,12},{8,0},{12,4},{16,24},{20,28},{24,16},{28,20},{1,9},{5... | collective-permute-start | bytes 1572872 | tf_op jit(solution)/shard_map/ppermute | solution.py:418
  172.4 12.9 %collective-permute-start.31 = (f32[128,1024]{1,0:T(8,128)S(1)}, f32[128,1024]{1,0:T(8,128)}, u32[]{:S(2)}, u32[]{:S(2)}) collective-permute-start(f32[128,1024]{1,0:T(8,128)S(1)} %get-tuple-element.123.refs_2_), channel_id=1, source_target_pairs={{8,16},{12,20},{16,8},{20,12},{9,17},{13,21},{17,9},{21,13},{10,18... | collective-permute-start | bytes 1572872 | tf_op jit(solution)/shard_map/ppermute | solution.py:423
  174.6 17.4 %collective-permute-start.38 = (f32[256,256]{1,0:T(8,128)}, f32[256,256]{1,0:T(8,128)}, u32[]{:S(2)}, u32[]{:S(2)}) collective-permute-start(f32[256,256]{1,0:T(8,128)} %maximum_select_fusion), channel_id=1, source_target_pairs={{0,3},{1,2},{2,1},{3,0},{4,7},{5,6},{6,5},{7,4},{8,11},{9,10},{10,... | collective-permute-start | bytes 786440 | tf_op jit(solution)/shard_map/ppermute | solution.py:434
  174.6 17.5 %collective-permute-start.37 = (f32[256,256]{1,0:T(8,128)}, f32[256,256]{1,0:T(8,128)}, u32[]{:S(2)}, u32[]{:S(2)}) collective-permute-start(f32[256,256]{1,0:T(8,128)} %maximum_select_fusion), channel_id=1, source_target_pairs={{0,2},{1,3},{2,0},{3,1},{4,6},{5,7},{6,4},{7,5},{8,10},{9,11},{10,... | collective-permute-start | bytes 786440 | tf_op jit(solution)/shard_map/ppermute | solution.py:434
  175.4 16.7 %collective-permute-start.36 = (f32[256,256]{1,0:T(8,128)}, f32[256,256]{1,0:T(8,128)}, u32[]{:S(2)}, u32[]{:S(2)}) collective-permute-start(f32[256,256]{1,0:T(8,128)} %maximum_select_fusion), channel_id=1, source_target_pairs={{0,1},{1,0},{2,3},{3,2},{4,5},{5,4},{6,7},{7,6},{8,9},{9,8},{10,11... | collective-permute-start | bytes 786440 | tf_op jit(solution)/shard_map/ppermute | solution.py:434
  187.8 6.2 %copy-start.23 = (f32[3,256,256]{2,1,0:T(8,128)S(1)}, f32[3,256,256]{2,1,0:T(8,128)}, u32[]{:S(2)}) copy-start(f32[3,256,256]{2,1,0:T(8,128)} %refs_6_.5) | copy-start | bytes 2359300
  187.8 6.2 %copy-start.25 = (f32[128,1024]{1,0:T(8,128)S(1)}, f32[128,1024]{1,0:T(8,128)}, u32[]{:S(2)}) copy-start(f32[128,1024]{1,0:T(8,128)} %copy-done.24) | copy-start | bytes 1572868
  187.8 6.2 %copy-start.27 = (f32[128,1024]{1,0:T(8,128)S(1)}, f32[128,1024]{1,0:T(8,128)}, u32[]{:S(2)}) copy-start(f32[128,1024]{1,0:T(8,128)} %copy-done.26) | copy-start | bytes 1572868
  187.8 18.2 %collective-permute-start.33 = (f32[128,1024]{1,0:T(8,128)S(1)}, f32[128,1024]{1,0:T(8,128)S(1)}, u32[]{:S(2)}, u32[]{:S(2)}) collective-permute-start(f32[128,1024]{1,0:T(8,128)S(1)} %get-tuple-element.126), channel_id=1, source_target_pairs={{0,8},{4,12},{8,0},{12,4},{16,24},{20,28},{24,16},{28,20},{1,9},{5... | collective-permute-start | bytes 1572872 | tf_op jit(solution)/shard_map/ppermute | solution.py:418
  191.3 14.7 %collective-permute-start.34 = (f32[128,1024]{1,0:T(8,128)S(1)}, f32[128,1024]{1,0:T(8,128)S(1)}, u32[]{:S(2)}, u32[]{:S(2)}) collective-permute-start(f32[128,1024]{1,0:T(8,128)S(1)} %get-tuple-element.127.refs_1_), channel_id=1, source_target_pairs={{8,16},{12,20},{16,8},{20,12},{9,17},{13,21},{17,9},{21,13},{10,18... | collective-permute-start | bytes 1572872 | tf_op jit(solution)/shard_map/ppermute | solution.py:423
  192.0 2.0 collective-permute-start.35
  206.1 14.5 %collective-permute-start.40 = (f32[128,1024]{1,0:T(8,128)S(1)}, f32[128,1024]{1,0:T(8,128)S(1)}, u32[]{:S(2)}, u32[]{:S(2)}) collective-permute-start(f32[128,1024]{1,0:T(8,128)S(1)} %get-tuple-element.135), channel_id=1, source_target_pairs={{0,8},{4,12},{8,0},{12,4},{16,24},{20,28},{24,16},{28,20},{1,9},{5... | collective-permute-start | bytes 1572872 | tf_op jit(solution)/shard_map/ppermute | solution.py:418
  208.4 12.6 %collective-permute-start.39 = (f32[128,1024]{1,0:T(8,128)S(1)}, f32[128,1024]{1,0:T(8,128)S(1)}, u32[]{:S(2)}, u32[]{:S(2)}) collective-permute-start(f32[128,1024]{1,0:T(8,128)S(1)} %get-tuple-element.134.refs_2_), channel_id=1, source_target_pairs={{0,4},{4,0},{8,12},{12,8},{16,20},{20,16},{24,28},{28,24},{1,5},{5... | collective-permute-start | bytes 1572872 | tf_op jit(solution)/shard_map/ppermute | solution.py:235
  220.7 2.0 collective-permute-start.41
  (24 other events, 27.6 us)

commit v2 on v1

--- a/solution.py
+++ b/solution.py
@@ -63,7 +63,7 @@
         in_specs=[pl.BlockSpec((step, columns), lambda i: (i, 0))],
         out_specs=pl.BlockSpec((blocks, 2, step, width), lambda i: (0, 0, i, 0)),
         out_shape=pltpu.HBM((blocks, 2, rows, width), BF16),
-        compiler_params=params(49),
+        compiler_params=params(63),
         cost_estimate=cost(rows * columns * 4, rows * columns * 8),
         name="split_x",
     )(x)
@@ -408,9 +408,9 @@
             shapes["out"] = max(sent, key=lambda shape: shape[1])
         ahead = [] if out is None else [finished]
         if step + 1 == chunks.index((PANELS - 1, 0)):
-            ahead.extend(rounds[-1][0][:2])
+            ahead.extend(map(pinned, rounds[-1][0][:2]))
         if step == gram_chunk - 1:
-            ahead.extend(gram_sides)
+            ahead.extend([gram_sides[0], pinned(gram_sides[1])])
         if 0 <= outward - 1 < count - 2:
             ahead.append(sums[chunks[outward - 1]][1])
         results = exchange(ends, operands, shapes, ahead)

time: 242 us -> 245 us (1.012)
  waiting for transfers between devices: 29.7 us -> 36 us
  local copies, waits for them, and re-layouts: 26.3 us -> 22.9 us
    ppermute x6, waiting for transfers between devices: 12 us -> 17.9 us  [fetch_square(): along = lambda value, step: lax.ppermute(value, 'col', pairs_of(4, step))]
    unnamed x92 -> x68, local copies, waits for them, and re-layouts: 20.7 us -> 17.3 us
  transfers between devices with their start and end apart: 42 -> 42, of which waited for: 14 -> 14; matrix products, arithmetic and copies ran while one was open for 2% -> 2% of each run, Pallas kernels for 46% -> 45%
where the time goes in v2:
time: 245 us; the launch traced here: 244 us
  Pallas kernels  133 us (54%)
  starting transfers between devices  43 us (18%)
  waiting for transfers between devices  36 us (15%)
  local copies, waits for them, and re-layouts  22.9 us (9%)
  between operations  7.48 us (3%)
    pallas_call x13, Pallas kernels, products(): pl.pallas_call(functools.partial(products_kernel, block), in_specs=[in_vm...  43.8 us
    pallas_call x3, Pallas kernels, update(): pl.pallas_call(functools.partial(update_kernel, offset), grid_spec=pltpu....  42.6 us
    pallas_call x5, Pallas kernels, choose(): pl.pallas_call(functools.partial(choose_kernel, outputs, len(cases)), in_...  22.9 us
    ppermute x8, starting transfers between devices, shards_square(): outer[step] = lax.ppermute(results['out'], 'row', outer_pairs)  22.3 us
    ppermute x6, waiting for transfers between devices, fetch_square(): along = lambda value, step: lax.ppermute(value, 'col', pairs_of(4, step))  17.9 us
    unnamed x68, local copies, waits for them, and re-layouts  17.3 us
    pallas_call x1, Pallas kernels, split_array(): pl.pallas_call(split_kernel, grid=(rows // step,), in_specs=[pl.BlockSpec...  14.6 us
    ppermute x8, waiting for transfers between devices, shards_square(): outer[step] = lax.ppermute(results['out'], 'row', outer_pairs)  10.2 us
  transfers between devices with their start and end apart: 42, of which 14 were waited for; matrix products, arithmetic and copies ran while one was open for 2% of the time, Pallas kernels for 45%

profile of v2, /device:TPU:0, one launch (start us, length us, event | category | flops | bytes accessed | tf_op | source)
XLA Modules:
  0.0 243.6 jit_solution(14118674993810683941)
XLA Ops:
  0.0 3.1 %fusion.14 = (f32[2048,128]{1,0:T(8,128)}, f32[2048,128]{1,0:T(8,128)}) fusion(f32[2048,256]{1,0:T(8,128)} %bitcast.37), kind=kLoop, calls=%fused_computation.37 | loop fusion | bytes 4194304 | tf_op jit(solution)/shard_map/slice | solution.py:266
  3.1 3.0 %collective-permute-start.2 = (f32[2048,128]{1,0:T(8,128)}, f32[2048,128]{1,0:T(8,128)}, u32[]{:S(2)}, u32[]{:S(2)}) collective-permute-start(f32[2048,128]{1,0:T(8,128)} %get-tuple-element.142.refs_0_), channel_id=1, source_target_pairs={{0,2},{1,3},{2,0},{3,1},{4,6},{5,7},{6,4},{7,5},{8,10},{9,11},{10,... | collective-permute-start | bytes 3145736 | tf_op jit(solution)/shard_map/ppermute | solution.py:265
  6.0 1.5 collective-permute-start
  8.1 14.6 %split_x.1.both_ref = bf16[4,2,2048,512]{3,2,1,0:T(8,128)(2,1)} custom-call(f32[2048,2048]{1,0:T(8,128)} %refs_11_.5), custom_call_target="tpu_custom_call" | custom-call | flops 262144 | bytes 524288 | tf_op jit(solution)/shard_map/split_x/pallas_call | solution.py:60
  22.9 7.4 %collective-permute-done.2.refs_3_.refs_4_.refs_2_ = f32[2048,128]{1,0:T(8,128)} collective-permute-done((f32[2048,128]{1,0:T(8,128)}, f32[2048,128]{1,0:T(8,128)}, u32[]{:S(2)}, u32[]{:S(2)}) %collective-permute-start.2) | collective-permute-done | bytes 1048608 | tf_op jit(solution)/shard_map/ppermute | solution.py:265
  30.3 2.1 collective-permute-done.refs_2_.refs_0_
  32.4 4.9 %choose_panel.5 = (bf16[1,2,2048,256]{3,2,1,0:T(8,128)(2,1)}, bf16[512,2048]{1,0:T(8,128)(2,1)S(1)}) custom-call(s32[2]{0:T(128)S(1)} %broadcast_select_fusion.2.which_ref, f32[2048,128]{1,0:T(8,128)} %get-tuple-element.142.refs_0_, f32[2048,128]{1,0:T(8,128)} %get-tuple-element.141.refs_1_, f32[2048,128]{1,0:T(8,128)} %collective-permute-done.refs_2_.refs_0_, ...), custom_call_target="tpu_custom_call" | custom-call | flops 32768 | bytes 98304 | tf_op jit(solution)/shard_map/choose_panel/pallas_call | solution.py:106
  37.3 3.2 %products.14 = (f32[128,512]{1,0:T(8,128)S(1)}, f32[128,512]{1,0:T(8,128)S(1)}) custom-call(bf16[512,2048]{1,0:T(8,128)(2,1)S(1)} %get-tuple-element.73.flipped_ref, bf16[4,2,2048,512]{3,2,1,0:T(8,128)(2,1)} %split_x.1.both_ref), custom_call_target="tpu_custom_call" | custom-call | flops 25165824 | bytes 98304 | tf_op jit(solution)/shard_map/products/pallas_call | solution.py:150
  40.6 3.9 %products.13 = (f32[128,512]{1,0:T(8,128)S(1)}, f32[128,512]{1,0:T(8,128)}) custom-call(bf16[512,2048]{1,0:T(8,128)(2,1)S(1)} %get-tuple-element.73.flipped_ref, bf16[4,2,2048,512]{3,2,1,0:T(8,128)(2,1)} %split_x.1.both_ref), custom_call_target="tpu_custom_call" | custom-call | flops 25165824 | bytes 98304 | tf_op jit(solution)/shard_map/products/pallas_call | solution.py:150
  45.1 8.4 %collective-permute-done.1.refs_3_.refs_1_.refs_2_ = f32[2048,128]{1,0:T(8,128)} collective-permute-done((f32[2048,128]{1,0:T(8,128)}, f32[2048,128]{1,0:T(8,128)}, u32[]{:S(2)}, u32[]{:S(2)}) %collective-permute-start.1) | collective-permute-done | bytes 1048608 | tf_op jit(solution)/shard_map/ppermute | solution.py:265
  54.5 0.9 copy-done.23
  56.3 1.8 collective-permute-start.8
  58.1 1.5 collective-permute-start.9
  60.8 3.9 %products.16 = (f32[128,512]{1,0:T(8,128)S(1)}, f32[128,512]{1,0:T(8,128)}) custom-call(bf16[512,2048]{1,0:T(8,128)(2,1)S(1)} %get-tuple-element.73.flipped_ref, bf16[4,2,2048,512]{3,2,1,0:T(8,128)(2,1)} %split_x.1.both_ref, f32[128,1024]{1,0:T(8,128)S(1)} %get-tuple-element.78.refs_0_.refs_6_.refs_5_), custom_call_target="tpu_custom_call" | custom-call | flops 25165824 | bytes 98304 | tf_op jit(solution)/shard_map/products/pallas_call | solution.py:150
  64.8 3.9 %products.15 = (f32[128,512]{1,0:T(8,128)S(1)}, f32[128,512]{1,0:T(8,128)}) custom-call(bf16[512,2048]{1,0:T(8,128)(2,1)S(1)} %get-tuple-element.73.flipped_ref, bf16[4,2,2048,512]{3,2,1,0:T(8,128)(2,1)} %split_x.1.both_ref, f32[128,1024]{1,0:T(8,128)S(1)} %get-tuple-element.78.refs_0_.refs_6_.refs_5_), custom_call_target="tpu_custom_call" | custom-call | flops 25165824 | bytes 98304 | tf_op jit(solution)/shard_map/products/pallas_call | solution.py:150
  71.2 4.6 %choose_panel.7.refs_7_.both_ref = bf16[1,2,2048,256]{3,2,1,0:T(8,128)(2,1)} custom-call(s32[2]{0:T(128)S(1)} %iota_add_fusion.which_ref, f32[2048,128]{1,0:T(8,128)} %get-tuple-element.142.refs_0_, f32[2048,128]{1,0:T(8,128)} %get-tuple-element.141.refs_1_, f32[2048,128]{1,0:T(8,128)} %collective-permute-done.refs_2_.refs_0_, ...), custom_call_target="tpu_custom_call" | custom-call | flops 32768 | bytes 98304 | tf_op jit(solution)/shard_map/choose_panel/pallas_call | solution.py:106
  75.8 3.7 %choose_panel.6.refs_6_.flipped_ref = bf16[512,2048]{1,0:T(8,128)(2,1)S(1)} custom-call(s32[2]{0:T(128)S(1)} %broadcast_select_fusion.1.which_ref, f32[2048,128]{1,0:T(8,128)} %get-tuple-element.142.refs_0_, f32[2048,128]{1,0:T(8,128)} %get-tuple-element.141.refs_1_, f32[2048,128]{1,0:T(8,128)} %collective-permute-done.refs_2_.refs_0_, ...), custom_call_target="tpu_custom_call" | custom-call | flops 32768 | bytes 98304 | tf_op jit(solution)/shard_map/choose_panel/pallas_call | solution.py:106
  80.4 1.0 copy-done.9
  81.4 2.2 exchange.10
  84.1 1.5 collective-permute-start.15
  85.7 3.0 %products.19 = (f32[128,256]{1,0:T(8,128)S(1)}, f32[128,256]{1,0:T(8,128)S(1)}) custom-call(bf16[512,2048]{1,0:T(8,128)(2,1)S(1)} %choose_panel.6.refs_6_.flipped_ref, bf16[1,2,2048,256]{3,2,1,0:T(8,128)(2,1)} %choose_panel.7.refs_7_.both_ref, f32[128,1024]{1,0:T(8,128)S(1)} %get-tuple-element.84.refs_4_.refs_0_.refs_7_), custom_call_target="tpu_custom_call" | custom-call | flops 12582912 | bytes 65536 | tf_op jit(solution)/shard_map/products/pallas_call | solution.py:150
  88.8 4.9 %choose_panel.8 = (bf16[1,2,2048,256]{3,2,1,0:T(8,128)(2,1)}, bf16[512,2048]{1,0:T(8,128)(2,1)S(1)}) custom-call(s32[2]{0:T(128)S(1)} %broadcast_select_fusion.3.which_ref, f32[2048,128]{1,0:T(8,128)} %collective-permute-done.refs_2_.refs_0_, f32[2048,128]{1,0:T(8,128)} %collective-permute-done.1.refs_3_.refs_1_.refs_2_, ...), custom_call_target="tpu_custom_call" | custom-call | flops 32768 | bytes 98304 | tf_op jit(solution)/shard_map/choose_panel/pallas_call | solution.py:106
  93.7 3.2 %products.18 = (f32[128,512]{1,0:T(8,128)S(1)}, f32[128,512]{1,0:T(8,128)S(1)}) custom-call(bf16[512,2048]{1,0:T(8,128)(2,1)S(1)} %get-tuple-element.85.flipped_ref, bf16[4,2,2048,512]{3,2,1,0:T(8,128)(2,1)} %split_x.1.both_ref, f32[128,1024]{1,0:T(8,128)S(1)} %get-tuple-element.84.refs_4_.refs_0_.refs_7_), custom_call_target="tpu_custom_call" | custom-call | flops 25165824 | bytes 98304 | tf_op jit(solution)/shard_map/products/pallas_call | solution.py:150
  96.9 3.2 %products.17 = (f32[128,512]{1,0:T(8,128)S(1)}, f32[128,512]{1,0:T(8,128)S(1)}) custom-call(bf16[512,2048]{1,0:T(8,128)(2,1)S(1)} %get-tuple-element.85.flipped_ref, bf16[4,2,2048,512]{3,2,1,0:T(8,128)(2,1)} %split_x.1.both_ref, f32[128,1024]{1,0:T(8,128)S(1)} %get-tuple-element.84.refs_4_.refs_0_.refs_7_), custom_call_target="tpu_custom_call" | custom-call | flops 25165824 | bytes 98304 | tf_op jit(solution)/shard_map/products/pallas_call | solution.py:150
  100.8 1.1 collective-permute-done.12.refs_3_
  102.2 2.4 exchange.11
  104.6 0.9 copy-done
  106.3 3.6 %collective-permute-start.18 = (f32[128,1280]{1,0:T(8,128)}, f32[128,1280]{1,0:T(8,128)S(1)}, u32[]{:S(2)}, u32[]{:S(2)}) collective-permute-start(f32[128,1280]{1,0:T(8,128)} %get-tuple-element.100), channel_id=1, source_target_pairs={{0,8},{4,12},{8,0},{12,4},{16,24},{20,28},{24,16},{28,20},{1,9},{5... | collective-permute-start | bytes 1966088 | tf_op jit(solution)/shard_map/ppermute | solution.py:418
  110.9 1.1 copy-done.1
  112.0 4.9 %choose_panel.9 = (bf16[1,2,2048,256]{3,2,1,0:T(8,128)(2,1)}, bf16[512,2048]{1,0:T(8,128)(2,1)S(1)}) custom-call(s32[2]{0:T(128)S(1)} %broadcast_select_fusion.which_ref, f32[2048,128]{1,0:T(8,128)} %collective-permute-done.9.refs_10_.refs_0_, f32[2048,128]{1,0:T(8,128)} %collective-permute-done.10.refs_11_.refs_1_, ...), custom_call_target="tpu_custom_call" | custom-call | flops 32768 | bytes 98304 | tf_op jit(solution)/shard_map/choose_panel/pallas_call | solution.py:106
  116.9 3.2 %products.21 = (f32[128,512]{1,0:T(8,128)S(1)}, f32[128,512]{1,0:T(8,128)S(1)}) custom-call(bf16[512,2048]{1,0:T(8,128)(2,1)S(1)} %get-tuple-element.95.flipped_ref, bf16[4,2,2048,512]{3,2,1,0:T(8,128)(2,1)} %split_x.1.both_ref, f32[128,1280]{1,0:T(8,128)S(1)} %copy-done.1), custom_call_target="tpu_custom_call" | custom-call | flops 25165824 | bytes 98304 | tf_op jit(solution)/shard_map/products/pallas_call | solution.py:150
  120.3 3.3 %products.20 = (f32[128,512]{1,0:T(8,128)S(1)}, f32[128,512]{1,0:T(8,128)S(1)}) custom-call(bf16[512,2048]{1,0:T(8,128)(2,1)S(1)} %get-tuple-element.95.flipped_ref, bf16[4,2,2048,512]{3,2,1,0:T(8,128)(2,1)} %split_x.1.both_ref, f32[128,1280]{1,0:T(8,128)S(1)} %copy-done.1), custom_call_target="tpu_custom_call" | custom-call | flops 25165824 | bytes 98304 | tf_op jit(solution)/shard_map/products/pallas_call | solution.py:150
  124.0 1.2 collective-permute-done.16.refs_1_
  126.0 0.9 copy-done.4
  126.9 1.1 copy-done.5
  128.0 1.0 copy-done.13
  129.1 1.3 exchange.12
  131.1 4.5 %collective-permute-start.22 = (f32[128,1024]{1,0:T(8,128)S(1)}, f32[128,1024]{1,0:T(8,128)S(1)}, u32[]{:S(2)}, u32[]{:S(2)}) collective-permute-start(f32[128,1024]{1,0:T(8,128)S(1)} %get-tuple-element.108), channel_id=1, source_target_pairs={{0,8},{4,12},{8,0},{12,4},{16,24},{20,28},{24,16},{28,20},{1,9},{5... | collective-permute-start | bytes 1572872 | tf_op jit(solution)/shard_map/ppermute | solution.py:418
  135.6 3.2 %products.23 = (f32[128,512]{1,0:T(8,128)S(1)}, f32[128,512]{1,0:T(8,128)S(1)}) custom-call(bf16[512,2048]{1,0:T(8,128)(2,1)S(1)} %get-tuple-element.85.flipped_ref, bf16[4,2,2048,512]{3,2,1,0:T(8,128)(2,1)} %split_x.1.both_ref, f32[128,1024]{1,0:T(8,128)S(1)} %get-tuple-element.103.refs_0_.refs_5_), custom_call_target="tpu_custom_call" | custom-call | flops 25165824 | bytes 98304 | tf_op jit(solution)/shard_map/products/pallas_call | solution.py:150
  139.4 3.2 %products.22 = (f32[128,512]{1,0:T(8,128)S(1)}, f32[128,512]{1,0:T(8,128)S(1)}) custom-call(bf16[512,2048]{1,0:T(8,128)(2,1)S(1)} %get-tuple-element.85.flipped_ref, bf16[4,2,2048,512]{3,2,1,0:T(8,128)(2,1)} %split_x.1.both_ref, f32[128,1024]{1,0:T(8,128)S(1)} %get-tuple-element.103.refs_0_.refs_5_), custom_call_target="tpu_custom_call" | custom-call | flops 25165824 | bytes 98304 | tf_op jit(solution)/shard_map/products/pallas_call | solution.py:150
  142.7 1.5 collective-permute-done.20.refs_1_
  144.2 3.6 %collective-permute-done.22.refs_4_ = f32[128,1024]{1,0:T(8,128)S(1)} collective-permute-done((f32[128,1024]{1,0:T(8,128)S(1)}, f32[128,1024]{1,0:T(8,128)S(1)}, u32[]{:S(2)}, u32[]{:S(2)}) %collective-permute-start.22) | collective-permute-done | bytes 524320 | tf_op jit(solution)/shard_map/ppermute | solution.py:418
  148.1 3.9 %collective-permute-start.28 = (f32[128,1280]{1,0:T(8,128)S(1)}, f32[128,1280]{1,0:T(8,128)S(1)}, u32[]{:S(2)}, u32[]{:S(2)}) collective-permute-start(f32[128,1280]{1,0:T(8,128)S(1)} %get-tuple-element.118), channel_id=1, source_target_pairs={{0,8},{4,12},{8,0},{12,4},{16,24},{20,28},{24,16},{28,20},{1,9},{5... | collective-permute-start | bytes 1966088 | tf_op jit(solution)/shard_map/ppermute | solution.py:418
  152.7 3.2 %products.25 = (f32[128,512]{1,0:T(8,128)S(1)}, f32[128,512]{1,0:T(8,128)S(1)}) custom-call(bf16[512,2048]{1,0:T(8,128)(2,1)S(1)} %get-tuple-element.95.flipped_ref, bf16[4,2,2048,512]{3,2,1,0:T(8,128)(2,1)} %split_x.1.both_ref, f32[128,1024]{1,0:T(8,128)S(1)} %get-tuple-element.113.refs_0_.refs_5_), custom_call_target="tpu_custom_call" | custom-call | flops 25165824 | bytes 98304 | tf_op jit(solution)/shard_map/products/pallas_call | solution.py:150
  156.5 3.2 %products.24 = (f32[128,512]{1,0:T(8,128)S(1)}, f32[128,512]{1,0:T(8,128)S(1)}) custom-call(bf16[512,2048]{1,0:T(8,128)(2,1)S(1)} %get-tuple-element.95.flipped_ref, bf16[4,2,2048,512]{3,2,1,0:T(8,128)(2,1)} %split_x.1.both_ref, f32[128,1024]{1,0:T(8,128)S(1)} %get-tuple-element.113.refs_0_.refs_5_), custom_call_target="tpu_custom_call" | custom-call | flops 25165824 | bytes 98304 | tf_op jit(solution)/shard_map/products/pallas_call | solution.py:150
  159.8 1.5 collective-permute-done.26.refs_1_
  161.4 5.1 %collective-permute-done.28.refs_4_ = f32[128,1280]{1,0:T(8,128)S(1)} collective-permute-done((f32[128,1280]{1,0:T(8,128)S(1)}, f32[128,1280]{1,0:T(8,128)S(1)}, u32[]{:S(2)}, u32[]{:S(2)}) %collective-permute-start.28) | collective-permute-done | bytes 655392 | tf_op jit(solution)/shard_map/ppermute | solution.py:418
  170.2 1.9 collective-permute-start.30
  172.2 1.4 collective-permute-start.31
  173.6 1.6 collective-permute-start.38
  175.8 1.5 collective-permute-start.36
  183.7 1.3 collective-permute-done.30.refs_0_
  185.1 1.0 copy-done.15
  186.1 1.0 copy-done.17
  187.2 1.0 copy-done.19
  188.2 1.4 exchange.15
  189.6 3.7 %collective-permute-start.33 = (f32[128,1024]{1,0:T(8,128)S(1)}, f32[128,1024]{1,0:T(8,128)S(1)}, u32[]{:S(2)}, u32[]{:S(2)}) collective-permute-start(f32[128,1024]{1,0:T(8,128)S(1)} %get-tuple-element.126), channel_id=1, source_target_pairs={{0,8},{4,12},{8,0},{12,4},{16,24},{20,28},{24,16},{28,20},{1,9},{5... | collective-permute-start | bytes 1572872 | tf_op jit(solution)/shard_map/ppermute | solution.py:418
  193.3 0.9 collective-permute-start.34
  194.4 1.1 select_bitcast_fusion.2
  196.2 12.0 %update.3 = (f32[2048,2048]{1,0:T(8,128)}, f32[8,128]{1,0:T(8,128)S(1)}) custom-call(s32[6]{0:T(128)S(1)} %broadcast_select_fusion.4.place_ref, f32[128,1024]{1,0:T(8,128)S(1)} %get-tuple-element.111.refs_0_, f32[128,1024]{1,0:T(8,128)S(1)} %collective-permute-done.24.refs_9_.refs_1_, f32[128,1280]{1,0:T(8,128)S(1)} %get-tuple-element.125.refs_2_, ...), custom_call_target="tpu_custom_call" | custom-call | flops 75497472 | bytes 229376 | tf_op jit(solution)/shard_map/update/pallas_call | solution.py:209
  208.4 2.4 collective-permute-start.40
  210.7 12.0 %update.4 = (f32[2048,2048]{1,0:T(8,128)}, f32[8,128]{1,0:T(8,128)S(1)}) custom-call(s32[6]{0:T(128)S(1)} %broadcast_select_fusion.4.place_ref, f32[128,1024]{1,0:T(8,128)S(1)} %get-tuple-element.111.refs_0_, f32[128,1024]{1,0:T(8,128)S(1)} %collective-permute-done.24.refs_9_.refs_1_, ...), custom_call_target="tpu_custom_call", output_to_operand_aliasing={{0}: (13, {})} | custom-call | flops 75497472 | bytes 229376 | tf_op jit(solution)/shard_map/update/pallas_call | solution.py:209
  223.3 1.6 collective-permute-done.41.refs_5_
  225.0 18.6 %update.5 = (f32[2048,2048]{1,0:T(8,128)}, f32[8,128]{1,0:T(8,128)}) custom-call(s32[6]{0:T(128)S(1)} %broadcast_select_fusion.4.place_ref, f32[128,1024]{1,0:T(8,128)S(1)} %copy-done.7, f32[128,1024]{1,0:T(8,128)S(1)} %collective-permute-done.25.refs_9_.refs_1_, f32[128,1024]{1,0:T(8,128)S(1)} %get-tuple-element.134.refs_2_, ...), custom_call_target="tpu_custom_call", output_to_operand_aliasing={{0}: (13, {})} | custom-call | flops 150994944 | bytes 360448 | tf_op jit(solution)/shard_map/update/pallas_call | solution.py:209
  (148 shorter events, 21.3 us)
Async XLA Ops:
  3.1 27.3 %collective-permute-start.2 = (f32[2048,128]{1,0:T(8,128)}, f32[2048,128]{1,0:T(8,128)}, u32[]{:S(2)}, u32[]{:S(2)}) collective-permute-start(f32[2048,128]{1,0:T(8,128)} %get-tuple-element.142.refs_0_), channel_id=1, source_target_pairs={{0,2},{1,3},{2,0},{3,1},{4,6},{5,7},{6,4},{7,5},{8,10},{9,11},{10,... | collective-permute-start | bytes 3145736 | tf_op jit(solution)/shard_map/ppermute | solution.py:265
  6.0 26.4 %collective-permute-start = (f32[2048,128]{1,0:T(8,128)}, f32[2048,128]{1,0:T(8,128)}, u32[]{:S(2)}, u32[]{:S(2)}) collective-permute-start(f32[2048,128]{1,0:T(8,128)} %get-tuple-element.142.refs_0_), channel_id=1, source_target_pairs={{0,1},{1,0},{2,3},{3,2},{4,5},{5,4},{6,7},{7,6},{8,9},{9,8},{10,11... | collective-permute-start | bytes 3145736 | tf_op jit(solution)/shard_map/ppermute | solution.py:265
  7.5 15.2 %copy-start.25 = (s32[3]{0:T(128)S(1)}, s32[3]{0:T(128)}, u32[]{:S(2)}) copy-start(s32[3]{0:T(128)} %param.14) | copy-start | bytes 40
  7.5 15.3 %copy-start.26 = (s32[4,2]{1,0:T(4,128)S(1)}, s32[4,2]{1,0:T(4,128)}, u32[]{:S(2)}) copy-start(s32[4,2]{1,0:T(4,128)} %constant.100.clone) | copy-start | bytes 100
  7.5 15.3 %copy-start.27 = (s32[4,2]{1,0:T(4,128)S(1)}, s32[4,2]{1,0:T(4,128)}, u32[]{:S(2)}) copy-start(s32[4,2]{1,0:T(4,128)} %constant.99.clone) | copy-start | bytes 100
  7.5 45.9 %collective-permute-start.1 = (f32[2048,128]{1,0:T(8,128)}, f32[2048,128]{1,0:T(8,128)}, u32[]{:S(2)}, u32[]{:S(2)}) collective-permute-start(f32[2048,128]{1,0:T(8,128)} %get-tuple-element.141.refs_1_), channel_id=1, source_target_pairs={{0,1},{1,0},{2,3},{3,2},{4,5},{5,4},{6,7},{7,6},{8,9},{9,8},{10,11... | collective-permute-start | bytes 3145736 | tf_op jit(solution)/shard_map/ppermute | solution.py:265
  8.1 61.4 %collective-permute-start.3 = (f32[2048,128]{1,0:T(8,128)}, f32[2048,128]{1,0:T(8,128)}, u32[]{:S(2)}, u32[]{:S(2)}) collective-permute-start(f32[2048,128]{1,0:T(8,128)} %get-tuple-element.141.refs_1_), channel_id=1, source_target_pairs={{0,2},{1,3},{2,0},{3,1},{4,6},{5,7},{6,4},{7,5},{8,10},{9,11},{10,... | collective-permute-start | bytes 3145736 | tf_op jit(solution)/shard_map/ppermute | solution.py:265
  40.5 19.1 %copy-start.32 = (s32[2,4]{1,0:T(2,128)S(1)}, s32[2,4]{1,0:T(2,128)}, u32[]{:S(2)}) copy-start(s32[2,4]{1,0:T(2,128)} %constant.105.clone) | copy-start | bytes 100
  40.5 13.2 %collective-permute-start.5 = (f32[128,512]{1,0:T(8,128)S(1)}, f32[128,512]{1,0:T(8,128)S(1)}, u32[]{:S(2)}, u32[]{:S(2)}) collective-permute-start(f32[128,512]{1,0:T(8,128)S(1)} %get-tuple-element.77), channel_id=1, source_target_pairs={{0,4},{4,0},{8,12},{12,8},{16,20},{20,16},{24,28},{28,24},{1,5},{5... | collective-permute-start | bytes 786440 | tf_op jit(solution)/shard_map/ppermute | solution.py:235
  44.5 9.2 %collective-permute-start.4 = (f32[128,512]{1,0:T(8,128)}, f32[128,512]{1,0:T(8,128)S(1)}, u32[]{:S(2)}, u32[]{:S(2)}) collective-permute-start(f32[128,512]{1,0:T(8,128)} %get-tuple-element.75), channel_id=1, source_target_pairs={{0,4},{4,0},{8,12},{12,8},{16,20},{20,16},{24,28},{28,24},{1,5},{5... | collective-permute-start | bytes 786440 | tf_op jit(solution)/shard_map/ppermute | solution.py:235
  53.4 47.2 %collective-permute-start.10 = (f32[2048,128]{1,0:T(8,128)}, f32[2048,128]{1,0:T(8,128)}, u32[]{:S(2)}, u32[]{:S(2)}) collective-permute-start(f32[2048,128]{1,0:T(8,128)} %collective-permute-done.1.refs_3_.refs_1_.refs_2_), channel_id=1, source_target_pairs={{0,2},{1,3},{2,0},{3,1},{4,6},{5,7},{6,4},{7,5},{8,10},{9,11},{10,... | collective-permute-start | bytes 3145736 | tf_op jit(solution)/shard_map/ppermute | solution.py:265
  56.3 23.3 %collective-permute-start.8 = (f32[128,1024]{1,0:T(8,128)}, f32[128,1024]{1,0:T(8,128)S(1)}, u32[]{:S(2)}, u32[]{:S(2)}) collective-permute-start(f32[128,1024]{1,0:T(8,128)} %get-tuple-element.83), channel_id=1, source_target_pairs={{0,8},{4,12},{8,0},{12,4},{16,24},{20,28},{24,16},{28,20},{1,9},{5... | collective-permute-start | bytes 1572872 | tf_op jit(solution)/shard_map/ppermute | solution.py:418
  58.1 42.7 %collective-permute-start.9 = (f32[2048,128]{1,0:T(8,128)}, f32[2048,128]{1,0:T(8,128)}, u32[]{:S(2)}, u32[]{:S(2)}) collective-permute-start(f32[2048,128]{1,0:T(8,128)} %collective-permute-done.2.refs_3_.refs_4_.refs_2_), channel_id=1, source_target_pairs={{0,1},{1,0},{2,3},{3,2},{4,5},{5,4},{6,7},{7,6},{8,9},{9,8},{10,11... | collective-permute-start | bytes 3145736 | tf_op jit(solution)/shard_map/ppermute | solution.py:265
  64.7 5.2 %copy-start.31 = (s32[2,4]{1,0:T(2,128)S(1)}, s32[2,4]{1,0:T(2,128)}, u32[]{:S(2)}) copy-start(s32[2,4]{1,0:T(2,128)} %constant.104.clone) | copy-start | bytes 100
  64.7 14.8 %collective-permute-start.7 = (f32[128,512]{1,0:T(8,128)}, f32[128,512]{1,0:T(8,128)}, u32[]{:S(2)}, u32[]{:S(2)}) collective-permute-start(f32[128,512]{1,0:T(8,128)} %get-tuple-element.82), channel_id=1, source_target_pairs={{0,4},{4,0},{8,12},{12,8},{16,20},{20,16},{24,28},{28,24},{1,5},{5... | collective-permute-start | bytes 786440 | tf_op jit(solution)/shard_map/ppermute | solution.py:235
  69.4 10.1 %collective-permute-start.6 = (f32[128,512]{1,0:T(8,128)}, f32[128,512]{1,0:T(8,128)}, u32[]{:S(2)}, u32[]{:S(2)}) collective-permute-start(f32[128,512]{1,0:T(8,128)} %get-tuple-element.80), channel_id=1, source_target_pairs={{0,4},{4,0},{8,12},{12,8},{16,20},{20,16},{24,28},{28,24},{1,5},{5... | collective-permute-start | bytes 786440 | tf_op jit(solution)/shard_map/ppermute | solution.py:235
  75.8 4.6 %copy-start.21 = (f32[128,512]{1,0:T(8,128)S(1)}, f32[128,512]{1,0:T(8,128)}, u32[]{:S(2)}) copy-start(f32[128,512]{1,0:T(8,128)} %copy-done.20) | copy-start | bytes 786436
  80.4 1.0 copy-start.9
  83.7 18.6 %collective-permute-start.14 = (f32[128,1024]{1,0:T(8,128)}, f32[128,1024]{1,0:T(8,128)S(1)}, u32[]{:S(2)}, u32[]{:S(2)}) collective-permute-start(f32[128,1024]{1,0:T(8,128)} %get-tuple-element.92), channel_id=1, source_target_pairs={{0,8},{4,12},{8,0},{12,4},{16,24},{20,28},{24,16},{28,20},{1,9},{5... | collective-permute-start | bytes 1572872 | tf_op jit(solution)/shard_map/ppermute | solution.py:418
  84.1 18.1 %collective-permute-start.15 = (f32[128,1024]{1,0:T(8,128)}, f32[128,1024]{1,0:T(8,128)}, u32[]{:S(2)}, u32[]{:S(2)}) collective-permute-start(f32[128,1024]{1,0:T(8,128)} %get-tuple-element.93.refs_8_), channel_id=1, source_target_pairs={{8,16},{12,20},{16,8},{20,12},{9,17},{13,21},{17,9},{21,13},{10,18... | collective-permute-start | bytes 1572872 | tf_op jit(solution)/shard_map/ppermute | solution.py:423
  88.7 11.4 %collective-permute-start.13 = (f32[128,256]{1,0:T(8,128)S(1)}, f32[128,256]{1,0:T(8,128)S(1)}, u32[]{:S(2)}, u32[]{:S(2)}) collective-permute-start(f32[128,256]{1,0:T(8,128)S(1)} %get-tuple-element.91), channel_id=1, source_target_pairs={{0,4},{4,0},{8,12},{12,8},{16,20},{20,16},{24,28},{28,24},{1,5},{5... | collective-permute-start | bytes 393224 | tf_op jit(solution)/shard_map/ppermute | solution.py:235
  100.1 1.7 collective-permute-start.12
  100.7 1.5 collective-permute-start.11
  102.2 8.6 %copy-start.33 = (s32[4,2]{1,0:T(4,128)S(1)}, s32[4,2]{1,0:T(4,128)}, u32[]{:S(2)}) copy-start(s32[4,2]{1,0:T(4,128)} %constant.101.clone) | copy-start | bytes 100
  106.3 19.7 %collective-permute-start.18 = (f32[128,1280]{1,0:T(8,128)}, f32[128,1280]{1,0:T(8,128)S(1)}, u32[]{:S(2)}, u32[]{:S(2)}) collective-permute-start(f32[128,1280]{1,0:T(8,128)} %get-tuple-element.100), channel_id=1, source_target_pairs={{0,8},{4,12},{8,0},{12,4},{16,24},{20,28},{24,16},{28,20},{1,9},{5... | collective-permute-start | bytes 1966088 | tf_op jit(solution)/shard_map/ppermute | solution.py:418
  109.9 15.3 %collective-permute-start.19 = (f32[128,1024]{1,0:T(8,128)}, f32[128,1024]{1,0:T(8,128)S(1)}, u32[]{:S(2)}, u32[]{:S(2)}) collective-permute-start(f32[128,1024]{1,0:T(8,128)} %get-tuple-element.101.refs_6_), channel_id=1, source_target_pairs={{8,16},{12,20},{16,8},{20,12},{9,17},{13,21},{17,9},{21,13},{10,18... | collective-permute-start | bytes 1572872 | tf_op jit(solution)/shard_map/ppermute | solution.py:423
  110.9 1.1 copy-start.1
  120.1 6.8 %copy-start.2 = (f32[128,1280]{1,0:T(8,128)S(1)}, f32[128,1280]{1,0:T(8,128)}, u32[]{:S(2)}) copy-start(f32[128,1280]{1,0:T(8,128)} %copy-done) | copy-start | bytes 1966084
  120.1 6.8 %copy-start.11 = (f32[128,1024]{1,0:T(8,128)S(1)}, f32[128,1024]{1,0:T(8,128)}, u32[]{:S(2)}) copy-start(f32[128,1024]{1,0:T(8,128)} %copy-done.10) | copy-start | bytes 1572868
  120.2 3.9 %collective-permute-start.17 = (f32[128,512]{1,0:T(8,128)S(1)}, f32[128,512]{1,0:T(8,128)S(1)}, u32[]{:S(2)}, u32[]{:S(2)}) collective-permute-start(f32[128,512]{1,0:T(8,128)S(1)} %get-tuple-element.99), channel_id=1, source_target_pairs={{0,4},{4,0},{8,12},{12,8},{16,20},{20,16},{24,28},{28,24},{1,5},{5... | collective-permute-start | bytes 786440 | tf_op jit(solution)/shard_map/ppermute | solution.py:235
  123.6 1.6 collective-permute-start.16
  126.9 1.1 copy-start.5
  128.0 1.0 copy-start.13
  130.4 17.4 %collective-permute-start.23 = (f32[128,1280]{1,0:T(8,128)S(1)}, f32[128,1280]{1,0:T(8,128)S(1)}, u32[]{:S(2)}, u32[]{:S(2)}) collective-permute-start(f32[128,1280]{1,0:T(8,128)S(1)} %get-tuple-element.109.refs_6_), channel_id=1, source_target_pairs={{8,16},{12,20},{16,8},{20,12},{9,17},{13,21},{17,9},{21,13},{10,18... | collective-permute-start | bytes 1966088 | tf_op jit(solution)/shard_map/ppermute | solution.py:423
  131.1 16.7 %collective-permute-start.22 = (f32[128,1024]{1,0:T(8,128)S(1)}, f32[128,1024]{1,0:T(8,128)S(1)}, u32[]{:S(2)}, u32[]{:S(2)}) collective-permute-start(f32[128,1024]{1,0:T(8,128)S(1)} %get-tuple-element.108), channel_id=1, source_target_pairs={{0,8},{4,12},{8,0},{12,4},{16,24},{20,28},{24,16},{28,20},{1,9},{5... | collective-permute-start | bytes 1572872 | tf_op jit(solution)/shard_map/ppermute | solution.py:418
  135.6 12.2 %collective-permute-start.24 = (f32[128,1024]{1,0:T(8,128)S(1)}, f32[128,1024]{1,0:T(8,128)S(1)}, u32[]{:S(2)}, u32[]{:S(2)}) collective-permute-start(f32[128,1024]{1,0:T(8,128)S(1)} %get-tuple-element.111.refs_0_), channel_id=1, source_target_pairs={{0,4},{4,0},{8,12},{12,8},{16,20},{20,16},{24,28},{28,24},{1,5},{5... | collective-permute-start | bytes 1572872 | tf_op jit(solution)/shard_map/ppermute | solution.py:235
  138.9 3.9 %collective-permute-start.21 = (f32[128,512]{1,0:T(8,128)S(1)}, f32[128,512]{1,0:T(8,128)S(1)}, u32[]{:S(2)}, u32[]{:S(2)}) collective-permute-start(f32[128,512]{1,0:T(8,128)S(1)} %get-tuple-element.107), channel_id=1, source_target_pairs={{0,4},{4,0},{8,12},{12,8},{16,20},{20,16},{24,28},{28,24},{1,5},{5... | collective-permute-start | bytes 786440 | tf_op jit(solution)/shard_map/ppermute | solution.py:235
  142.6 1.6 collective-permute-start.20
  148.1 7.8 %copy-start.6 = (f32[128,1024]{1,0:T(8,128)}, f32[128,1024]{1,0:T(8,128)S(1)}, u32[]{:S(2)}) copy-start(f32[128,1024]{1,0:T(8,128)S(1)} %get-tuple-element.112.refs_0_) | copy-start | bytes 1572868
  148.1 18.3 %collective-permute-start.28 = (f32[128,1280]{1,0:T(8,128)S(1)}, f32[128,1280]{1,0:T(8,128)S(1)}, u32[]{:S(2)}, u32[]{:S(2)}) collective-permute-start(f32[128,1280]{1,0:T(8,128)S(1)} %get-tuple-element.118), channel_id=1, source_target_pairs={{0,8},{4,12},{8,0},{12,4},{16,24},{20,28},{24,16},{28,20},{1,9},{5... | collective-permute-start | bytes 1966088 | tf_op jit(solution)/shard_map/ppermute | solution.py:418
  152.0 9.4 %collective-permute-start.25 = (f32[128,1024]{1,0:T(8,128)S(1)}, f32[128,1024]{1,0:T(8,128)S(1)}, u32[]{:S(2)}, u32[]{:S(2)}) collective-permute-start(f32[128,1024]{1,0:T(8,128)S(1)} %get-tuple-element.112.refs_0_), channel_id=1, source_target_pairs={{0,4},{4,0},{8,12},{12,8},{16,20},{20,16},{24,28},{28,24},{1,5},{5... | collective-permute-start | bytes 1572872 | tf_op jit(solution)/shard_map/ppermute | solution.py:235
  152.0 9.4 %collective-permute-start.29 = (f32[128,1024]{1,0:T(8,128)S(1)}, f32[128,1024]{1,0:T(8,128)S(1)}, u32[]{:S(2)}, u32[]{:S(2)}) collective-permute-start(f32[128,1024]{1,0:T(8,128)S(1)} %get-tuple-element.119.refs_6_), channel_id=1, source_target_pairs={{8,16},{12,20},{16,8},{20,12},{9,17},{13,21},{17,9},{21,13},{10,18... | collective-permute-start | bytes 1572872 | tf_op jit(solution)/shard_map/ppermute | solution.py:423
  155.9 3.9 %collective-permute-start.27 = (f32[128,512]{1,0:T(8,128)S(1)}, f32[128,512]{1,0:T(8,128)S(1)}, u32[]{:S(2)}, u32[]{:S(2)}) collective-permute-start(f32[128,512]{1,0:T(8,128)S(1)} %get-tuple-element.117), channel_id=1, source_target_pairs={{0,4},{4,0},{8,12},{12,8},{16,20},{20,16},{24,28},{28,24},{1,5},{5... | collective-permute-start | bytes 786440 | tf_op jit(solution)/shard_map/ppermute | solution.py:235
  159.7 1.6 collective-permute-start.26
  166.4 3.5 %copy-start.28 = (s32[4,6]{1,0:T(4,128)S(1)}, s32[4,6]{1,0:T(4,128)}, u32[]{:S(2)}) copy-start(s32[4,6]{1,0:T(4,128)} %constant.103.clone) | copy-start | bytes 292
  166.4 3.5 %copy-start.29 = (s32[4,6]{1,0:T(4,128)S(1)}, s32[4,6]{1,0:T(4,128)}, u32[]{:S(2)}) copy-start(s32[4,6]{1,0:T(4,128)} %constant.102.clone) | copy-start | bytes 292
  166.4 8.8 %copy-start.30 = (s32[2,3]{1,0:T(2,128)S(1)}, s32[2,3]{1,0:T(2,128)}, u32[]{:S(2)}) copy-start(s32[2,3]{1,0:T(2,128)} %constant.106.clone) | copy-start | bytes 76
  170.0 3.6 %collective-permute-start.32 = (f32[128,1280]{1,0:T(8,128)S(1)}, f32[128,1280]{1,0:T(8,128)S(1)}, u32[]{:S(2)}, u32[]{:S(2)}) collective-permute-start(f32[128,1280]{1,0:T(8,128)S(1)} %get-tuple-element.125.refs_2_), channel_id=1, source_target_pairs={{0,4},{4,0},{8,12},{12,8},{16,20},{20,16},{24,28},{28,24},{1,5},{5... | collective-permute-start | bytes 1966088 | tf_op jit(solution)/shard_map/ppermute | solution.py:235
  170.2 14.8 %collective-permute-start.30 = (f32[128,1024]{1,0:T(8,128)}, f32[128,1024]{1,0:T(8,128)}, u32[]{:S(2)}, u32[]{:S(2)}) collective-permute-start(f32[128,1024]{1,0:T(8,128)} %copy-done.24), channel_id=1, source_target_pairs={{0,8},{4,12},{8,0},{12,4},{16,24},{20,28},{24,16},{28,20},{1,9},{5... | collective-permute-start | bytes 1572872 | tf_op jit(solution)/shard_map/ppermute | solution.py:418
  172.2 12.9 %collective-permute-start.31 = (f32[128,1024]{1,0:T(8,128)}, f32[128,1024]{1,0:T(8,128)}, u32[]{:S(2)}, u32[]{:S(2)}) collective-permute-start(f32[128,1024]{1,0:T(8,128)} %copy-done.16), channel_id=1, source_target_pairs={{8,16},{12,20},{16,8},{20,12},{9,17},{13,21},{17,9},{21,13},{10,18... | collective-permute-start | bytes 1572872 | tf_op jit(solution)/shard_map/ppermute | solution.py:423
  173.6 20.6 %collective-permute-start.38 = (f32[256,256]{1,0:T(8,128)S(1)}, f32[256,256]{1,0:T(8,128)S(1)}, u32[]{:S(2)}, u32[]{:S(2)}) collective-permute-start(f32[256,256]{1,0:T(8,128)S(1)} %maximum_select_fusion), channel_id=1, source_target_pairs={{0,3},{1,2},{2,1},{3,0},{4,7},{5,6},{6,5},{7,4},{8,11},{9,10},{10,... | collective-permute-start | bytes 786440 | tf_op jit(solution)/shard_map/ppermute | solution.py:434
  175.3 19.1 %collective-permute-start.37 = (f32[256,256]{1,0:T(8,128)S(1)}, f32[256,256]{1,0:T(8,128)}, u32[]{:S(2)}, u32[]{:S(2)}) collective-permute-start(f32[256,256]{1,0:T(8,128)S(1)} %maximum_select_fusion), channel_id=1, source_target_pairs={{0,2},{1,3},{2,0},{3,1},{4,6},{5,7},{6,4},{7,5},{8,10},{9,11},{10,... | collective-permute-start | bytes 786440 | tf_op jit(solution)/shard_map/ppermute | solution.py:434
  175.8 18.6 %collective-permute-start.36 = (f32[256,256]{1,0:T(8,128)S(1)}, f32[256,256]{1,0:T(8,128)}, u32[]{:S(2)}, u32[]{:S(2)}) collective-permute-start(f32[256,256]{1,0:T(8,128)S(1)} %maximum_select_fusion), channel_id=1, source_target_pairs={{0,1},{1,0},{2,3},{3,2},{4,5},{5,4},{6,7},{7,6},{8,9},{9,8},{10,11... | collective-permute-start | bytes 786440 | tf_op jit(solution)/shard_map/ppermute | solution.py:434
  185.1 1.0 copy-start.15
  186.1 1.0 copy-start.17
  187.2 1.0 copy-start.19
  189.6 6.6 %copy-start.3 = (f32[3,256,256]{2,1,0:T(8,128)S(1)}, f32[3,256,256]{2,1,0:T(8,128)}, u32[]{:S(2)}) copy-start(f32[3,256,256]{2,1,0:T(8,128)} %refs_6_.5) | copy-start | bytes 2359300
  189.6 18.6 %collective-permute-start.33 = (f32[128,1024]{1,0:T(8,128)S(1)}, f32[128,1024]{1,0:T(8,128)S(1)}, u32[]{:S(2)}, u32[]{:S(2)}) collective-permute-start(f32[128,1024]{1,0:T(8,128)S(1)} %get-tuple-element.126), channel_id=1, source_target_pairs={{0,8},{4,12},{8,0},{12,4},{16,24},{20,28},{24,16},{28,20},{1,9},{5... | collective-permute-start | bytes 1572872 | tf_op jit(solution)/shard_map/ppermute | solution.py:418
  193.3 14.9 %collective-permute-start.34 = (f32[128,1024]{1,0:T(8,128)S(1)}, f32[128,1024]{1,0:T(8,128)S(1)}, u32[]{:S(2)}, u32[]{:S(2)}) collective-permute-start(f32[128,1024]{1,0:T(8,128)S(1)} %get-tuple-element.127.refs_1_), channel_id=1, source_target_pairs={{8,16},{12,20},{16,8},{20,12},{9,17},{13,21},{17,9},{21,13},{10,18... | collective-permute-start | bytes 1572872 | tf_op jit(solution)/shard_map/ppermute | solution.py:423
  194.3 2.0 collective-permute-start.35
  208.4 14.6 %collective-permute-start.40 = (f32[128,1024]{1,0:T(8,128)S(1)}, f32[128,1024]{1,0:T(8,128)S(1)}, u32[]{:S(2)}, u32[]{:S(2)}) collective-permute-start(f32[128,1024]{1,0:T(8,128)S(1)} %get-tuple-element.135), channel_id=1, source_target_pairs={{0,8},{4,12},{8,0},{12,4},{16,24},{20,28},{24,16},{28,20},{1,9},{5... | collective-permute-start | bytes 1572872 | tf_op jit(solution)/shard_map/ppermute | solution.py:418
  210.7 12.6 %collective-permute-start.39 = (f32[128,1024]{1,0:T(8,128)S(1)}, f32[128,1024]{1,0:T(8,128)S(1)}, u32[]{:S(2)}, u32[]{:S(2)}) collective-permute-start(f32[128,1024]{1,0:T(8,128)S(1)} %get-tuple-element.134.refs_2_), channel_id=1, source_target_pairs={{0,4},{4,0},{8,12},{12,8},{16,20},{20,16},{24,28},{28,24},{1,5},{5... | collective-permute-start | bytes 1572872 | tf_op jit(solution)/shard_map/ppermute | solution.py:235
  210.7 14.2 %copy-start.7 = (f32[128,1024]{1,0:T(8,128)S(1)}, f32[128,1024]{1,0:T(8,128)}, u32[]{:S(2)}) copy-start(f32[128,1024]{1,0:T(8,128)} %copy-done.6) | copy-start | bytes 1572868
  223.0 2.0 collective-permute-start.41
  (12 other events, 9.8 us)

commit v3 on v2

--- a/solution.py
+++ b/solution.py
@@ -407,8 +407,6 @@
         if sent:
             shapes["out"] = max(sent, key=lambda shape: shape[1])
         ahead = [] if out is None else [finished]
-        if step + 1 == chunks.index((PANELS - 1, 0)):
-            ahead.extend(map(pinned, rounds[-1][0][:2]))
         if step == gram_chunk - 1:
             ahead.extend([gram_sides[0], pinned(gram_sides[1])])
         if 0 <= outward - 1 < count - 2:

time: 245 us -> 239 us (0.976)
  local copies, waits for them, and re-layouts: 22.9 us -> 17.1 us
    ppermute x6, waiting for transfers between devices: 17.9 us -> 9.55 us  [fetch_square(): along = lambda value, step: lax.ppermute(value, 'col', pairs_of(4, step))]
    ppermute x8, waiting for transfers between devices: 10.2 us -> 18 us  [shards_square(): outer[step] = lax.ppermute(results['out'], 'row', outer_pairs)]
    unnamed x68 -> x50, local copies, waits for them, and re-layouts: 17.3 us -> 11.6 us
  transfers between devices with their start and end apart: 42 -> 42, of which waited for: 14 -> 13; matrix products, arithmetic and copies ran while one was open for 2% -> 3% of each run, Pallas kernels for 45% -> 46%
where the time goes in v3:
time: 239 us; the launch traced here: 237 us
  Pallas kernels  131 us (55%)
  starting transfers between devices  42.1 us (18%)
  waiting for transfers between devices  36.5 us (15%)
  local copies, waits for them, and re-layouts  17.1 us (7%)
  between operations  7.27 us (3%)
  other arithmetic  3.4 us (1%)
    pallas_call x13, Pallas kernels, products(): pl.pallas_call(functools.partial(products_kernel, block), in_specs=[in_vm...  43.8 us
    pallas_call x3, Pallas kernels, update(): pl.pallas_call(functools.partial(update_kernel, offset), grid_spec=pltpu....  42.6 us
    pallas_call x5, Pallas kernels, choose(): pl.pallas_call(functools.partial(choose_kernel, outputs, len(cases)), in_...  22.9 us
    ppermute x8, starting transfers between devices, shards_square(): outer[step] = lax.ppermute(results['out'], 'row', outer_pairs)  21.5 us
    ppermute x8, waiting for transfers between devices, shards_square(): outer[step] = lax.ppermute(results['out'], 'row', outer_pairs)  18 us
    pallas_call x1, Pallas kernels, split_array(): pl.pallas_call(split_kernel, grid=(rows // step,), in_specs=[pl.BlockSpec...  14.6 us
    unnamed x50, local copies, waits for them, and re-layouts  11.6 us
    ppermute x6, waiting for transfers between devices, fetch_square(): along = lambda value, step: lax.ppermute(value, 'col', pairs_of(4, step))  9.55 us
  transfers between devices with their start and end apart: 42, of which 13 were waited for; matrix products, arithmetic and copies ran while one was open for 3% of the time, Pallas kernels for 46%

profile of v3, /device:TPU:0, one launch (start us, length us, event | category | flops | bytes accessed | tf_op | source)
XLA Modules:
  0.0 237.2 jit_solution(12042391594291889132)
XLA Ops:
  0.0 3.0 %fusion.14 = (f32[2048,128]{1,0:T(8,128)}, f32[2048,128]{1,0:T(8,128)}) fusion(f32[2048,256]{1,0:T(8,128)} %bitcast.37), kind=kLoop, calls=%fused_computation.37 | loop fusion | bytes 4194304 | tf_op jit(solution)/shard_map/slice | solution.py:266
  3.0 3.0 %collective-permute-start.2 = (f32[2048,128]{1,0:T(8,128)}, f32[2048,128]{1,0:T(8,128)}, u32[]{:S(2)}, u32[]{:S(2)}) collective-permute-start(f32[2048,128]{1,0:T(8,128)} %get-tuple-element.142.refs_0_), channel_id=1, source_target_pairs={{0,2},{1,3},{2,0},{3,1},{4,6},{5,7},{6,4},{7,5},{8,10},{9,11},{10,... | collective-permute-start | bytes 3145736 | tf_op jit(solution)/shard_map/ppermute | solution.py:265
  6.0 1.5 collective-permute-start
  8.1 14.6 %split_x.1.both_ref = bf16[4,2,2048,512]{3,2,1,0:T(8,128)(2,1)} custom-call(f32[2048,2048]{1,0:T(8,128)} %refs_11_.5), custom_call_target="tpu_custom_call" | custom-call | flops 262144 | bytes 524288 | tf_op jit(solution)/shard_map/split_x/pallas_call | solution.py:60
  22.8 7.4 %collective-permute-done.2.refs_3_.refs_4_.refs_2_ = f32[2048,128]{1,0:T(8,128)} collective-permute-done((f32[2048,128]{1,0:T(8,128)}, f32[2048,128]{1,0:T(8,128)}, u32[]{:S(2)}, u32[]{:S(2)}) %collective-permute-start.2) | collective-permute-done | bytes 1048608 | tf_op jit(solution)/shard_map/ppermute | solution.py:265
  30.3 2.1 collective-permute-done.refs_2_.refs_0_
  32.4 4.8 %choose_panel.5 = (bf16[1,2,2048,256]{3,2,1,0:T(8,128)(2,1)}, bf16[512,2048]{1,0:T(8,128)(2,1)S(1)}) custom-call(s32[2]{0:T(128)S(1)} %broadcast_select_fusion.2.which_ref, f32[2048,128]{1,0:T(8,128)} %get-tuple-element.142.refs_0_, f32[2048,128]{1,0:T(8,128)} %get-tuple-element.141.refs_1_, f32[2048,128]{1,0:T(8,128)} %collective-permute-done.refs_2_.refs_0_, ...), custom_call_target="tpu_custom_call" | custom-call | flops 32768 | bytes 98304 | tf_op jit(solution)/shard_map/choose_panel/pallas_call | solution.py:106
  37.2 3.2 %products.14 = (f32[128,512]{1,0:T(8,128)S(1)}, f32[128,512]{1,0:T(8,128)S(1)}) custom-call(bf16[512,2048]{1,0:T(8,128)(2,1)S(1)} %get-tuple-element.73.flipped_ref, bf16[4,2,2048,512]{3,2,1,0:T(8,128)(2,1)} %split_x.1.both_ref), custom_call_target="tpu_custom_call" | custom-call | flops 25165824 | bytes 98304 | tf_op jit(solution)/shard_map/products/pallas_call | solution.py:150
  40.5 3.9 %products.13 = (f32[128,512]{1,0:T(8,128)S(1)}, f32[128,512]{1,0:T(8,128)}) custom-call(bf16[512,2048]{1,0:T(8,128)(2,1)S(1)} %get-tuple-element.73.flipped_ref, bf16[4,2,2048,512]{3,2,1,0:T(8,128)(2,1)} %split_x.1.both_ref), custom_call_target="tpu_custom_call" | custom-call | flops 25165824 | bytes 98304 | tf_op jit(solution)/shard_map/products/pallas_call | solution.py:150
  45.0 1.4 collective-permute-done.4.refs_1_
  47.1 0.9 copy-done.16
  48.0 0.9 exchange.9
  48.9 1.6 collective-permute-start.8
  51.8 3.9 %products.16 = (f32[128,512]{1,0:T(8,128)S(1)}, f32[128,512]{1,0:T(8,128)}) custom-call(bf16[512,2048]{1,0:T(8,128)(2,1)S(1)} %get-tuple-element.73.flipped_ref, bf16[4,2,2048,512]{3,2,1,0:T(8,128)(2,1)} %split_x.1.both_ref, f32[128,1024]{1,0:T(8,128)S(1)} %get-tuple-element.78.refs_0_.refs_6_.refs_5_), custom_call_target="tpu_custom_call" | custom-call | flops 25165824 | bytes 98304 | tf_op jit(solution)/shard_map/products/pallas_call | solution.py:150
  55.8 3.9 %products.15 = (f32[128,512]{1,0:T(8,128)S(1)}, f32[128,512]{1,0:T(8,128)}) custom-call(bf16[512,2048]{1,0:T(8,128)(2,1)S(1)} %get-tuple-element.73.flipped_ref, bf16[4,2,2048,512]{3,2,1,0:T(8,128)(2,1)} %split_x.1.both_ref, f32[128,1024]{1,0:T(8,128)S(1)} %get-tuple-element.78.refs_0_.refs_6_.refs_5_), custom_call_target="tpu_custom_call" | custom-call | flops 25165824 | bytes 98304 | tf_op jit(solution)/shard_map/products/pallas_call | solution.py:150
  62.3 1.6 collective-permute-start.9
  64.4 4.6 %choose_panel.7.refs_7_.both_ref = bf16[1,2,2048,256]{3,2,1,0:T(8,128)(2,1)} custom-call(s32[2]{0:T(128)S(1)} %iota_add_fusion.which_ref, f32[2048,128]{1,0:T(8,128)} %get-tuple-element.142.refs_0_, f32[2048,128]{1,0:T(8,128)} %get-tuple-element.141.refs_1_, f32[2048,128]{1,0:T(8,128)} %collective-permute-done.refs_2_.refs_0_, ...), custom_call_target="tpu_custom_call" | custom-call | flops 32768 | bytes 98304 | tf_op jit(solution)/shard_map/choose_panel/pallas_call | solution.py:106
  69.0 3.7 %choose_panel.6.refs_6_.flipped_ref = bf16[512,2048]{1,0:T(8,128)(2,1)S(1)} custom-call(s32[2]{0:T(128)S(1)} %broadcast_select_fusion.1.which_ref, f32[2048,128]{1,0:T(8,128)} %get-tuple-element.142.refs_0_, f32[2048,128]{1,0:T(8,128)} %get-tuple-element.141.refs_1_, f32[2048,128]{1,0:T(8,128)} %collective-permute-done.refs_2_.refs_0_, ...), custom_call_target="tpu_custom_call" | custom-call | flops 32768 | bytes 98304 | tf_op jit(solution)/shard_map/choose_panel/pallas_call | solution.py:106
  72.7 1.1 exchange.10
  73.8 3.0 %products.19 = (f32[128,256]{1,0:T(8,128)S(1)}, f32[128,256]{1,0:T(8,128)S(1)}) custom-call(bf16[512,2048]{1,0:T(8,128)(2,1)S(1)} %choose_panel.6.refs_6_.flipped_ref, bf16[1,2,2048,256]{3,2,1,0:T(8,128)(2,1)} %choose_panel.7.refs_7_.both_ref, f32[128,1024]{1,0:T(8,128)S(1)} %get-tuple-element.84.refs_4_.refs_0_.refs_7_), custom_call_target="tpu_custom_call" | custom-call | flops 12582912 | bytes 65536 | tf_op jit(solution)/shard_map/products/pallas_call | solution.py:150
  76.9 4.9 %choose_panel.8 = (bf16[1,2,2048,256]{3,2,1,0:T(8,128)(2,1)}, bf16[512,2048]{1,0:T(8,128)(2,1)S(1)}) custom-call(s32[2]{0:T(128)S(1)} %broadcast_select_fusion.3.which_ref, f32[2048,128]{1,0:T(8,128)} %collective-permute-done.refs_2_.refs_0_, f32[2048,128]{1,0:T(8,128)} %collective-permute-done.1.refs_3_.refs_1_.refs_2_, ...), custom_call_target="tpu_custom_call" | custom-call | flops 32768 | bytes 98304 | tf_op jit(solution)/shard_map/choose_panel/pallas_call | solution.py:106
  81.9 3.2 %products.18 = (f32[128,512]{1,0:T(8,128)S(1)}, f32[128,512]{1,0:T(8,128)S(1)}) custom-call(bf16[512,2048]{1,0:T(8,128)(2,1)S(1)} %get-tuple-element.85.flipped_ref, bf16[4,2,2048,512]{3,2,1,0:T(8,128)(2,1)} %split_x.1.both_ref, f32[128,1024]{1,0:T(8,128)S(1)} %get-tuple-element.84.refs_4_.refs_0_.refs_7_), custom_call_target="tpu_custom_call" | custom-call | flops 25165824 | bytes 98304 | tf_op jit(solution)/shard_map/products/pallas_call | solution.py:150
  86.8 3.2 %products.17 = (f32[128,512]{1,0:T(8,128)S(1)}, f32[128,512]{1,0:T(8,128)S(1)}) custom-call(bf16[512,2048]{1,0:T(8,128)(2,1)S(1)} %get-tuple-element.85.flipped_ref, bf16[4,2,2048,512]{3,2,1,0:T(8,128)(2,1)} %split_x.1.both_ref, f32[128,1024]{1,0:T(8,128)S(1)} %get-tuple-element.84.refs_4_.refs_0_.refs_7_), custom_call_target="tpu_custom_call" | custom-call | flops 25165824 | bytes 98304 | tf_op jit(solution)/shard_map/products/pallas_call | solution.py:150
  90.1 1.5 collective-permute-done.11.refs_1_
  91.6 7.9 %collective-permute-done.14.refs_6_ = f32[128,1024]{1,0:T(8,128)S(1)} collective-permute-done((f32[128,1024]{1,0:T(8,128)S(1)}, f32[128,1024]{1,0:T(8,128)S(1)}, u32[]{:S(2)}, u32[]{:S(2)}) %collective-permute-start.14) | collective-permute-done | bytes 524320 | tf_op jit(solution)/shard_map/ppermute | solution.py:416
  99.5 1.2 exchange.11
  101.5 3.6 %collective-permute-start.18 = (f32[128,1280]{1,0:T(8,128)}, f32[128,1280]{1,0:T(8,128)S(1)}, u32[]{:S(2)}, u32[]{:S(2)}) collective-permute-start(f32[128,1280]{1,0:T(8,128)} %get-tuple-element.100), channel_id=1, source_target_pairs={{0,8},{4,12},{8,0},{12,4},{16,24},{20,28},{24,16},{28,20},{1,9},{5... | collective-permute-start | bytes 1966088 | tf_op jit(solution)/shard_map/ppermute | solution.py:416
  105.2 1.5 collective-permute-start.19
  106.8 4.9 %choose_panel.9 = (bf16[1,2,2048,256]{3,2,1,0:T(8,128)(2,1)}, bf16[512,2048]{1,0:T(8,128)(2,1)S(1)}) custom-call(s32[2]{0:T(128)S(1)} %broadcast_select_fusion.which_ref, f32[2048,128]{1,0:T(8,128)} %collective-permute-done.9.refs_0_, f32[2048,128]{1,0:T(8,128)} %collective-permute-done.10.refs_1_, ...), custom_call_target="tpu_custom_call" | custom-call | flops 32768 | bytes 98304 | tf_op jit(solution)/shard_map/choose_panel/pallas_call | solution.py:106
  111.6 3.2 %products.21 = (f32[128,512]{1,0:T(8,128)S(1)}, f32[128,512]{1,0:T(8,128)S(1)}) custom-call(bf16[512,2048]{1,0:T(8,128)(2,1)S(1)} %get-tuple-element.95.flipped_ref, bf16[4,2,2048,512]{3,2,1,0:T(8,128)(2,1)} %split_x.1.both_ref, f32[128,1280]{1,0:T(8,128)S(1)} %get-tuple-element.94.refs_4_.refs_0_.refs_5_), custom_call_target="tpu_custom_call" | custom-call | flops 25165824 | bytes 98304 | tf_op jit(solution)/shard_map/products/pallas_call | solution.py:150
  115.0 3.3 %products.20 = (f32[128,512]{1,0:T(8,128)S(1)}, f32[128,512]{1,0:T(8,128)S(1)}) custom-call(bf16[512,2048]{1,0:T(8,128)(2,1)S(1)} %get-tuple-element.95.flipped_ref, bf16[4,2,2048,512]{3,2,1,0:T(8,128)(2,1)} %split_x.1.both_ref, f32[128,1280]{1,0:T(8,128)S(1)} %get-tuple-element.94.refs_4_.refs_0_.refs_5_), custom_call_target="tpu_custom_call" | custom-call | flops 25165824 | bytes 98304 | tf_op jit(solution)/shard_map/products/pallas_call | solution.py:150
  118.8 1.2 collective-permute-done.16.refs_1_
  120.0 0.9 copy-done.1
  120.9 1.1 copy-done.2
  121.9 1.5 exchange.12
  124.2 4.0 %collective-permute-start.22 = (f32[128,1024]{1,0:T(8,128)S(1)}, f32[128,1024]{1,0:T(8,128)S(1)}, u32[]{:S(2)}, u32[]{:S(2)}) collective-permute-start(f32[128,1024]{1,0:T(8,128)S(1)} %get-tuple-element.108), channel_id=1, source_target_pairs={{0,8},{4,12},{8,0},{12,4},{16,24},{20,28},{24,16},{28,20},{1,9},{5... | collective-permute-start | bytes 1572872 | tf_op jit(solution)/shard_map/ppermute | solution.py:416
  128.1 3.2 %products.23 = (f32[128,512]{1,0:T(8,128)S(1)}, f32[128,512]{1,0:T(8,128)S(1)}) custom-call(bf16[512,2048]{1,0:T(8,128)(2,1)S(1)} %get-tuple-element.85.flipped_ref, bf16[4,2,2048,512]{3,2,1,0:T(8,128)(2,1)} %split_x.1.both_ref, f32[128,1024]{1,0:T(8,128)S(1)} %get-tuple-element.103.refs_0_.refs_5_), custom_call_target="tpu_custom_call" | custom-call | flops 25165824 | bytes 98304 | tf_op jit(solution)/shard_map/products/pallas_call | solution.py:150
  131.9 3.2 %products.22 = (f32[128,512]{1,0:T(8,128)S(1)}, f32[128,512]{1,0:T(8,128)S(1)}) custom-call(bf16[512,2048]{1,0:T(8,128)(2,1)S(1)} %get-tuple-element.85.flipped_ref, bf16[4,2,2048,512]{3,2,1,0:T(8,128)(2,1)} %split_x.1.both_ref, f32[128,1024]{1,0:T(8,128)S(1)} %get-tuple-element.103.refs_0_.refs_5_), custom_call_target="tpu_custom_call" | custom-call | flops 25165824 | bytes 98304 | tf_op jit(solution)/shard_map/products/pallas_call | solution.py:150
  135.2 1.5 collective-permute-done.20.refs_1_
  136.7 3.6 %collective-permute-done.22.refs_4_ = f32[128,1024]{1,0:T(8,128)S(1)} collective-permute-done((f32[128,1024]{1,0:T(8,128)S(1)}, f32[128,1024]{1,0:T(8,128)S(1)}, u32[]{:S(2)}, u32[]{:S(2)}) %collective-permute-start.22) | collective-permute-done | bytes 524320 | tf_op jit(solution)/shard_map/ppermute | solution.py:416
  140.6 4.3 %collective-permute-start.28 = (f32[128,1280]{1,0:T(8,128)S(1)}, f32[128,1280]{1,0:T(8,128)S(1)}, u32[]{:S(2)}, u32[]{:S(2)}) collective-permute-start(f32[128,1280]{1,0:T(8,128)S(1)} %get-tuple-element.118), channel_id=1, source_target_pairs={{0,8},{4,12},{8,0},{12,4},{16,24},{20,28},{24,16},{28,20},{1,9},{5... | collective-permute-start | bytes 1966088 | tf_op jit(solution)/shard_map/ppermute | solution.py:416
  145.6 3.2 %products.25 = (f32[128,512]{1,0:T(8,128)S(1)}, f32[128,512]{1,0:T(8,128)S(1)}) custom-call(bf16[512,2048]{1,0:T(8,128)(2,1)S(1)} %get-tuple-element.95.flipped_ref, bf16[4,2,2048,512]{3,2,1,0:T(8,128)(2,1)} %split_x.1.both_ref, f32[128,1024]{1,0:T(8,128)S(1)} %get-tuple-element.113.refs_0_.refs_5_), custom_call_target="tpu_custom_call" | custom-call | flops 25165824 | bytes 98304 | tf_op jit(solution)/shard_map/products/pallas_call | solution.py:150
  149.5 3.2 %products.24 = (f32[128,512]{1,0:T(8,128)S(1)}, f32[128,512]{1,0:T(8,128)S(1)}) custom-call(bf16[512,2048]{1,0:T(8,128)(2,1)S(1)} %get-tuple-element.95.flipped_ref, bf16[4,2,2048,512]{3,2,1,0:T(8,128)(2,1)} %split_x.1.both_ref, f32[128,1024]{1,0:T(8,128)S(1)} %get-tuple-element.113.refs_0_.refs_5_), custom_call_target="tpu_custom_call" | custom-call | flops 25165824 | bytes 98304 | tf_op jit(solution)/shard_map/products/pallas_call | solution.py:150
  152.8 1.5 collective-permute-done.26.refs_1_
  154.3 5.1 %collective-permute-done.28.refs_4_ = f32[128,1280]{1,0:T(8,128)S(1)} collective-permute-done((f32[128,1280]{1,0:T(8,128)S(1)}, f32[128,1280]{1,0:T(8,128)S(1)}, u32[]{:S(2)}, u32[]{:S(2)}) %collective-permute-start.28) | collective-permute-done | bytes 655392 | tf_op jit(solution)/shard_map/ppermute | solution.py:416
  159.7 0.9 copy-done.7
  161.3 0.8 copy-done.11
  163.9 1.9 collective-permute-start.30
  165.8 1.4 collective-permute-start.31
  167.3 1.6 collective-permute-start.38
  170.1 1.5 collective-permute-start.36
  177.7 1.0 collective-permute-done.30.refs_0_
  178.7 1.0 copy-done.8
  179.7 1.0 copy-done.10
  180.8 1.0 copy-done.12
  181.8 1.4 exchange.15
  183.3 3.7 %collective-permute-start.33 = (f32[128,1024]{1,0:T(8,128)S(1)}, f32[128,1024]{1,0:T(8,128)S(1)}, u32[]{:S(2)}, u32[]{:S(2)}) collective-permute-start(f32[128,1024]{1,0:T(8,128)S(1)} %get-tuple-element.126), channel_id=1, source_target_pairs={{0,8},{4,12},{8,0},{12,4},{16,24},{20,28},{24,16},{28,20},{1,9},{5... | collective-permute-start | bytes 1572872 | tf_op jit(solution)/shard_map/ppermute | solution.py:416
  187.0 0.9 collective-permute-start.34
  188.7 1.1 select_bitcast_fusion.2
  189.9 12.0 %update.3 = (f32[2048,2048]{1,0:T(8,128)}, f32[8,128]{1,0:T(8,128)S(1)}) custom-call(s32[6]{0:T(128)S(1)} %broadcast_select_fusion.4.place_ref, f32[128,1024]{1,0:T(8,128)S(1)} %get-tuple-element.111.refs_0_, f32[128,1024]{1,0:T(8,128)S(1)} %collective-permute-done.24.refs_9_.refs_1_, f32[128,1280]{1,0:T(8,128)S(1)} %get-tuple-element.125.refs_2_, ...), custom_call_target="tpu_custom_call" | custom-call | flops 75497472 | bytes 229376 | tf_op jit(solution)/shard_map/update/pallas_call | solution.py:209
  202.1 1.9 collective-permute-start.40
  204.2 12.0 %update.4 = (f32[2048,2048]{1,0:T(8,128)}, f32[8,128]{1,0:T(8,128)S(1)}) custom-call(s32[6]{0:T(128)S(1)} %broadcast_select_fusion.4.place_ref, f32[128,1024]{1,0:T(8,128)S(1)} %get-tuple-element.111.refs_0_, f32[128,1024]{1,0:T(8,128)S(1)} %collective-permute-done.24.refs_9_.refs_1_, ...), custom_call_target="tpu_custom_call", output_to_operand_aliasing={{0}: (13, {})} | custom-call | flops 75497472 | bytes 229376 | tf_op jit(solution)/shard_map/update/pallas_call | solution.py:209
  216.7 1.9 collective-permute-done.41.refs_5_
  218.6 18.6 %update.5 = (f32[2048,2048]{1,0:T(8,128)}, f32[8,128]{1,0:T(8,128)}) custom-call(s32[6]{0:T(128)S(1)} %broadcast_select_fusion.4.place_ref, f32[128,1024]{1,0:T(8,128)S(1)} %copy-done.4, f32[128,1024]{1,0:T(8,128)S(1)} %collective-permute-done.25.refs_9_.refs_1_, f32[128,1024]{1,0:T(8,128)S(1)} %get-tuple-element.134.refs_2_, ...), custom_call_target="tpu_custom_call", output_to_operand_aliasing={{0}: (13, {})} | custom-call | flops 150994944 | bytes 360448 | tf_op jit(solution)/shard_map/update/pallas_call | solution.py:209
  (130 shorter events, 18.1 us)
Async XLA Ops:
  0.0 8.0 %copy-start.18 = (s32[3]{0:T(128)S(1)}, s32[3]{0:T(128)}, u32[]{:S(2)}) copy-start(s32[3]{0:T(128)} %param.14) | copy-start | bytes 40
  0.0 8.1 %copy-start.19 = (s32[4,2]{1,0:T(4,128)S(1)}, s32[4,2]{1,0:T(4,128)}, u32[]{:S(2)}) copy-start(s32[4,2]{1,0:T(4,128)} %constant.100.clone) | copy-start | bytes 100
  0.0 8.1 %copy-start.20 = (s32[4,2]{1,0:T(4,128)S(1)}, s32[4,2]{1,0:T(4,128)}, u32[]{:S(2)}) copy-start(s32[4,2]{1,0:T(4,128)} %constant.99.clone) | copy-start | bytes 100
  3.0 27.3 %collective-permute-start.2 = (f32[2048,128]{1,0:T(8,128)}, f32[2048,128]{1,0:T(8,128)}, u32[]{:S(2)}, u32[]{:S(2)}) collective-permute-start(f32[2048,128]{1,0:T(8,128)} %get-tuple-element.142.refs_0_), channel_id=1, source_target_pairs={{0,2},{1,3},{2,0},{3,1},{4,6},{5,7},{6,4},{7,5},{8,10},{9,11},{10,... | collective-permute-start | bytes 3145736 | tf_op jit(solution)/shard_map/ppermute | solution.py:265
  6.0 26.4 %collective-permute-start = (f32[2048,128]{1,0:T(8,128)}, f32[2048,128]{1,0:T(8,128)}, u32[]{:S(2)}, u32[]{:S(2)}) collective-permute-start(f32[2048,128]{1,0:T(8,128)} %get-tuple-element.142.refs_0_), channel_id=1, source_target_pairs={{0,1},{1,0},{2,3},{3,2},{4,5},{5,4},{6,7},{7,6},{8,9},{9,8},{10,11... | collective-permute-start | bytes 3145736 | tf_op jit(solution)/shard_map/ppermute | solution.py:265
  7.5 54.8 %collective-permute-start.3 = (f32[2048,128]{1,0:T(8,128)}, f32[2048,128]{1,0:T(8,128)}, u32[]{:S(2)}, u32[]{:S(2)}) collective-permute-start(f32[2048,128]{1,0:T(8,128)} %get-tuple-element.141.refs_1_), channel_id=1, source_target_pairs={{0,2},{1,3},{2,0},{3,1},{4,6},{5,7},{6,4},{7,5},{8,10},{9,11},{10,... | collective-permute-start | bytes 3145736 | tf_op jit(solution)/shard_map/ppermute | solution.py:265
  8.0 55.9 %collective-permute-start.1 = (f32[2048,128]{1,0:T(8,128)}, f32[2048,128]{1,0:T(8,128)}, u32[]{:S(2)}, u32[]{:S(2)}) collective-permute-start(f32[2048,128]{1,0:T(8,128)} %get-tuple-element.141.refs_1_), channel_id=1, source_target_pairs={{0,1},{1,0},{2,3},{3,2},{4,5},{5,4},{6,7},{7,6},{8,9},{9,8},{10,11... | collective-permute-start | bytes 3145736 | tf_op jit(solution)/shard_map/ppermute | solution.py:265
  40.5 10.1 %copy-start.23 = (s32[2,4]{1,0:T(2,128)S(1)}, s32[2,4]{1,0:T(2,128)}, u32[]{:S(2)}) copy-start(s32[2,4]{1,0:T(2,128)} %constant.105.clone) | copy-start | bytes 100
  40.5 4.6 %collective-permute-start.5 = (f32[128,512]{1,0:T(8,128)S(1)}, f32[128,512]{1,0:T(8,128)S(1)}, u32[]{:S(2)}, u32[]{:S(2)}) collective-permute-start(f32[128,512]{1,0:T(8,128)S(1)} %get-tuple-element.77), channel_id=1, source_target_pairs={{0,4},{4,0},{8,12},{12,8},{16,20},{20,16},{24,28},{28,24},{1,5},{5... | collective-permute-start | bytes 786440 | tf_op jit(solution)/shard_map/ppermute | solution.py:235
  44.5 1.9 collective-permute-start.4
  47.1 0.9 copy-start.16
  48.9 23.8 %collective-permute-start.8 = (f32[128,1024]{1,0:T(8,128)}, f32[128,1024]{1,0:T(8,128)S(1)}, u32[]{:S(2)}, u32[]{:S(2)}) collective-permute-start(f32[128,1024]{1,0:T(8,128)} %get-tuple-element.83), channel_id=1, source_target_pairs={{0,8},{4,12},{8,0},{12,4},{16,24},{20,28},{24,16},{28,20},{1,9},{5... | collective-permute-start | bytes 1572872 | tf_op jit(solution)/shard_map/ppermute | solution.py:416
  55.7 5.2 %copy-start.22 = (s32[2,4]{1,0:T(2,128)S(1)}, s32[2,4]{1,0:T(2,128)}, u32[]{:S(2)}) copy-start(s32[2,4]{1,0:T(2,128)} %constant.104.clone) | copy-start | bytes 100
  55.7 17.0 %collective-permute-start.7 = (f32[128,512]{1,0:T(8,128)}, f32[128,512]{1,0:T(8,128)}, u32[]{:S(2)}, u32[]{:S(2)}) collective-permute-start(f32[128,512]{1,0:T(8,128)} %get-tuple-element.82), channel_id=1, source_target_pairs={{0,4},{4,0},{8,12},{12,8},{16,20},{20,16},{24,28},{28,24},{1,5},{5... | collective-permute-start | bytes 786440 | tf_op jit(solution)/shard_map/ppermute | solution.py:235
  60.5 12.2 %collective-permute-start.6 = (f32[128,512]{1,0:T(8,128)}, f32[128,512]{1,0:T(8,128)S(1)}, u32[]{:S(2)}, u32[]{:S(2)}) collective-permute-start(f32[128,512]{1,0:T(8,128)} %get-tuple-element.80), channel_id=1, source_target_pairs={{0,4},{4,0},{8,12},{12,8},{16,20},{20,16},{24,28},{28,24},{1,5},{5... | collective-permute-start | bytes 786440 | tf_op jit(solution)/shard_map/ppermute | solution.py:235
  62.3 44.5 %collective-permute-start.9 = (f32[2048,128]{1,0:T(8,128)}, f32[2048,128]{1,0:T(8,128)}, u32[]{:S(2)}, u32[]{:S(2)}) collective-permute-start(f32[2048,128]{1,0:T(8,128)} %collective-permute-done.2.refs_3_.refs_4_.refs_2_), channel_id=1, source_target_pairs={{0,1},{1,0},{2,3},{3,2},{4,5},{5,4},{6,7},{7,6},{8,9},{9,8},{10,11... | collective-permute-start | bytes 3145736 | tf_op jit(solution)/shard_map/ppermute | solution.py:265
  63.8 42.9 %collective-permute-start.10 = (f32[2048,128]{1,0:T(8,128)}, f32[2048,128]{1,0:T(8,128)}, u32[]{:S(2)}, u32[]{:S(2)}) collective-permute-start(f32[2048,128]{1,0:T(8,128)} %collective-permute-done.1.refs_3_.refs_1_.refs_2_), channel_id=1, source_target_pairs={{0,2},{1,3},{2,0},{3,1},{4,6},{5,7},{6,4},{7,5},{8,10},{9,11},{10,... | collective-permute-start | bytes 3145736 | tf_op jit(solution)/shard_map/ppermute | solution.py:265
  69.0 3.7 %copy-start.14 = (f32[128,512]{1,0:T(8,128)S(1)}, f32[128,512]{1,0:T(8,128)}, u32[]{:S(2)}) copy-start(f32[128,512]{1,0:T(8,128)} %copy-done.13) | copy-start | bytes 786436
  76.8 9.2 %collective-permute-start.13 = (f32[128,256]{1,0:T(8,128)S(1)}, f32[128,256]{1,0:T(8,128)S(1)}, u32[]{:S(2)}, u32[]{:S(2)}) collective-permute-start(f32[128,256]{1,0:T(8,128)S(1)} %get-tuple-element.91), channel_id=1, source_target_pairs={{0,4},{4,0},{8,12},{12,8},{16,20},{20,16},{24,28},{28,24},{1,5},{5... | collective-permute-start | bytes 393224 | tf_op jit(solution)/shard_map/ppermute | solution.py:235
  85.1 4.9 %collective-permute-start.12 = (f32[128,512]{1,0:T(8,128)S(1)}, f32[128,512]{1,0:T(8,128)S(1)}, u32[]{:S(2)}, u32[]{:S(2)}) collective-permute-start(f32[128,512]{1,0:T(8,128)S(1)} %get-tuple-element.89), channel_id=1, source_target_pairs={{0,4},{4,0},{8,12},{12,8},{16,20},{20,16},{24,28},{28,24},{1,5},{5... | collective-permute-start | bytes 786440 | tf_op jit(solution)/shard_map/ppermute | solution.py:235
  85.6 13.9 %collective-permute-start.14 = (f32[128,1024]{1,0:T(8,128)S(1)}, f32[128,1024]{1,0:T(8,128)S(1)}, u32[]{:S(2)}, u32[]{:S(2)}) collective-permute-start(f32[128,1024]{1,0:T(8,128)S(1)} %get-tuple-element.92), channel_id=1, source_target_pairs={{0,8},{4,12},{8,0},{12,4},{16,24},{20,28},{24,16},{28,20},{1,9},{5... | collective-permute-start | bytes 1572872 | tf_op jit(solution)/shard_map/ppermute | solution.py:416
  86.1 13.5 %collective-permute-start.15 = (f32[128,1024]{1,0:T(8,128)S(1)}, f32[128,1024]{1,0:T(8,128)S(1)}, u32[]{:S(2)}, u32[]{:S(2)}) collective-permute-start(f32[128,1024]{1,0:T(8,128)S(1)} %get-tuple-element.93.refs_8_), channel_id=1, source_target_pairs={{8,16},{12,20},{16,8},{20,12},{9,17},{13,21},{17,9},{21,13},{10,18... | collective-permute-start | bytes 1572872 | tf_op jit(solution)/shard_map/ppermute | solution.py:421
  90.0 16.7 %copy-start.24 = (s32[4,2]{1,0:T(4,128)S(1)}, s32[4,2]{1,0:T(4,128)}, u32[]{:S(2)}) copy-start(s32[4,2]{1,0:T(4,128)} %constant.101.clone) | copy-start | bytes 100
  90.0 1.6 collective-permute-start.11
  100.8 0.8 copy-start.5
  101.5 18.4 %collective-permute-start.18 = (f32[128,1280]{1,0:T(8,128)}, f32[128,1280]{1,0:T(8,128)S(1)}, u32[]{:S(2)}, u32[]{:S(2)}) collective-permute-start(f32[128,1280]{1,0:T(8,128)} %get-tuple-element.100), channel_id=1, source_target_pairs={{0,8},{4,12},{8,0},{12,4},{16,24},{20,28},{24,16},{28,20},{1,9},{5... | collective-permute-start | bytes 1966088 | tf_op jit(solution)/shard_map/ppermute | solution.py:416
  105.2 14.8 %collective-permute-start.19 = (f32[128,1024]{1,0:T(8,128)}, f32[128,1024]{1,0:T(8,128)}, u32[]{:S(2)}, u32[]{:S(2)}) collective-permute-start(f32[128,1024]{1,0:T(8,128)} %get-tuple-element.101.refs_6_), channel_id=1, source_target_pairs={{8,16},{12,20},{16,8},{20,12},{9,17},{13,21},{17,9},{21,13},{10,18... | collective-permute-start | bytes 1572872 | tf_op jit(solution)/shard_map/ppermute | solution.py:421
  114.9 6.0 %copy-start.6 = (f32[128,1024]{1,0:T(8,128)S(1)}, f32[128,1024]{1,0:T(8,128)}, u32[]{:S(2)}) copy-start(f32[128,1024]{1,0:T(8,128)} %copy-done.5) | copy-start | bytes 1572868
  114.9 3.9 %collective-permute-start.17 = (f32[128,512]{1,0:T(8,128)S(1)}, f32[128,512]{1,0:T(8,128)S(1)}, u32[]{:S(2)}, u32[]{:S(2)}) collective-permute-start(f32[128,512]{1,0:T(8,128)S(1)} %get-tuple-element.99), channel_id=1, source_target_pairs={{0,4},{4,0},{8,12},{12,8},{16,20},{20,16},{24,28},{28,24},{1,5},{5... | collective-permute-start | bytes 786440 | tf_op jit(solution)/shard_map/ppermute | solution.py:235
  118.3 1.7 collective-permute-start.16
  120.0 0.9 copy-start.1
  120.9 1.1 copy-start.2
  123.4 16.8 %collective-permute-start.23 = (f32[128,1280]{1,0:T(8,128)S(1)}, f32[128,1280]{1,0:T(8,128)S(1)}, u32[]{:S(2)}, u32[]{:S(2)}) collective-permute-start(f32[128,1280]{1,0:T(8,128)S(1)} %get-tuple-element.109.refs_6_), channel_id=1, source_target_pairs={{8,16},{12,20},{16,8},{20,12},{9,17},{13,21},{17,9},{21,13},{10,18... | collective-permute-start | bytes 1966088 | tf_op jit(solution)/shard_map/ppermute | solution.py:421
  124.2 16.1 %collective-permute-start.22 = (f32[128,1024]{1,0:T(8,128)S(1)}, f32[128,1024]{1,0:T(8,128)S(1)}, u32[]{:S(2)}, u32[]{:S(2)}) collective-permute-start(f32[128,1024]{1,0:T(8,128)S(1)} %get-tuple-element.108), channel_id=1, source_target_pairs={{0,8},{4,12},{8,0},{12,4},{16,24},{20,28},{24,16},{28,20},{1,9},{5... | collective-permute-start | bytes 1572872 | tf_op jit(solution)/shard_map/ppermute | solution.py:416
  128.1 12.2 %collective-permute-start.24 = (f32[128,1024]{1,0:T(8,128)S(1)}, f32[128,1024]{1,0:T(8,128)S(1)}, u32[]{:S(2)}, u32[]{:S(2)}) collective-permute-start(f32[128,1024]{1,0:T(8,128)S(1)} %get-tuple-element.111.refs_0_), channel_id=1, source_target_pairs={{0,4},{4,0},{8,12},{12,8},{16,20},{20,16},{24,28},{28,24},{1,5},{5... | collective-permute-start | bytes 1572872 | tf_op jit(solution)/shard_map/ppermute | solution.py:235
  131.3 3.9 %collective-permute-start.21 = (f32[128,512]{1,0:T(8,128)S(1)}, f32[128,512]{1,0:T(8,128)S(1)}, u32[]{:S(2)}, u32[]{:S(2)}) collective-permute-start(f32[128,512]{1,0:T(8,128)S(1)} %get-tuple-element.107), channel_id=1, source_target_pairs={{0,4},{4,0},{8,12},{12,8},{16,20},{20,16},{24,28},{28,24},{1,5},{5... | collective-permute-start | bytes 786440 | tf_op jit(solution)/shard_map/ppermute | solution.py:235
  135.1 1.6 collective-permute-start.20
  140.6 8.3 %copy-start.3 = (f32[128,1024]{1,0:T(8,128)}, f32[128,1024]{1,0:T(8,128)S(1)}, u32[]{:S(2)}) copy-start(f32[128,1024]{1,0:T(8,128)S(1)} %get-tuple-element.112.refs_0_) | copy-start | bytes 1572868
  140.6 18.8 %collective-permute-start.28 = (f32[128,1280]{1,0:T(8,128)S(1)}, f32[128,1280]{1,0:T(8,128)S(1)}, u32[]{:S(2)}, u32[]{:S(2)}) collective-permute-start(f32[128,1280]{1,0:T(8,128)S(1)} %get-tuple-element.118), channel_id=1, source_target_pairs={{0,8},{4,12},{8,0},{12,4},{16,24},{20,28},{24,16},{28,20},{1,9},{5... | collective-permute-start | bytes 1966088 | tf_op jit(solution)/shard_map/ppermute | solution.py:416
  144.9 9.4 %collective-permute-start.25 = (f32[128,1024]{1,0:T(8,128)S(1)}, f32[128,1024]{1,0:T(8,128)S(1)}, u32[]{:S(2)}, u32[]{:S(2)}) collective-permute-start(f32[128,1024]{1,0:T(8,128)S(1)} %get-tuple-element.112.refs_0_), channel_id=1, source_target_pairs={{0,4},{4,0},{8,12},{12,8},{16,20},{20,16},{24,28},{28,24},{1,5},{5... | collective-permute-start | bytes 1572872 | tf_op jit(solution)/shard_map/ppermute | solution.py:235
  144.9 9.4 %collective-permute-start.29 = (f32[128,1024]{1,0:T(8,128)S(1)}, f32[128,1024]{1,0:T(8,128)S(1)}, u32[]{:S(2)}, u32[]{:S(2)}) collective-permute-start(f32[128,1024]{1,0:T(8,128)S(1)} %get-tuple-element.119.refs_6_), channel_id=1, source_target_pairs={{8,16},{12,20},{16,8},{20,12},{9,17},{13,21},{17,9},{21,13},{10,18... | collective-permute-start | bytes 1572872 | tf_op jit(solution)/shard_map/ppermute | solution.py:421
  148.9 3.9 %collective-permute-start.27 = (f32[128,512]{1,0:T(8,128)S(1)}, f32[128,512]{1,0:T(8,128)S(1)}, u32[]{:S(2)}, u32[]{:S(2)}) collective-permute-start(f32[128,512]{1,0:T(8,128)S(1)} %get-tuple-element.117), channel_id=1, source_target_pairs={{0,4},{4,0},{8,12},{12,8},{16,20},{20,16},{24,28},{28,24},{1,5},{5... | collective-permute-start | bytes 786440 | tf_op jit(solution)/shard_map/ppermute | solution.py:235
  152.7 1.6 collective-permute-start.26
  159.4 3.6 %copy-start.21 = (s32[4,6]{1,0:T(4,128)S(1)}, s32[4,6]{1,0:T(4,128)}, u32[]{:S(2)}) copy-start(s32[4,6]{1,0:T(4,128)} %constant.103.clone) | copy-start | bytes 292
  159.7 0.9 copy-start.7
  161.3 0.8 copy-start.11
  162.1 0.8 copy-start.17
  162.9 4.3 %collective-permute-start.32 = (f32[128,1280]{1,0:T(8,128)S(1)}, f32[128,1280]{1,0:T(8,128)S(1)}, u32[]{:S(2)}, u32[]{:S(2)}) collective-permute-start(f32[128,1280]{1,0:T(8,128)S(1)} %get-tuple-element.125.refs_2_), channel_id=1, source_target_pairs={{0,4},{4,0},{8,12},{12,8},{16,20},{20,16},{24,28},{28,24},{1,5},{5... | collective-permute-start | bytes 1966088 | tf_op jit(solution)/shard_map/ppermute | solution.py:235
  163.9 14.8 %collective-permute-start.30 = (f32[128,1024]{1,0:T(8,128)}, f32[128,1024]{1,0:T(8,128)}, u32[]{:S(2)}, u32[]{:S(2)}) collective-permute-start(f32[128,1024]{1,0:T(8,128)} %copy-done.17), channel_id=1, source_target_pairs={{0,8},{4,12},{8,0},{12,4},{16,24},{20,28},{24,16},{28,20},{1,9},{5... | collective-permute-start | bytes 1572872 | tf_op jit(solution)/shard_map/ppermute | solution.py:416
  165.8 12.9 %collective-permute-start.31 = (f32[128,1024]{1,0:T(8,128)}, f32[128,1024]{1,0:T(8,128)}, u32[]{:S(2)}, u32[]{:S(2)}) collective-permute-start(f32[128,1024]{1,0:T(8,128)} %copy-done.9), channel_id=1, source_target_pairs={{8,16},{12,20},{16,8},{20,12},{9,17},{13,21},{17,9},{21,13},{10,18... | collective-permute-start | bytes 1572872 | tf_op jit(solution)/shard_map/ppermute | solution.py:421
  167.3 20.6 %collective-permute-start.38 = (f32[256,256]{1,0:T(8,128)S(1)}, f32[256,256]{1,0:T(8,128)S(1)}, u32[]{:S(2)}, u32[]{:S(2)}) collective-permute-start(f32[256,256]{1,0:T(8,128)S(1)} %maximum_select_fusion), channel_id=1, source_target_pairs={{0,3},{1,2},{2,1},{3,0},{4,7},{5,6},{6,5},{7,4},{8,11},{9,10},{10,... | collective-permute-start | bytes 786440 | tf_op jit(solution)/shard_map/ppermute | solution.py:432
  169.6 19.1 %collective-permute-start.37 = (f32[256,256]{1,0:T(8,128)S(1)}, f32[256,256]{1,0:T(8,128)}, u32[]{:S(2)}, u32[]{:S(2)}) collective-permute-start(f32[256,256]{1,0:T(8,128)S(1)} %maximum_select_fusion), channel_id=1, source_target_pairs={{0,2},{1,3},{2,0},{3,1},{4,6},{5,7},{6,4},{7,5},{8,10},{9,11},{10,... | collective-permute-start | bytes 786440 | tf_op jit(solution)/shard_map/ppermute | solution.py:432
  170.1 18.7 %collective-permute-start.36 = (f32[256,256]{1,0:T(8,128)S(1)}, f32[256,256]{1,0:T(8,128)}, u32[]{:S(2)}, u32[]{:S(2)}) collective-permute-start(f32[256,256]{1,0:T(8,128)S(1)} %maximum_select_fusion), channel_id=1, source_target_pairs={{0,1},{1,0},{2,3},{3,2},{4,5},{5,4},{6,7},{7,6},{8,9},{9,8},{10,11... | collective-permute-start | bytes 786440 | tf_op jit(solution)/shard_map/ppermute | solution.py:432
  178.7 1.0 copy-start.8
  179.7 1.0 copy-start.10
  180.8 1.0 copy-start.12
  183.2 6.7 %copy-start = (f32[3,256,256]{2,1,0:T(8,128)S(1)}, f32[3,256,256]{2,1,0:T(8,128)}, u32[]{:S(2)}) copy-start(f32[3,256,256]{2,1,0:T(8,128)} %refs_6_.5) | copy-start | bytes 2359300
  183.3 18.7 %collective-permute-start.33 = (f32[128,1024]{1,0:T(8,128)S(1)}, f32[128,1024]{1,0:T(8,128)S(1)}, u32[]{:S(2)}, u32[]{:S(2)}) collective-permute-start(f32[128,1024]{1,0:T(8,128)S(1)} %get-tuple-element.126), channel_id=1, source_target_pairs={{0,8},{4,12},{8,0},{12,4},{16,24},{20,28},{24,16},{28,20},{1,9},{5... | collective-permute-start | bytes 1572872 | tf_op jit(solution)/shard_map/ppermute | solution.py:416
  187.0 15.0 %collective-permute-start.34 = (f32[128,1024]{1,0:T(8,128)S(1)}, f32[128,1024]{1,0:T(8,128)S(1)}, u32[]{:S(2)}, u32[]{:S(2)}) collective-permute-start(f32[128,1024]{1,0:T(8,128)S(1)} %get-tuple-element.127.refs_1_), channel_id=1, source_target_pairs={{8,16},{12,20},{16,8},{20,12},{9,17},{13,21},{17,9},{21,13},{10,18... | collective-permute-start | bytes 1572872 | tf_op jit(solution)/shard_map/ppermute | solution.py:421
  187.9 2.0 collective-permute-start.35
  202.1 14.5 %collective-permute-start.40 = (f32[128,1024]{1,0:T(8,128)S(1)}, f32[128,1024]{1,0:T(8,128)S(1)}, u32[]{:S(2)}, u32[]{:S(2)}) collective-permute-start(f32[128,1024]{1,0:T(8,128)S(1)} %get-tuple-element.135), channel_id=1, source_target_pairs={{0,8},{4,12},{8,0},{12,4},{16,24},{20,28},{24,16},{28,20},{1,9},{5... | collective-permute-start | bytes 1572872 | tf_op jit(solution)/shard_map/ppermute | solution.py:416
  204.0 12.7 %collective-permute-start.39 = (f32[128,1024]{1,0:T(8,128)S(1)}, f32[128,1024]{1,0:T(8,128)S(1)}, u32[]{:S(2)}, u32[]{:S(2)}) collective-permute-start(f32[128,1024]{1,0:T(8,128)S(1)} %get-tuple-element.134.refs_2_), channel_id=1, source_target_pairs={{0,4},{4,0},{8,12},{12,8},{16,20},{20,16},{24,28},{28,24},{1,5},{5... | collective-permute-start | bytes 1572872 | tf_op jit(solution)/shard_map/ppermute | solution.py:235
  204.2 14.4 %copy-start.4 = (f32[128,1024]{1,0:T(8,128)S(1)}, f32[128,1024]{1,0:T(8,128)}, u32[]{:S(2)}) copy-start(f32[128,1024]{1,0:T(8,128)} %copy-done.3) | copy-start | bytes 1572868
  216.6 2.0 collective-permute-start.41
  (3 other events, 2.2 us)

commit v4 on v3

--- a/solution.py
+++ b/solution.py
@@ -361,7 +361,7 @@
     x_both = split_array(eigvec, PIECE)
     chunks = [(0, 0), (0, 1), (1, 0), (2, 0), (1, 1), (2, 1)]
     count = len(chunks)
-    gram_chunk = 2
+    gram_chunk = 3
     prepared, arrived, sizes, gram_sides = {}, {}, {}, []
 
     def start(number, after):

time: 239 us -> 243 us (1.017)
  waiting for transfers between devices: 36.5 us -> 43.5 us
  starting transfers between devices: 42.1 us -> 38.6 us
  Pallas kernels: 131 us -> 134 us
    ppermute x8, waiting for transfers between devices: 18 us -> 21.8 us  [shards_square(): outer[step] = lax.ppermute(results['out'], 'row', outer_pairs)]
    ppermute x8, starting transfers between devices: 21.5 us -> 17.9 us  [shards_square(): outer[step] = lax.ppermute(results['out'], 'row', outer_pairs)]
    unnamed x50 -> x74, local copies, waits for them, and re-layouts: 11.6 us -> 10.4 us
  transfers between devices with their start and end apart: 42 -> 42, of which waited for: 13 -> 15; matrix products, arithmetic and copies ran while one was open for 3% -> 2% of each run, Pallas kernels for 46% -> 47%
where the time goes in v4:
time: 243 us; the launch traced here: 241 us
  Pallas kernels  134 us (55%)
  waiting for transfers between devices  43.5 us (18%)
  starting transfers between devices  38.6 us (16%)
  local copies, waits for them, and re-layouts  16.1 us (7%)
  between operations  7.83 us (3%)
    pallas_call x13, Pallas kernels, products(): pl.pallas_call(functools.partial(products_kernel, block), in_specs=[in_vm...  45.1 us
    pallas_call x3, Pallas kernels, update(): pl.pallas_call(functools.partial(update_kernel, offset), grid_spec=pltpu....  42.5 us
    pallas_call x5, Pallas kernels, choose(): pl.pallas_call(functools.partial(choose_kernel, outputs, len(cases)), in_...  22.9 us
    ppermute x8, waiting for transfers between devices, shards_square(): outer[step] = lax.ppermute(results['out'], 'row', outer_pairs)  21.8 us
    ppermute x8, starting transfers between devices, shards_square(): outer[step] = lax.ppermute(results['out'], 'row', outer_pairs)  17.9 us
    pallas_call x1, Pallas kernels, split_array(): pl.pallas_call(split_kernel, grid=(rows // step,), in_specs=[pl.BlockSpec...  14.6 us
    unnamed x74, local copies, waits for them, and re-layouts  10.4 us
    ppermute x19, waiting for transfers between devices, swap_cores(): return lax.ppermute(value, 'row', pairs_of(lax.axis_size('row'), 1))  9.97 us
  transfers between devices with their start and end apart: 42, of which 15 were waited for; matrix products, arithmetic and copies ran while one was open for 2% of the time, Pallas kernels for 47%

profile of v4, /device:TPU:0, one launch (start us, length us, event | category | flops | bytes accessed | tf_op | source)
XLA Modules:
  0.0 241.3 jit_solution(7854566486685243739)
XLA Ops:
  0.0 3.0 %fusion.14 = (f32[2048,128]{1,0:T(8,128)}, f32[2048,128]{1,0:T(8,128)}) fusion(f32[2048,256]{1,0:T(8,128)} %bitcast.37), kind=kLoop, calls=%fused_computation.37 | loop fusion | bytes 4194304 | tf_op jit(solution)/shard_map/slice | solution.py:266
  3.1 3.0 %collective-permute-start.2 = (f32[2048,128]{1,0:T(8,128)}, f32[2048,128]{1,0:T(8,128)}, u32[]{:S(2)}, u32[]{:S(2)}) collective-permute-start(f32[2048,128]{1,0:T(8,128)} %get-tuple-element.142.refs_0_), channel_id=1, source_target_pairs={{0,2},{1,3},{2,0},{3,1},{4,6},{5,7},{6,4},{7,5},{8,10},{9,11},{10,... | collective-permute-start | bytes 3145736 | tf_op jit(solution)/shard_map/ppermute | solution.py:265
  6.0 1.5 collective-permute-start
  8.2 14.6 %split_x.1.both_ref = bf16[4,2,2048,512]{3,2,1,0:T(8,128)(2,1)} custom-call(f32[2048,2048]{1,0:T(8,128)} %refs_11_.5), custom_call_target="tpu_custom_call" | custom-call | flops 262144 | bytes 524288 | tf_op jit(solution)/shard_map/split_x/pallas_call | solution.py:60
  22.9 7.4 %collective-permute-done.2.refs_3_.refs_2_.refs_4_ = f32[2048,128]{1,0:T(8,128)} collective-permute-done((f32[2048,128]{1,0:T(8,128)}, f32[2048,128]{1,0:T(8,128)}, u32[]{:S(2)}, u32[]{:S(2)}) %collective-permute-start.2) | collective-permute-done | bytes 1048608 | tf_op jit(solution)/shard_map/ppermute | solution.py:265
  30.3 2.1 collective-permute-done.refs_2_.refs_0_
  32.4 4.9 %choose_panel.5 = (bf16[1,2,2048,256]{3,2,1,0:T(8,128)(2,1)}, bf16[512,2048]{1,0:T(8,128)(2,1)S(1)}) custom-call(s32[2]{0:T(128)S(1)} %broadcast_select_fusion.2.which_ref, f32[2048,128]{1,0:T(8,128)} %get-tuple-element.142.refs_0_, f32[2048,128]{1,0:T(8,128)} %get-tuple-element.141.refs_1_, f32[2048,128]{1,0:T(8,128)} %collective-permute-done.refs_2_.refs_0_, ...), custom_call_target="tpu_custom_call" | custom-call | flops 32768 | bytes 98304 | tf_op jit(solution)/shard_map/choose_panel/pallas_call | solution.py:106
  37.3 3.2 %products.14 = (f32[128,512]{1,0:T(8,128)S(1)}, f32[128,512]{1,0:T(8,128)S(1)}) custom-call(bf16[512,2048]{1,0:T(8,128)(2,1)S(1)} %get-tuple-element.73.flipped_ref, bf16[4,2,2048,512]{3,2,1,0:T(8,128)(2,1)} %split_x.1.both_ref), custom_call_target="tpu_custom_call" | custom-call | flops 25165824 | bytes 98304 | tf_op jit(solution)/shard_map/products/pallas_call | solution.py:150
  40.6 3.9 %products.13 = (f32[128,512]{1,0:T(8,128)S(1)}, f32[128,512]{1,0:T(8,128)}) custom-call(bf16[512,2048]{1,0:T(8,128)(2,1)S(1)} %get-tuple-element.73.flipped_ref, bf16[4,2,2048,512]{3,2,1,0:T(8,128)(2,1)} %split_x.1.both_ref), custom_call_target="tpu_custom_call" | custom-call | flops 25165824 | bytes 98304 | tf_op jit(solution)/shard_map/products/pallas_call | solution.py:150
  45.0 1.4 collective-permute-done.4.refs_1_
  47.1 0.9 copy-done.24
  48.1 0.9 exchange.9
  48.9 1.6 collective-permute-start.8
  50.5 3.9 %products.16 = (f32[128,512]{1,0:T(8,128)S(1)}, f32[128,512]{1,0:T(8,128)}) custom-call(bf16[512,2048]{1,0:T(8,128)(2,1)S(1)} %get-tuple-element.73.flipped_ref, bf16[4,2,2048,512]{3,2,1,0:T(8,128)(2,1)} %split_x.1.both_ref, f32[128,1024]{1,0:T(8,128)S(1)} %get-tuple-element.78.refs_0_.refs_5_), custom_call_target="tpu_custom_call" | custom-call | flops 25165824 | bytes 98304 | tf_op jit(solution)/shard_map/products/pallas_call | solution.py:150
  54.6 3.9 %products.15 = (f32[128,512]{1,0:T(8,128)S(1)}, f32[128,512]{1,0:T(8,128)}) custom-call(bf16[512,2048]{1,0:T(8,128)(2,1)S(1)} %get-tuple-element.73.flipped_ref, bf16[4,2,2048,512]{3,2,1,0:T(8,128)(2,1)} %split_x.1.both_ref, f32[128,1024]{1,0:T(8,128)S(1)} %get-tuple-element.78.refs_0_.refs_5_), custom_call_target="tpu_custom_call" | custom-call | flops 25165824 | bytes 98304 | tf_op jit(solution)/shard_map/products/pallas_call | solution.py:150
  59.7 1.5 collective-permute-start.9
  61.7 1.6 collective-permute-done.8.refs_4_
  63.3 0.8 copy-done.13
  64.1 1.0 copy-done.14
  65.2 0.9 copy-done.22
  66.1 1.9 exchange.10
  68.0 4.9 %choose_panel.6 = (bf16[1,2,2048,256]{3,2,1,0:T(8,128)(2,1)}, bf16[512,2048]{1,0:T(8,128)(2,1)S(1)}) custom-call(s32[2]{0:T(128)S(1)} %broadcast_select_fusion.3.which_ref, f32[2048,128]{1,0:T(8,128)} %collective-permute-done.refs_2_.refs_0_, f32[2048,128]{1,0:T(8,128)} %collective-permute-done.1.refs_1_.refs_3_.refs_2_, ...), custom_call_target="tpu_custom_call" | custom-call | flops 32768 | bytes 98304 | tf_op jit(solution)/shard_map/choose_panel/pallas_call | solution.py:106
  72.9 3.9 %products.18 = (f32[128,512]{1,0:T(8,128)S(1)}, f32[128,512]{1,0:T(8,128)}) custom-call(bf16[512,2048]{1,0:T(8,128)(2,1)S(1)} %get-tuple-element.85.flipped_ref, bf16[4,2,2048,512]{3,2,1,0:T(8,128)(2,1)} %split_x.1.both_ref, f32[128,1024]{1,0:T(8,128)S(1)} %get-tuple-element.84.refs_4_.refs_0_.refs_6_.refs_5_), custom_call_target="tpu_custom_call" | custom-call | flops 25165824 | bytes 98304 | tf_op jit(solution)/shard_map/products/pallas_call | solution.py:150
  76.9 1.6 collective-permute-start.13
  78.6 1.4 collective-permute-start.14
  81.4 3.9 %products.17 = (f32[128,512]{1,0:T(8,128)S(1)}, f32[128,512]{1,0:T(8,128)}) custom-call(bf16[512,2048]{1,0:T(8,128)(2,1)S(1)} %get-tuple-element.85.flipped_ref, bf16[4,2,2048,512]{3,2,1,0:T(8,128)(2,1)} %split_x.1.both_ref, f32[128,1024]{1,0:T(8,128)S(1)} %get-tuple-element.84.refs_4_.refs_0_.refs_6_.refs_5_), custom_call_target="tpu_custom_call" | custom-call | flops 25165824 | bytes 98304 | tf_op jit(solution)/shard_map/products/pallas_call | solution.py:150
  87.5 4.6 %choose_panel.8.refs_9_.both_ref = bf16[1,2,2048,256]{3,2,1,0:T(8,128)(2,1)} custom-call(s32[2]{0:T(128)S(1)} %iota_add_fusion.which_ref, f32[2048,128]{1,0:T(8,128)} %get-tuple-element.142.refs_0_, f32[2048,128]{1,0:T(8,128)} %get-tuple-element.141.refs_1_, f32[2048,128]{1,0:T(8,128)} %collective-permute-done.refs_2_.refs_0_, ...), custom_call_target="tpu_custom_call" | custom-call | flops 32768 | bytes 98304 | tf_op jit(solution)/shard_map/choose_panel/pallas_call | solution.py:106
  92.2 3.7 %choose_panel.7.refs_8_.flipped_ref = bf16[512,2048]{1,0:T(8,128)(2,1)S(1)} custom-call(s32[2]{0:T(128)S(1)} %broadcast_select_fusion.which_ref, f32[2048,128]{1,0:T(8,128)} %get-tuple-element.142.refs_0_, f32[2048,128]{1,0:T(8,128)} %get-tuple-element.141.refs_1_, f32[2048,128]{1,0:T(8,128)} %collective-permute-done.refs_2_.refs_0_, ...), custom_call_target="tpu_custom_call" | custom-call | flops 32768 | bytes 98304 | tf_op jit(solution)/shard_map/choose_panel/pallas_call | solution.py:106
  95.9 3.2 %exchange.11 = (f32[128,1024]{1,0:T(8,128)S(1)}, f32[128,1024]{1,0:T(8,128)}, f32[128,1024]{1,0:T(8,128)S(1)}, f32[128,1024]{1,0:T(8,128)}) custom-call(s32[1]{0:T(128)} %bitcast.3.ends_ref, f32[128,512]{1,0:T(8,128)S(1)} %copy-done.26, f32[128,512]{1,0:T(8,128)} %collective-permute-done.11.refs_1_, f32[128,512]{1,0:T(8,128)S(1)} %get-tuple-element.88.refs_2_, ...), custom_call_target="tpu_custom_call" | custom-call | tf_op jit(solution)/shard_map/exchange/pallas_call | solution.py:340
  99.9 3.5 %collective-permute-start.18 = (f32[128,1024]{1,0:T(8,128)}, f32[128,1024]{1,0:T(8,128)}, u32[]{:S(2)}, u32[]{:S(2)}) collective-permute-start(f32[128,1024]{1,0:T(8,128)} %get-tuple-element.100), channel_id=1, source_target_pairs={{0,8},{4,12},{8,0},{12,4},{16,24},{20,28},{24,16},{28,20},{1,9},{5... | collective-permute-start | bytes 1572872 | tf_op jit(solution)/shard_map/ppermute | solution.py:416
  103.4 1.4 collective-permute-start.19
  104.9 4.9 %choose_panel.9 = (bf16[1,2,2048,256]{3,2,1,0:T(8,128)(2,1)}, bf16[512,2048]{1,0:T(8,128)(2,1)S(1)}) custom-call(s32[2]{0:T(128)S(1)} %broadcast_select_fusion.1.which_ref, f32[2048,128]{1,0:T(8,128)} %collective-permute-done.9.refs_0_, f32[2048,128]{1,0:T(8,128)} %collective-permute-done.10.refs_1_, ...), custom_call_target="tpu_custom_call" | custom-call | flops 32768 | bytes 98304 | tf_op jit(solution)/shard_map/choose_panel/pallas_call | solution.py:106
  109.8 3.2 %products.20 = (f32[128,512]{1,0:T(8,128)S(1)}, f32[128,512]{1,0:T(8,128)S(1)}) custom-call(bf16[512,2048]{1,0:T(8,128)(2,1)S(1)} %get-tuple-element.93.flipped_ref, bf16[4,2,2048,512]{3,2,1,0:T(8,128)(2,1)} %split_x.1.both_ref, f32[128,1024]{1,0:T(8,128)S(1)} %get-tuple-element.92.refs_4_.refs_0_.refs_7_), custom_call_target="tpu_custom_call" | custom-call | flops 25165824 | bytes 98304 | tf_op jit(solution)/shard_map/products/pallas_call | solution.py:150
  113.3 3.3 %products.19 = (f32[128,512]{1,0:T(8,128)S(1)}, f32[128,512]{1,0:T(8,128)S(1)}) custom-call(bf16[512,2048]{1,0:T(8,128)(2,1)S(1)} %get-tuple-element.93.flipped_ref, bf16[4,2,2048,512]{3,2,1,0:T(8,128)(2,1)} %split_x.1.both_ref, f32[128,1024]{1,0:T(8,128)S(1)} %get-tuple-element.92.refs_4_.refs_0_.refs_7_), custom_call_target="tpu_custom_call" | custom-call | flops 25165824 | bytes 98304 | tf_op jit(solution)/shard_map/products/pallas_call | solution.py:150
  117.1 3.0 %products.21 = (f32[128,256]{1,0:T(8,128)S(1)}, f32[128,256]{1,0:T(8,128)S(1)}) custom-call(bf16[512,2048]{1,0:T(8,128)(2,1)S(1)} %copy-done.1, bf16[1,2,2048,256]{3,2,1,0:T(8,128)(2,1)} %choose_panel.8.refs_9_.both_ref, f32[128,1024]{1,0:T(8,128)S(1)} %get-tuple-element.92.refs_4_.refs_0_.refs_7_), custom_call_target="tpu_custom_call" | custom-call | flops 12582912 | bytes 65536 | tf_op jit(solution)/shard_map/products/pallas_call | solution.py:150
  120.4 1.2 collective-permute-done.17.refs_5_
  121.6 1.7 exchange.12
  123.2 0.9 collective-permute-start.22
  125.0 3.2 %products.23 = (f32[128,512]{1,0:T(8,128)S(1)}, f32[128,512]{1,0:T(8,128)S(1)}) custom-call(bf16[512,2048]{1,0:T(8,128)(2,1)S(1)} %get-tuple-element.85.flipped_ref, bf16[4,2,2048,512]{3,2,1,0:T(8,128)(2,1)} %split_x.1.both_ref, f32[128,1280]{1,0:T(8,128)S(1)} %get-tuple-element.103.refs_0_.refs_5_), custom_call_target="tpu_custom_call" | custom-call | flops 25165824 | bytes 98304 | tf_op jit(solution)/shard_map/products/pallas_call | solution.py:150
  128.7 3.2 %products.22 = (f32[128,512]{1,0:T(8,128)S(1)}, f32[128,512]{1,0:T(8,128)S(1)}) custom-call(bf16[512,2048]{1,0:T(8,128)(2,1)S(1)} %get-tuple-element.85.flipped_ref, bf16[4,2,2048,512]{3,2,1,0:T(8,128)(2,1)} %split_x.1.both_ref, f32[128,1280]{1,0:T(8,128)S(1)} %get-tuple-element.103.refs_0_.refs_5_), custom_call_target="tpu_custom_call" | custom-call | flops 25165824 | bytes 98304 | tf_op jit(solution)/shard_map/products/pallas_call | solution.py:150
  132.1 1.5 collective-permute-done.20.refs_1_
  133.5 6.6 %collective-permute-done.22.refs_4_ = f32[128,1280]{1,0:T(8,128)S(1)} collective-permute-done((f32[128,1280]{1,0:T(8,128)S(1)}, f32[128,1280]{1,0:T(8,128)S(1)}, u32[]{:S(2)}, u32[]{:S(2)}) %collective-permute-start.22) | collective-permute-done | bytes 655392 | tf_op jit(solution)/shard_map/ppermute | solution.py:416
  141.1 4.0 %collective-permute-start.28 = (f32[128,1024]{1,0:T(8,128)S(1)}, f32[128,1024]{1,0:T(8,128)S(1)}, u32[]{:S(2)}, u32[]{:S(2)}) collective-permute-start(f32[128,1024]{1,0:T(8,128)S(1)} %get-tuple-element.118), channel_id=1, source_target_pairs={{0,8},{4,12},{8,0},{12,4},{16,24},{20,28},{24,16},{28,20},{1,9},{5... | collective-permute-start | bytes 1572872 | tf_op jit(solution)/shard_map/ppermute | solution.py:416
  145.1 3.2 %products.25 = (f32[128,512]{1,0:T(8,128)S(1)}, f32[128,512]{1,0:T(8,128)S(1)}) custom-call(bf16[512,2048]{1,0:T(8,128)(2,1)S(1)} %get-tuple-element.93.flipped_ref, bf16[4,2,2048,512]{3,2,1,0:T(8,128)(2,1)} %split_x.1.both_ref, f32[128,1024]{1,0:T(8,128)S(1)} %get-tuple-element.113.refs_0_.refs_5_), custom_call_target="tpu_custom_call" | custom-call | flops 25165824 | bytes 98304 | tf_op jit(solution)/shard_map/products/pallas_call | solution.py:150
  148.9 3.2 %products.24 = (f32[128,512]{1,0:T(8,128)S(1)}, f32[128,512]{1,0:T(8,128)S(1)}) custom-call(bf16[512,2048]{1,0:T(8,128)(2,1)S(1)} %get-tuple-element.93.flipped_ref, bf16[4,2,2048,512]{3,2,1,0:T(8,128)(2,1)} %split_x.1.both_ref, f32[128,1024]{1,0:T(8,128)S(1)} %get-tuple-element.113.refs_0_.refs_5_), custom_call_target="tpu_custom_call" | custom-call | flops 25165824 | bytes 98304 | tf_op jit(solution)/shard_map/products/pallas_call | solution.py:150
  152.2 1.5 collective-permute-done.26.refs_1_
  153.7 2.6 %collective-permute-done.28.refs_4_ = f32[128,1024]{1,0:T(8,128)S(1)} collective-permute-done((f32[128,1024]{1,0:T(8,128)S(1)}, f32[128,1024]{1,0:T(8,128)S(1)}, u32[]{:S(2)}, u32[]{:S(2)}) %collective-permute-start.28) | collective-permute-done | bytes 524320 | tf_op jit(solution)/shard_map/ppermute | solution.py:416
  157.1 2.8 %collective-permute-start.30 = (f32[128,1280]{1,0:T(8,128)S(1)}, f32[128,1280]{1,0:T(8,128)S(1)}, u32[]{:S(2)}, u32[]{:S(2)}) collective-permute-start(f32[128,1280]{1,0:T(8,128)S(1)} %get-tuple-element.121), channel_id=1, source_target_pairs={{0,8},{4,12},{8,0},{12,4},{16,24},{20,28},{24,16},{28,20},{1,9},{5... | collective-permute-start | bytes 1966088 | tf_op jit(solution)/shard_map/ppermute | solution.py:416
  161.5 1.1 collective-permute-done.32.refs_5_.refs_3_
  162.6 10.9 %collective-permute-done.30.refs_0_ = f32[128,1280]{1,0:T(8,128)S(1)} collective-permute-done((f32[128,1280]{1,0:T(8,128)S(1)}, f32[128,1280]{1,0:T(8,128)S(1)}, u32[]{:S(2)}, u32[]{:S(2)}) %collective-permute-start.30) | collective-permute-done | bytes 655392 | tf_op jit(solution)/shard_map/ppermute | solution.py:416
  173.6 0.8 copy-done.15
  175.2 0.8 copy-done.27
  176.3 1.8 collective-permute-done.35.refs_5_
  178.2 1.5 collective-permute-start.38
  179.7 1.5 collective-permute-start.37
  188.3 1.7 collective-permute-start.33
  190.1 0.9 collective-permute-start.34
  191.0 2.2 collective-permute-done.37
  193.2 1.2 select_bitcast_fusion.2
  194.5 12.0 %update.3 = (f32[2048,2048]{1,0:T(8,128)}, f32[8,128]{1,0:T(8,128)S(1)}) custom-call(s32[6]{0:T(128)S(1)} %broadcast_select_fusion.4.place_ref, f32[128,1024]{1,0:T(8,128)S(1)} %copy-done.4, f32[128,1024]{1,0:T(8,128)S(1)} %collective-permute-done.24.refs_9_.refs_1_, f32[128,1024]{1,0:T(8,128)S(1)} %copy-done.8, ...), custom_call_target="tpu_custom_call" | custom-call | flops 75497472 | bytes 229376 | tf_op jit(solution)/shard_map/update/pallas_call | solution.py:209
  206.7 1.8 collective-permute-start.40
  208.5 12.0 %update.4 = (f32[2048,2048]{1,0:T(8,128)}, f32[8,128]{1,0:T(8,128)S(1)}) custom-call(s32[6]{0:T(128)S(1)} %broadcast_select_fusion.4.place_ref, f32[128,1024]{1,0:T(8,128)S(1)} %copy-done.4, f32[128,1024]{1,0:T(8,128)S(1)} %collective-permute-done.24.refs_9_.refs_1_, f32[128,1024]{1,0:T(8,128)S(1)} %copy-done.8, ...), custom_call_target="tpu_custom_call", output_to_operand_aliasing={{0}: (13, {})} | custom-call | flops 75497472 | bytes 229376 | tf_op jit(solution)/shard_map/update/pallas_call | solution.py:209
  221.1 1.5 collective-permute-done.41.refs_5_
  222.7 18.6 %update.5 = (f32[2048,2048]{1,0:T(8,128)}, f32[8,128]{1,0:T(8,128)}) custom-call(s32[6]{0:T(128)S(1)} %broadcast_select_fusion.4.place_ref, f32[128,1024]{1,0:T(8,128)S(1)} %copy-done.10, f32[128,1024]{1,0:T(8,128)S(1)} %copy-done.6, f32[128,1024]{1,0:T(8,128)S(1)} %get-tuple-element.134.refs_2_, ...), custom_call_target="tpu_custom_call", output_to_operand_aliasing={{0}: (13, {})} | custom-call | flops 150994944 | bytes 360448 | tf_op jit(solution)/shard_map/update/pallas_call | solution.py:209
  (154 shorter events, 17.1 us)
Async XLA Ops:
  0.0 8.1 %copy-start.28 = (s32[3]{0:T(128)S(1)}, s32[3]{0:T(128)}, u32[]{:S(2)}) copy-start(s32[3]{0:T(128)} %param.14) | copy-start | bytes 40
  0.0 8.1 %copy-start.29 = (s32[4,2]{1,0:T(4,128)S(1)}, s32[4,2]{1,0:T(4,128)}, u32[]{:S(2)}) copy-start(s32[4,2]{1,0:T(4,128)} %constant.100.clone) | copy-start | bytes 100
  0.0 8.1 %copy-start.30 = (s32[4,2]{1,0:T(4,128)S(1)}, s32[4,2]{1,0:T(4,128)}, u32[]{:S(2)}) copy-start(s32[4,2]{1,0:T(4,128)} %constant.99.clone) | copy-start | bytes 100
  3.1 27.3 %collective-permute-start.2 = (f32[2048,128]{1,0:T(8,128)}, f32[2048,128]{1,0:T(8,128)}, u32[]{:S(2)}, u32[]{:S(2)}) collective-permute-start(f32[2048,128]{1,0:T(8,128)} %get-tuple-element.142.refs_0_), channel_id=1, source_target_pairs={{0,2},{1,3},{2,0},{3,1},{4,6},{5,7},{6,4},{7,5},{8,10},{9,11},{10,... | collective-permute-start | bytes 3145736 | tf_op jit(solution)/shard_map/ppermute | solution.py:265
  6.0 26.4 %collective-permute-start = (f32[2048,128]{1,0:T(8,128)}, f32[2048,128]{1,0:T(8,128)}, u32[]{:S(2)}, u32[]{:S(2)}) collective-permute-start(f32[2048,128]{1,0:T(8,128)} %get-tuple-element.142.refs_0_), channel_id=1, source_target_pairs={{0,1},{1,0},{2,3},{3,2},{4,5},{5,4},{6,7},{7,6},{8,9},{9,8},{10,11... | collective-permute-start | bytes 3145736 | tf_op jit(solution)/shard_map/ppermute | solution.py:265
  7.5 52.2 %collective-permute-start.1 = (f32[2048,128]{1,0:T(8,128)}, f32[2048,128]{1,0:T(8,128)}, u32[]{:S(2)}, u32[]{:S(2)}) collective-permute-start(f32[2048,128]{1,0:T(8,128)} %get-tuple-element.141.refs_1_), channel_id=1, source_target_pairs={{0,1},{1,0},{2,3},{3,2},{4,5},{5,4},{6,7},{7,6},{8,9},{9,8},{10,11... | collective-permute-start | bytes 3145736 | tf_op jit(solution)/shard_map/ppermute | solution.py:265
  8.0 60.0 %collective-permute-start.3 = (f32[2048,128]{1,0:T(8,128)}, f32[2048,128]{1,0:T(8,128)}, u32[]{:S(2)}, u32[]{:S(2)}) collective-permute-start(f32[2048,128]{1,0:T(8,128)} %get-tuple-element.141.refs_1_), channel_id=1, source_target_pairs={{0,2},{1,3},{2,0},{3,1},{4,6},{5,7},{6,4},{7,5},{8,10},{9,11},{10,... | collective-permute-start | bytes 3145736 | tf_op jit(solution)/shard_map/ppermute | solution.py:265
  40.5 4.6 %collective-permute-start.5 = (f32[128,512]{1,0:T(8,128)S(1)}, f32[128,512]{1,0:T(8,128)S(1)}, u32[]{:S(2)}, u32[]{:S(2)}) collective-permute-start(f32[128,512]{1,0:T(8,128)S(1)} %get-tuple-element.77), channel_id=1, source_target_pairs={{0,4},{4,0},{8,12},{12,8},{16,20},{20,16},{24,28},{28,24},{1,5},{5... | collective-permute-start | bytes 786440 | tf_op jit(solution)/shard_map/ppermute | solution.py:235
  44.5 1.9 collective-permute-start.4
  48.9 14.4 %collective-permute-start.8 = (f32[128,1024]{1,0:T(8,128)}, f32[128,1024]{1,0:T(8,128)S(1)}, u32[]{:S(2)}, u32[]{:S(2)}) collective-permute-start(f32[128,1024]{1,0:T(8,128)} %get-tuple-element.83), channel_id=1, source_target_pairs={{0,8},{4,12},{8,0},{12,4},{16,24},{20,28},{24,16},{28,20},{1,9},{5... | collective-permute-start | bytes 1572872 | tf_op jit(solution)/shard_map/ppermute | solution.py:416
  54.4 6.8 %collective-permute-start.7 = (f32[128,512]{1,0:T(8,128)}, f32[128,512]{1,0:T(8,128)}, u32[]{:S(2)}, u32[]{:S(2)}) collective-permute-start(f32[128,512]{1,0:T(8,128)} %get-tuple-element.82), channel_id=1, source_target_pairs={{0,4},{4,0},{8,12},{12,8},{16,20},{20,16},{24,28},{28,24},{1,5},{5... | collective-permute-start | bytes 786440 | tf_op jit(solution)/shard_map/ppermute | solution.py:235
  59.2 2.5 %collective-permute-start.6 = (f32[128,512]{1,0:T(8,128)}, f32[128,512]{1,0:T(8,128)S(1)}, u32[]{:S(2)}, u32[]{:S(2)}) collective-permute-start(f32[128,512]{1,0:T(8,128)} %get-tuple-element.80), channel_id=1, source_target_pairs={{0,4},{4,0},{8,12},{12,8},{16,20},{20,16},{24,28},{28,24},{1,5},{5... | collective-permute-start | bytes 786440 | tf_op jit(solution)/shard_map/ppermute | solution.py:235
  59.7 45.2 %collective-permute-start.9 = (f32[2048,128]{1,0:T(8,128)}, f32[2048,128]{1,0:T(8,128)}, u32[]{:S(2)}, u32[]{:S(2)}) collective-permute-start(f32[2048,128]{1,0:T(8,128)} %collective-permute-done.2.refs_3_.refs_2_.refs_4_), channel_id=1, source_target_pairs={{0,1},{1,0},{2,3},{3,2},{4,5},{5,4},{6,7},{7,6},{8,9},{9,8},{10,11... | collective-permute-start | bytes 3145736 | tf_op jit(solution)/shard_map/ppermute | solution.py:265
  61.2 43.7 %collective-permute-start.10 = (f32[2048,128]{1,0:T(8,128)}, f32[2048,128]{1,0:T(8,128)}, u32[]{:S(2)}, u32[]{:S(2)}) collective-permute-start(f32[2048,128]{1,0:T(8,128)} %collective-permute-done.1.refs_1_.refs_3_.refs_2_), channel_id=1, source_target_pairs={{0,2},{1,3},{2,0},{3,1},{4,6},{5,7},{6,4},{7,5},{8,10},{9,11},{10,... | collective-permute-start | bytes 3145736 | tf_op jit(solution)/shard_map/ppermute | solution.py:265
  68.0 10.5 %copy-start.19 = (f32[128,1024]{1,0:T(8,128)}, f32[128,1024]{1,0:T(8,128)S(1)}, u32[]{:S(2)}) copy-start(f32[128,1024]{1,0:T(8,128)S(1)} %get-tuple-element.91.refs_6_) | copy-start | bytes 1572868
  72.9 7.2 %copy-start.35 = (s32[2,4]{1,0:T(2,128)S(1)}, s32[2,4]{1,0:T(2,128)}, u32[]{:S(2)}) copy-start(s32[2,4]{1,0:T(2,128)} %constant.105.clone) | copy-start | bytes 100
  76.8 9.1 %collective-permute-start.12 = (f32[128,512]{1,0:T(8,128)}, f32[128,512]{1,0:T(8,128)}, u32[]{:S(2)}, u32[]{:S(2)}) collective-permute-start(f32[128,512]{1,0:T(8,128)} %get-tuple-element.89), channel_id=1, source_target_pairs={{0,4},{4,0},{8,12},{12,8},{16,20},{20,16},{24,28},{28,24},{1,5},{5... | collective-permute-start | bytes 786440 | tf_op jit(solution)/shard_map/ppermute | solution.py:235
  76.9 19.0 %collective-permute-start.13 = (f32[128,1024]{1,0:T(8,128)}, f32[128,1024]{1,0:T(8,128)}, u32[]{:S(2)}, u32[]{:S(2)}) collective-permute-start(f32[128,1024]{1,0:T(8,128)} %get-tuple-element.90), channel_id=1, source_target_pairs={{0,8},{4,12},{8,0},{12,4},{16,24},{20,28},{24,16},{28,20},{1,9},{5... | collective-permute-start | bytes 1572872 | tf_op jit(solution)/shard_map/ppermute | solution.py:416
  78.6 17.3 %collective-permute-start.14 = (f32[128,1024]{1,0:T(8,128)S(1)}, f32[128,1024]{1,0:T(8,128)}, u32[]{:S(2)}, u32[]{:S(2)}) collective-permute-start(f32[128,1024]{1,0:T(8,128)S(1)} %get-tuple-element.91.refs_6_), channel_id=1, source_target_pairs={{8,16},{12,20},{16,8},{20,12},{9,17},{13,21},{17,9},{21,13},{10,18... | collective-permute-start | bytes 1572872 | tf_op jit(solution)/shard_map/ppermute | solution.py:421
  81.3 4.8 %copy-start.34 = (s32[2,4]{1,0:T(2,128)S(1)}, s32[2,4]{1,0:T(2,128)}, u32[]{:S(2)}) copy-start(s32[2,4]{1,0:T(2,128)} %constant.104.clone) | copy-start | bytes 100
  86.0 9.9 %collective-permute-start.11 = (f32[128,512]{1,0:T(8,128)}, f32[128,512]{1,0:T(8,128)}, u32[]{:S(2)}, u32[]{:S(2)}) collective-permute-start(f32[128,512]{1,0:T(8,128)} %get-tuple-element.87), channel_id=1, source_target_pairs={{0,4},{4,0},{8,12},{12,8},{16,20},{20,16},{24,28},{28,24},{1,5},{5... | collective-permute-start | bytes 786440 | tf_op jit(solution)/shard_map/ppermute | solution.py:235
  92.1 3.8 %copy-start.20 = (f32[128,1024]{1,0:T(8,128)S(1)}, f32[128,1024]{1,0:T(8,128)}, u32[]{:S(2)}) copy-start(f32[128,1024]{1,0:T(8,128)} %copy-done.19) | copy-start | bytes 1572868
  95.9 8.9 %copy-start.36 = (s32[4,2]{1,0:T(4,128)S(1)}, s32[4,2]{1,0:T(4,128)}, u32[]{:S(2)}) copy-start(s32[4,2]{1,0:T(4,128)} %constant.101.clone) | copy-start | bytes 100
  99.9 21.6 %collective-permute-start.18 = (f32[128,1024]{1,0:T(8,128)}, f32[128,1024]{1,0:T(8,128)}, u32[]{:S(2)}, u32[]{:S(2)}) collective-permute-start(f32[128,1024]{1,0:T(8,128)} %get-tuple-element.100), channel_id=1, source_target_pairs={{0,8},{4,12},{8,0},{12,4},{16,24},{20,28},{24,16},{28,20},{1,9},{5... | collective-permute-start | bytes 1572872 | tf_op jit(solution)/shard_map/ppermute | solution.py:416
  103.4 18.2 %collective-permute-start.19 = (f32[128,1024]{1,0:T(8,128)}, f32[128,1024]{1,0:T(8,128)}, u32[]{:S(2)}, u32[]{:S(2)}) collective-permute-start(f32[128,1024]{1,0:T(8,128)} %get-tuple-element.101.refs_8_), channel_id=1, source_target_pairs={{8,16},{12,20},{16,8},{20,12},{9,17},{13,21},{17,9},{21,13},{10,18... | collective-permute-start | bytes 1572872 | tf_op jit(solution)/shard_map/ppermute | solution.py:421
  113.0 4.1 %copy-start.1 = (bf16[512,2048]{1,0:T(8,128)(2,1)S(1)}, bf16[512,2048]{1,0:T(8,128)(2,1)}, u32[]{:S(2)}) copy-start(bf16[512,2048]{1,0:T(8,128)(2,1)} %copy-done) | copy-start | bytes 6291460
  113.0 8.5 %collective-permute-start.16 = (f32[128,512]{1,0:T(8,128)S(1)}, f32[128,512]{1,0:T(8,128)S(1)}, u32[]{:S(2)}, u32[]{:S(2)}) collective-permute-start(f32[128,512]{1,0:T(8,128)S(1)} %get-tuple-element.97), channel_id=1, source_target_pairs={{0,4},{4,0},{8,12},{12,8},{16,20},{20,16},{24,28},{28,24},{1,5},{5... | collective-permute-start | bytes 786440 | tf_op jit(solution)/shard_map/ppermute | solution.py:235
  116.7 4.9 %copy-start.12 = (f32[128,1024]{1,0:T(8,128)S(1)}, f32[128,1024]{1,0:T(8,128)}, u32[]{:S(2)}) copy-start(f32[128,1024]{1,0:T(8,128)} %copy-done.11) | copy-start | bytes 1572868
  116.7 4.8 %collective-permute-start.15 = (f32[128,512]{1,0:T(8,128)S(1)}, f32[128,512]{1,0:T(8,128)S(1)}, u32[]{:S(2)}, u32[]{:S(2)}) collective-permute-start(f32[128,512]{1,0:T(8,128)S(1)} %get-tuple-element.95), channel_id=1, source_target_pairs={{0,4},{4,0},{8,12},{12,8},{16,20},{20,16},{24,28},{28,24},{1,5},{5... | collective-permute-start | bytes 786440 | tf_op jit(solution)/shard_map/ppermute | solution.py:235
  120.1 1.4 collective-permute-start.17
  123.2 5.0 %copy-start.3 = (f32[128,1024]{1,0:T(8,128)}, f32[128,1024]{1,0:T(8,128)S(1)}, u32[]{:S(2)}) copy-start(f32[128,1024]{1,0:T(8,128)S(1)} %get-tuple-element.111.refs_0_) | copy-start | bytes 1572868
  123.2 16.9 %collective-permute-start.22 = (f32[128,1280]{1,0:T(8,128)S(1)}, f32[128,1280]{1,0:T(8,128)S(1)}, u32[]{:S(2)}, u32[]{:S(2)}) collective-permute-start(f32[128,1280]{1,0:T(8,128)S(1)} %get-tuple-element.108), channel_id=1, source_target_pairs={{0,8},{4,12},{8,0},{12,4},{16,24},{20,28},{24,16},{28,20},{1,9},{5... | collective-permute-start | bytes 1966088 | tf_op jit(solution)/shard_map/ppermute | solution.py:416
  124.2 9.4 %collective-permute-start.23 = (f32[128,1024]{1,0:T(8,128)S(1)}, f32[128,1024]{1,0:T(8,128)S(1)}, u32[]{:S(2)}, u32[]{:S(2)}) collective-permute-start(f32[128,1024]{1,0:T(8,128)S(1)} %get-tuple-element.109.refs_6_), channel_id=1, source_target_pairs={{8,16},{12,20},{16,8},{20,12},{9,17},{13,21},{17,9},{21,13},{10,18... | collective-permute-start | bytes 1572872 | tf_op jit(solution)/shard_map/ppermute | solution.py:421
  124.8 8.7 %collective-permute-start.24 = (f32[128,1024]{1,0:T(8,128)S(1)}, f32[128,1024]{1,0:T(8,128)S(1)}, u32[]{:S(2)}, u32[]{:S(2)}) collective-permute-start(f32[128,1024]{1,0:T(8,128)S(1)} %get-tuple-element.111.refs_0_), channel_id=1, source_target_pairs={{0,4},{4,0},{8,12},{12,8},{16,20},{20,16},{24,28},{28,24},{1,5},{5... | collective-permute-start | bytes 1572872 | tf_op jit(solution)/shard_map/ppermute | solution.py:235
  128.2 3.9 %collective-permute-start.21 = (f32[128,512]{1,0:T(8,128)S(1)}, f32[128,512]{1,0:T(8,128)S(1)}, u32[]{:S(2)}, u32[]{:S(2)}) collective-permute-start(f32[128,512]{1,0:T(8,128)S(1)} %get-tuple-element.107), channel_id=1, source_target_pairs={{0,4},{4,0},{8,12},{12,8},{16,20},{20,16},{24,28},{28,24},{1,5},{5... | collective-permute-start | bytes 786440 | tf_op jit(solution)/shard_map/ppermute | solution.py:235
  131.9 1.6 collective-permute-start.20
  140.4 7.9 %copy-start.9 = (f32[128,1024]{1,0:T(8,128)}, f32[128,1024]{1,0:T(8,128)S(1)}, u32[]{:S(2)}) copy-start(f32[128,1024]{1,0:T(8,128)S(1)} %get-tuple-element.112.refs_0_) | copy-start | bytes 1572868
  140.4 15.9 %collective-permute-start.29 = (f32[128,1280]{1,0:T(8,128)S(1)}, f32[128,1280]{1,0:T(8,128)S(1)}, u32[]{:S(2)}, u32[]{:S(2)}) collective-permute-start(f32[128,1280]{1,0:T(8,128)S(1)} %get-tuple-element.119.refs_6_), channel_id=1, source_target_pairs={{8,16},{12,20},{16,8},{20,12},{9,17},{13,21},{17,9},{21,13},{10,18... | collective-permute-start | bytes 1966088 | tf_op jit(solution)/shard_map/ppermute | solution.py:421
  141.1 15.1 %collective-permute-start.28 = (f32[128,1024]{1,0:T(8,128)S(1)}, f32[128,1024]{1,0:T(8,128)S(1)}, u32[]{:S(2)}, u32[]{:S(2)}) collective-permute-start(f32[128,1024]{1,0:T(8,128)S(1)} %get-tuple-element.118), channel_id=1, source_target_pairs={{0,8},{4,12},{8,0},{12,4},{16,24},{20,28},{24,16},{28,20},{1,9},{5... | collective-permute-start | bytes 1572872 | tf_op jit(solution)/shard_map/ppermute | solution.py:416
  145.1 11.2 %collective-permute-start.25 = (f32[128,1024]{1,0:T(8,128)S(1)}, f32[128,1024]{1,0:T(8,128)S(1)}, u32[]{:S(2)}, u32[]{:S(2)}) collective-permute-start(f32[128,1024]{1,0:T(8,128)S(1)} %get-tuple-element.112.refs_0_), channel_id=1, source_target_pairs={{0,4},{4,0},{8,12},{12,8},{16,20},{20,16},{24,28},{28,24},{1,5},{5... | collective-permute-start | bytes 1572872 | tf_op jit(solution)/shard_map/ppermute | solution.py:235
  148.3 3.9 %collective-permute-start.27 = (f32[128,512]{1,0:T(8,128)S(1)}, f32[128,512]{1,0:T(8,128)S(1)}, u32[]{:S(2)}, u32[]{:S(2)}) collective-permute-start(f32[128,512]{1,0:T(8,128)S(1)} %get-tuple-element.117), channel_id=1, source_target_pairs={{0,4},{4,0},{8,12},{12,8},{16,20},{20,16},{24,28},{28,24},{1,5},{5... | collective-permute-start | bytes 786440 | tf_op jit(solution)/shard_map/ppermute | solution.py:235
  152.1 1.6 collective-permute-start.26
  157.1 18.9 %copy-start.31 = (s32[4,6]{1,0:T(4,128)S(1)}, s32[4,6]{1,0:T(4,128)}, u32[]{:S(2)}) copy-start(s32[4,6]{1,0:T(4,128)} %constant.103.clone) | copy-start | bytes 292
  157.1 18.9 %copy-start.32 = (s32[4,6]{1,0:T(4,128)S(1)}, s32[4,6]{1,0:T(4,128)}, u32[]{:S(2)}) copy-start(s32[4,6]{1,0:T(4,128)} %constant.102.clone) | copy-start | bytes 292
  157.1 19.1 %copy-start.33 = (s32[2,3]{1,0:T(2,128)S(1)}, s32[2,3]{1,0:T(2,128)}, u32[]{:S(2)}) copy-start(s32[2,3]{1,0:T(2,128)} %constant.106.clone) | copy-start | bytes 76
  157.1 16.3 %collective-permute-start.30 = (f32[128,1280]{1,0:T(8,128)S(1)}, f32[128,1280]{1,0:T(8,128)S(1)}, u32[]{:S(2)}, u32[]{:S(2)}) collective-permute-start(f32[128,1280]{1,0:T(8,128)S(1)} %get-tuple-element.121), channel_id=1, source_target_pairs={{0,8},{4,12},{8,0},{12,4},{16,24},{20,28},{24,16},{28,20},{1,9},{5... | collective-permute-start | bytes 1966088 | tf_op jit(solution)/shard_map/ppermute | solution.py:416
  159.9 1.6 collective-permute-start.31
  160.6 2.0 collective-permute-start.32
  176.0 2.1 collective-permute-start.35
  176.3 18.2 %copy-start.2 = (f32[3,256,256]{2,1,0:T(8,128)S(1)}, f32[3,256,256]{2,1,0:T(8,128)}, u32[]{:S(2)}) copy-start(f32[3,256,256]{2,1,0:T(8,128)} %refs_6_.5) | copy-start | bytes 2359300
  178.2 12.9 %collective-permute-start.38 = (f32[256,256]{1,0:T(8,128)S(1)}, f32[256,256]{1,0:T(8,128)}, u32[]{:S(2)}, u32[]{:S(2)}) collective-permute-start(f32[256,256]{1,0:T(8,128)S(1)} %maximum_select_fusion), channel_id=1, source_target_pairs={{0,3},{1,2},{2,1},{3,0},{4,7},{5,6},{6,5},{7,4},{8,11},{9,10},{10,... | collective-permute-start | bytes 786440 | tf_op jit(solution)/shard_map/ppermute | solution.py:432
  179.7 13.5 %collective-permute-start.37 = (f32[256,256]{1,0:T(8,128)S(1)}, f32[256,256]{1,0:T(8,128)}, u32[]{:S(2)}, u32[]{:S(2)}) collective-permute-start(f32[256,256]{1,0:T(8,128)S(1)} %maximum_select_fusion), channel_id=1, source_target_pairs={{0,2},{1,3},{2,0},{3,1},{4,6},{5,7},{6,4},{7,5},{8,10},{9,11},{10,... | collective-permute-start | bytes 786440 | tf_op jit(solution)/shard_map/ppermute | solution.py:432
  181.2 12.0 %collective-permute-start.36 = (f32[256,256]{1,0:T(8,128)S(1)}, f32[256,256]{1,0:T(8,128)}, u32[]{:S(2)}, u32[]{:S(2)}) collective-permute-start(f32[256,256]{1,0:T(8,128)S(1)} %maximum_select_fusion), channel_id=1, source_target_pairs={{0,1},{1,0},{2,3},{3,2},{4,5},{5,4},{6,7},{7,6},{8,9},{9,8},{10,11... | collective-permute-start | bytes 786440 | tf_op jit(solution)/shard_map/ppermute | solution.py:432
  188.3 6.2 %copy-start.4 = (f32[128,1024]{1,0:T(8,128)S(1)}, f32[128,1024]{1,0:T(8,128)}, u32[]{:S(2)}) copy-start(f32[128,1024]{1,0:T(8,128)} %copy-done.3) | copy-start | bytes 1572868
  188.3 6.2 %copy-start.8 = (f32[128,1024]{1,0:T(8,128)S(1)}, f32[128,1024]{1,0:T(8,128)}, u32[]{:S(2)}) copy-start(f32[128,1024]{1,0:T(8,128)} %copy-done.7) | copy-start | bytes 1572868
  188.3 18.2 %collective-permute-start.33 = (f32[128,1024]{1,0:T(8,128)}, f32[128,1024]{1,0:T(8,128)S(1)}, u32[]{:S(2)}, u32[]{:S(2)}) collective-permute-start(f32[128,1024]{1,0:T(8,128)} %copy-done.27), channel_id=1, source_target_pairs={{0,8},{4,12},{8,0},{12,4},{16,24},{20,28},{24,16},{28,20},{1,9},{5... | collective-permute-start | bytes 1572872 | tf_op jit(solution)/shard_map/ppermute | solution.py:416
  190.1 16.4 %collective-permute-start.34 = (f32[128,1024]{1,0:T(8,128)}, f32[128,1024]{1,0:T(8,128)S(1)}, u32[]{:S(2)}, u32[]{:S(2)}) collective-permute-start(f32[128,1024]{1,0:T(8,128)} %copy-done.15), channel_id=1, source_target_pairs={{8,16},{12,20},{16,8},{20,12},{9,17},{13,21},{17,9},{21,13},{10,18... | collective-permute-start | bytes 1572872 | tf_op jit(solution)/shard_map/ppermute | solution.py:421
  194.5 12.0 %copy-start.16 = (f32[128,1024]{1,0:T(8,128)S(1)}, f32[128,1024]{1,0:T(8,128)}, u32[]{:S(2)}) copy-start(f32[128,1024]{1,0:T(8,128)} %copy-done.15) | copy-start | bytes 1572868
  194.5 12.0 %copy-start.18 = (f32[128,1024]{1,0:T(8,128)S(1)}, f32[128,1024]{1,0:T(8,128)}, u32[]{:S(2)}) copy-start(f32[128,1024]{1,0:T(8,128)} %copy-done.17) | copy-start | bytes 1572868
  206.7 13.9 %collective-permute-start.40 = (f32[128,1024]{1,0:T(8,128)S(1)}, f32[128,1024]{1,0:T(8,128)S(1)}, u32[]{:S(2)}, u32[]{:S(2)}) collective-permute-start(f32[128,1024]{1,0:T(8,128)S(1)} %get-tuple-element.135), channel_id=1, source_target_pairs={{0,8},{4,12},{8,0},{12,4},{16,24},{20,28},{24,16},{28,20},{1,9},{5... | collective-permute-start | bytes 1572872 | tf_op jit(solution)/shard_map/ppermute | solution.py:416
  208.5 12.6 %collective-permute-start.39 = (f32[128,1024]{1,0:T(8,128)S(1)}, f32[128,1024]{1,0:T(8,128)S(1)}, u32[]{:S(2)}, u32[]{:S(2)}) collective-permute-start(f32[128,1024]{1,0:T(8,128)S(1)} %get-tuple-element.134.refs_2_), channel_id=1, source_target_pairs={{0,4},{4,0},{8,12},{12,8},{16,20},{20,16},{24,28},{28,24},{1,5},{5... | collective-permute-start | bytes 1572872 | tf_op jit(solution)/shard_map/ppermute | solution.py:235
  208.5 14.2 %copy-start.6 = (f32[128,1024]{1,0:T(8,128)S(1)}, f32[128,1024]{1,0:T(8,128)}, u32[]{:S(2)}) copy-start(f32[128,1024]{1,0:T(8,128)} %copy-done.5) | copy-start | bytes 1572868
  208.5 14.2 %copy-start.10 = (f32[128,1024]{1,0:T(8,128)S(1)}, f32[128,1024]{1,0:T(8,128)}, u32[]{:S(2)}) copy-start(f32[128,1024]{1,0:T(8,128)} %copy-done.9) | copy-start | bytes 1572868
  220.7 2.0 collective-permute-start.41
  (15 other events, 17.7 us)

commit v5 on v0

--- a/solution.py
+++ b/solution.py
@@ -63,7 +63,7 @@
         in_specs=[pl.BlockSpec((step, columns), lambda i: (i, 0))],
         out_specs=pl.BlockSpec((blocks, 2, step, width), lambda i: (0, 0, i, 0)),
         out_shape=pltpu.HBM((blocks, 2, rows, width), BF16),
-        compiler_params=params(49),
+        compiler_params=params(63),
         cost_estimate=cost(rows * columns * 4, rows * columns * 8),
         name="split_x",
     )(x)
@@ -410,7 +410,7 @@
         if step + 1 == chunks.index((PANELS - 1, 0)):
             ahead.extend(rounds[-1][0][:2])
         if step == gram_chunk - 1:
-            ahead.extend(gram_sides)
+            ahead.extend([gram_sides[0], pinned(gram_sides[1])])
         if step == count + 1:
             ahead.append(grams)
         if 0 <= outward - 1 < count - 2:

time: 236 us -> 235 us (level); the launches traced: 232 us -> 234 us
  waiting for transfers between devices: 38.7 us -> 47.8 us
  local copies, waits for them, and re-layouts: 18 us -> 9.54 us
  Pallas kernels: 119 us -> 122 us
    unnamed x70 -> x44, local copies, waits for them, and re-layouts: 12.4 us -> 3.85 us
    ppermute x8, waiting for transfers between devices: 17.8 us -> 25.3 us  [shards_square(): outer[step] = lax.ppermute(results['out'], 'row', outer_pairs)]
    pallas_call x5, Pallas kernels: 16.1 us -> 20.7 us  [choose(): pl.pallas_call(functools.partial(choose_kernel, outputs, len(cases)), in_...]
    ppermute x8, starting transfers between devices: 22.2 us -> 24.7 us  [shards_square(): outer[step] = lax.ppermute(results['out'], 'row', outer_pairs)]
  transfers between devices with their start and end apart: 42 -> 42, of which waited for: 13 -> 14; matrix products, arithmetic and copies ran while one was open for 1% -> 1% of each run, Pallas kernels for 41% -> 42%
where the time goes in v5:
time: 235 us; the launch traced here: 234 us
  Pallas kernels  122 us (52%)
  waiting for transfers between devices  47.8 us (20%)
  starting transfers between devices  46.9 us (20%)
  local copies, waits for them, and re-layouts  9.54 us (4%)
  between operations  7.51 us (3%)
    pallas_call x13, Pallas kernels, products(): pl.pallas_call(functools.partial(products_kernel, block), in_specs=[in_vm...  42.4 us
    pallas_call x2, Pallas kernels, update(): pl.pallas_call(update_kernel, grid_spec=pltpu.PrefetchScalarGridSpec(num_...  37.6 us
    ppermute x8, waiting for transfers between devices, shards_square(): outer[step] = lax.ppermute(results['out'], 'row', outer_pairs)  25.3 us
    ppermute x8, starting transfers between devices, shards_square(): outer[step] = lax.ppermute(results['out'], 'row', outer_pairs)  24.7 us
    pallas_call x5, Pallas kernels, choose(): pl.pallas_call(functools.partial(choose_kernel, outputs, len(cases)), in_...  20.7 us
    ppermute x6, waiting for transfers between devices, fetch_square(): along = lambda value, step: lax.ppermute(value, 'col', pairs_of(4, step))  15 us
    pallas_call x1, Pallas kernels, split_array(): pl.pallas_call(split_kernel, grid=(rows // step,), in_specs=[pl.BlockSpec...  14.6 us
    ppermute x6, starting transfers between devices, fetch_square(): along = lambda value, step: lax.ppermute(value, 'col', pairs_of(4, step))  8.25 us
  transfers between devices with their start and end apart: 42, of which 14 were waited for; matrix products, arithmetic and copies ran while one was open for 1% of the time, Pallas kernels for 42%

profile of v5, /device:TPU:0, one launch (start us, length us, event | category | flops | bytes accessed | tf_op | source)
XLA Modules:
  0.0 233.8 jit_solution(13943251624643633684)
XLA Ops:
  0.0 3.1 %fusion.14 = (f32[2048,128]{1,0:T(8,128)}, f32[2048,128]{1,0:T(8,128)}) fusion(f32[2048,256]{1,0:T(8,128)} %bitcast.37), kind=kLoop, calls=%fused_computation.37 | loop fusion | bytes 4194304 | tf_op jit(solution)/shard_map/slice | solution.py:266
  3.1 2.9 %collective-permute-start.5 = (f32[2048,128]{1,0:T(8,128)}, f32[2048,128]{1,0:T(8,128)}, u32[]{:S(2)}, u32[]{:S(2)}) collective-permute-start(f32[2048,128]{1,0:T(8,128)} %get-tuple-element.138.refs_0_), channel_id=1, source_target_pairs={{0,1},{1,0},{2,3},{3,2},{4,5},{5,4},{6,7},{7,6},{8,9},{9,8},{10,11... | collective-permute-start | bytes 3145736 | tf_op jit(solution)/shard_map/ppermute | solution.py:265
  6.0 1.5 collective-permute-start
  8.1 14.6 %split_x.1.both_ref = bf16[4,2,2048,512]{3,2,1,0:T(8,128)(2,1)} custom-call(f32[2048,2048]{1,0:T(8,128)} %refs_11_.3), custom_call_target="tpu_custom_call" | custom-call | flops 262144 | bytes 524288 | tf_op jit(solution)/shard_map/split_x/pallas_call | solution.py:60
  22.9 7.4 %collective-permute-done.5.refs_2_.refs_0_ = f32[2048,128]{1,0:T(8,128)} collective-permute-done((f32[2048,128]{1,0:T(8,128)}, f32[2048,128]{1,0:T(8,128)}, u32[]{:S(2)}, u32[]{:S(2)}) %collective-permute-start.5) | collective-permute-done | bytes 1048608 | tf_op jit(solution)/shard_map/ppermute | solution.py:265
  30.3 2.1 collective-permute-done.refs_3_.refs_4_.refs_2_
  32.4 4.8 %choose_panel.5 = (bf16[1,2,2048,256]{3,2,1,0:T(8,128)(2,1)}, bf16[512,2048]{1,0:T(8,128)(2,1)S(1)}) custom-call(s32[2]{0:T(128)S(1)} %broadcast_select_fusion.1.which_ref, f32[2048,128]{1,0:T(8,128)} %get-tuple-element.138.refs_0_, f32[2048,128]{1,0:T(8,128)} %get-tuple-element.137.refs_1_, f32[2048,128]{1,0:T(8,128)} %collective-permute-done.5.refs_2_.refs_0_, ...), custom_call_target="tpu_custom_call" | custom-call | flops 32768 | bytes 98304 | tf_op jit(solution)/shard_map/choose_panel/pallas_call | solution.py:106
  37.3 3.2 %products.14 = (f32[128,512]{1,0:T(8,128)S(1)}, f32[128,512]{1,0:T(8,128)S(1)}) custom-call(bf16[512,2048]{1,0:T(8,128)(2,1)S(1)} %get-tuple-element.71.flipped_ref, bf16[4,2,2048,512]{3,2,1,0:T(8,128)(2,1)} %split_x.1.both_ref), custom_call_target="tpu_custom_call" | custom-call | flops 25165824 | bytes 98304 | tf_op jit(solution)/shard_map/products/pallas_call | solution.py:150
  40.6 3.9 %products.13 = (f32[128,512]{1,0:T(8,128)S(1)}, f32[128,512]{1,0:T(8,128)}) custom-call(bf16[512,2048]{1,0:T(8,128)(2,1)S(1)} %get-tuple-element.71.flipped_ref, bf16[4,2,2048,512]{3,2,1,0:T(8,128)(2,1)} %split_x.1.both_ref), custom_call_target="tpu_custom_call" | custom-call | flops 25165824 | bytes 98304 | tf_op jit(solution)/shard_map/products/pallas_call | solution.py:150
  46.7 1.6 collective-permute-start.10
  48.3 3.6 %collective-permute-done.2.refs_3_.refs_1_.refs_2_ = f32[2048,128]{1,0:T(8,128)} collective-permute-done((f32[2048,128]{1,0:T(8,128)}, f32[2048,128]{1,0:T(8,128)}, u32[]{:S(2)}, u32[]{:S(2)}) %collective-permute-start.2) | collective-permute-done | bytes 1048608 | tf_op jit(solution)/shard_map/ppermute | solution.py:265
  51.9 1.8 collective-permute-start.3
  53.7 3.2 %products.16 = (f32[128,512]{1,0:T(8,128)S(1)}, f32[128,512]{1,0:T(8,128)S(1)}) custom-call(bf16[512,2048]{1,0:T(8,128)(2,1)S(1)} %get-tuple-element.71.flipped_ref, bf16[4,2,2048,512]{3,2,1,0:T(8,128)(2,1)} %split_x.1.both_ref, f32[128,1024]{1,0:T(8,128)S(1)} %get-tuple-element.76.refs_0_.refs_6_.refs_5_), custom_call_target="tpu_custom_call" | custom-call | flops 25165824 | bytes 98304 | tf_op jit(solution)/shard_map/products/pallas_call | solution.py:150
  57.0 3.2 %products.15 = (f32[128,512]{1,0:T(8,128)S(1)}, f32[128,512]{1,0:T(8,128)S(1)}) custom-call(bf16[512,2048]{1,0:T(8,128)(2,1)S(1)} %get-tuple-element.71.flipped_ref, bf16[4,2,2048,512]{3,2,1,0:T(8,128)(2,1)} %split_x.1.both_ref, f32[128,1024]{1,0:T(8,128)S(1)} %get-tuple-element.76.refs_0_.refs_6_.refs_5_), custom_call_target="tpu_custom_call" | custom-call | flops 25165824 | bytes 98304 | tf_op jit(solution)/shard_map/products/pallas_call | solution.py:150
  62.0 4.6 %choose_panel.7.refs_7_.both_ref = bf16[1,2,2048,256]{3,2,1,0:T(8,128)(2,1)} custom-call(s32[2]{0:T(128)S(1)} %iota_add_fusion.which_ref, f32[2048,128]{1,0:T(8,128)} %get-tuple-element.138.refs_0_, f32[2048,128]{1,0:T(8,128)} %get-tuple-element.137.refs_1_, f32[2048,128]{1,0:T(8,128)} %collective-permute-done.5.refs_2_.refs_0_, ...), custom_call_target="tpu_custom_call" | custom-call | flops 32768 | bytes 98304 | tf_op jit(solution)/shard_map/choose_panel/pallas_call | solution.py:106
  66.6 3.7 %choose_panel.6.refs_6_.flipped_ref = bf16[512,2048]{1,0:T(8,128)(2,1)S(1)} custom-call(s32[2]{0:T(128)S(1)} %broadcast_select_fusion.which_ref, f32[2048,128]{1,0:T(8,128)} %get-tuple-element.138.refs_0_, f32[2048,128]{1,0:T(8,128)} %get-tuple-element.137.refs_1_, f32[2048,128]{1,0:T(8,128)} %collective-permute-done.5.refs_2_.refs_0_, ...), custom_call_target="tpu_custom_call" | custom-call | flops 32768 | bytes 98304 | tf_op jit(solution)/shard_map/choose_panel/pallas_call | solution.py:106
  70.5 4.9 %choose_panel.8 = (bf16[1,2,2048,256]{3,2,1,0:T(8,128)(2,1)}, bf16[512,2048]{1,0:T(8,128)(2,1)S(1)}) custom-call(s32[2]{0:T(128)S(1)} %broadcast_select_fusion.2.which_ref, f32[2048,128]{1,0:T(8,128)} %collective-permute-done.5.refs_2_.refs_0_, f32[2048,128]{1,0:T(8,128)} %collective-permute-done.2.refs_3_.refs_1_.refs_2_, ...), custom_call_target="tpu_custom_call" | custom-call | flops 32768 | bytes 98304 | tf_op jit(solution)/shard_map/choose_panel/pallas_call | solution.py:106
  75.4 3.2 %products.18 = (f32[128,512]{1,0:T(8,128)S(1)}, f32[128,512]{1,0:T(8,128)S(1)}) custom-call(bf16[512,2048]{1,0:T(8,128)(2,1)S(1)} %get-tuple-element.83.flipped_ref, bf16[4,2,2048,512]{3,2,1,0:T(8,128)(2,1)} %split_x.1.both_ref, f32[128,1024]{1,0:T(8,128)S(1)} %get-tuple-element.82.refs_4_.refs_0_.refs_7_), custom_call_target="tpu_custom_call" | custom-call | flops 25165824 | bytes 98304 | tf_op jit(solution)/shard_map/products/pallas_call | solution.py:150
  78.8 3.0 %products.19 = (f32[128,256]{1,0:T(8,128)S(1)}, f32[128,256]{1,0:T(8,128)S(1)}) custom-call(bf16[512,2048]{1,0:T(8,128)(2,1)S(1)} %choose_panel.6.refs_6_.flipped_ref, bf16[1,2,2048,256]{3,2,1,0:T(8,128)(2,1)} %choose_panel.7.refs_7_.both_ref, f32[128,1024]{1,0:T(8,128)S(1)} %get-tuple-element.82.refs_4_.refs_0_.refs_7_), custom_call_target="tpu_custom_call" | custom-call | flops 12582912 | bytes 65536 | tf_op jit(solution)/shard_map/products/pallas_call | solution.py:150
  81.8 1.6 collective-permute-start.14
  83.5 0.7 collective-permute-start.15
  84.4 1.2 collective-permute-done.13.refs_5_
  85.6 1.5 collective-permute-start.1
  87.1 3.2 %products.17 = (f32[128,512]{1,0:T(8,128)S(1)}, f32[128,512]{1,0:T(8,128)S(1)}) custom-call(bf16[512,2048]{1,0:T(8,128)(2,1)S(1)} %get-tuple-element.83.flipped_ref, bf16[4,2,2048,512]{3,2,1,0:T(8,128)(2,1)} %split_x.1.both_ref, f32[128,1024]{1,0:T(8,128)S(1)} %get-tuple-element.82.refs_4_.refs_0_.refs_7_), custom_call_target="tpu_custom_call" | custom-call | flops 25165824 | bytes 98304 | tf_op jit(solution)/shard_map/products/pallas_call | solution.py:150
  90.4 1.5 collective-permute-done.11.refs_1_
  91.9 4.3 %collective-permute-done.14.refs_6_ = f32[128,1024]{1,0:T(8,128)S(1)} collective-permute-done((f32[128,1024]{1,0:T(8,128)S(1)}, f32[128,1024]{1,0:T(8,128)S(1)}, u32[]{:S(2)}, u32[]{:S(2)}) %collective-permute-start.14) | collective-permute-done | bytes 524320 | tf_op jit(solution)/shard_map/ppermute | solution.py:420
  96.5 4.7 %collective-permute-start.18 = (f32[128,1280]{1,0:T(8,128)S(1)}, f32[128,1280]{1,0:T(8,128)S(1)}, u32[]{:S(2)}, u32[]{:S(2)}) collective-permute-start(f32[128,1280]{1,0:T(8,128)S(1)} %get-tuple-element.97), channel_id=1, source_target_pairs={{0,8},{4,12},{8,0},{12,4},{16,24},{20,28},{24,16},{28,20},{1,9},{5... | collective-permute-start | bytes 1966088 | tf_op jit(solution)/shard_map/ppermute | solution.py:420
  101.1 0.9 collective-permute-start.19
  102.0 3.2 %products.21 = (f32[128,512]{1,0:T(8,128)S(1)}, f32[128,512]{1,0:T(8,128)S(1)}) custom-call(bf16[512,2048]{1,0:T(8,128)(2,1)S(1)} %get-tuple-element.83.flipped_ref, bf16[4,2,2048,512]{3,2,1,0:T(8,128)(2,1)} %split_x.1.both_ref, f32[128,1280]{1,0:T(8,128)S(1)} %get-tuple-element.92.refs_0_.refs_5_), custom_call_target="tpu_custom_call" | custom-call | flops 25165824 | bytes 98304 | tf_op jit(solution)/shard_map/products/pallas_call | solution.py:150
  105.3 3.2 %products.20 = (f32[128,512]{1,0:T(8,128)S(1)}, f32[128,512]{1,0:T(8,128)S(1)}) custom-call(bf16[512,2048]{1,0:T(8,128)(2,1)S(1)} %get-tuple-element.83.flipped_ref, bf16[4,2,2048,512]{3,2,1,0:T(8,128)(2,1)} %split_x.1.both_ref, f32[128,1280]{1,0:T(8,128)S(1)} %get-tuple-element.92.refs_0_.refs_5_), custom_call_target="tpu_custom_call" | custom-call | flops 25165824 | bytes 98304 | tf_op jit(solution)/shard_map/products/pallas_call | solution.py:150
  109.1 1.9 collective-permute-done.1.refs_9_.refs_0_
  111.0 4.7 %collective-permute-done.18.refs_4_ = f32[128,1280]{1,0:T(8,128)S(1)} collective-permute-done((f32[128,1280]{1,0:T(8,128)S(1)}, f32[128,1280]{1,0:T(8,128)S(1)}, u32[]{:S(2)}, u32[]{:S(2)}) %collective-permute-start.18) | collective-permute-done | bytes 655392 | tf_op jit(solution)/shard_map/ppermute | solution.py:420
  115.7 1.3 exchange.12
  117.0 0.8 copy-done.9
  117.8 1.5 collective-permute-start.23
  119.3 3.6 %collective-permute-start.22 = (f32[128,1024]{1,0:T(8,128)}, f32[128,1024]{1,0:T(8,128)}, u32[]{:S(2)}, u32[]{:S(2)}) collective-permute-start(f32[128,1024]{1,0:T(8,128)} %get-tuple-element.106), channel_id=1, source_target_pairs={{0,8},{4,12},{8,0},{12,4},{16,24},{20,28},{24,16},{28,20},{1,9},{5... | collective-permute-start | bytes 1572872 | tf_op jit(solution)/shard_map/ppermute | solution.py:420
  123.1 2.6 %choose_panel.9 = (bf16[1,2,2048,256]{3,2,1,0:T(8,128)(2,1)}, bf16[512,2048]{1,0:T(8,128)(2,1)S(1)}) custom-call(s32[2]{0:T(128)S(1)} %broadcast_select_fusion.3.which_ref, f32[2048,128]{1,0:T(8,128)S(1)} %collective-permute-done.1.refs_9_.refs_0_, f32[2048,128]{1,0:T(8,128)S(1)} %collective-permute-done.3.refs_10_.refs_1_, ...), custom_call_target="tpu_custom_call" | custom-call | flops 32768 | bytes 98304 | tf_op jit(solution)/shard_map/choose_panel/pallas_call | solution.py:106
  125.7 3.2 %products.23 = (f32[128,512]{1,0:T(8,128)S(1)}, f32[128,512]{1,0:T(8,128)S(1)}) custom-call(bf16[512,2048]{1,0:T(8,128)(2,1)S(1)} %get-tuple-element.101.flipped_ref, bf16[4,2,2048,512]{3,2,1,0:T(8,128)(2,1)} %split_x.1.both_ref, f32[128,1024]{1,0:T(8,128)S(1)} %get-tuple-element.100.refs_4_.refs_0_.refs_5_), custom_call_target="tpu_custom_call" | custom-call | flops 25165824 | bytes 98304 | tf_op jit(solution)/shard_map/products/pallas_call | solution.py:150
  129.5 3.2 %products.22 = (f32[128,512]{1,0:T(8,128)S(1)}, f32[128,512]{1,0:T(8,128)S(1)}) custom-call(bf16[512,2048]{1,0:T(8,128)(2,1)S(1)} %get-tuple-element.101.flipped_ref, bf16[4,2,2048,512]{3,2,1,0:T(8,128)(2,1)} %split_x.1.both_ref, f32[128,1024]{1,0:T(8,128)S(1)} %get-tuple-element.100.refs_4_.refs_0_.refs_5_), custom_call_target="tpu_custom_call" | custom-call | flops 25165824 | bytes 98304 | tf_op jit(solution)/shard_map/products/pallas_call | solution.py:150
  132.9 1.5 collective-permute-done.20.refs_1_
  134.4 1.9 exchange.13
  136.4 2.7 %collective-permute-start.28 = (f32[128,1280]{1,0:T(8,128)S(1)}, f32[128,1280]{1,0:T(8,128)S(1)}, u32[]{:S(2)}, u32[]{:S(2)}) collective-permute-start(f32[128,1280]{1,0:T(8,128)S(1)} %get-tuple-element.116), channel_id=1, source_target_pairs={{0,8},{4,12},{8,0},{12,4},{16,24},{20,28},{24,16},{28,20},{1,9},{5... | collective-permute-start | bytes 1966088 | tf_op jit(solution)/shard_map/ppermute | solution.py:420
  139.0 0.7 collective-permute-start.29
  139.7 3.2 %products.25 = (f32[128,512]{1,0:T(8,128)S(1)}, f32[128,512]{1,0:T(8,128)S(1)}) custom-call(bf16[512,2048]{1,0:T(8,128)(2,1)S(1)} %get-tuple-element.101.flipped_ref, bf16[4,2,2048,512]{3,2,1,0:T(8,128)(2,1)} %split_x.1.both_ref, f32[128,1024]{1,0:T(8,128)S(1)} %get-tuple-element.111.refs_0_.refs_5_), custom_call_target="tpu_custom_call" | custom-call | flops 25165824 | bytes 98304 | tf_op jit(solution)/shard_map/products/pallas_call | solution.py:150
  143.6 3.2 %products.24 = (f32[128,512]{1,0:T(8,128)S(1)}, f32[128,512]{1,0:T(8,128)S(1)}) custom-call(bf16[512,2048]{1,0:T(8,128)(2,1)S(1)} %get-tuple-element.101.flipped_ref, bf16[4,2,2048,512]{3,2,1,0:T(8,128)(2,1)} %split_x.1.both_ref, f32[128,1024]{1,0:T(8,128)S(1)} %get-tuple-element.111.refs_0_.refs_5_), custom_call_target="tpu_custom_call" | custom-call | flops 25165824 | bytes 98304 | tf_op jit(solution)/shard_map/products/pallas_call | solution.py:150
  146.9 1.5 collective-permute-done.26.refs_1_
  148.4 4.8 %collective-permute-done.28.refs_4_ = f32[128,1280]{1,0:T(8,128)S(1)} collective-permute-done((f32[128,1280]{1,0:T(8,128)S(1)}, f32[128,1280]{1,0:T(8,128)S(1)}, u32[]{:S(2)}, u32[]{:S(2)}) %collective-permute-start.28) | collective-permute-done | bytes 655392 | tf_op jit(solution)/shard_map/ppermute | solution.py:420
  153.6 2.2 collective-permute-start.30
  155.8 0.7 collective-permute-start.31
  156.6 1.5 collective-permute-start.38
  158.0 3.1 %collective-permute-start.37 = (f32[256,256]{1,0:T(8,128)S(1)}, f32[256,256]{1,0:T(8,128)S(1)}, u32[]{:S(2)}, u32[]{:S(2)}) collective-permute-start(f32[256,256]{1,0:T(8,128)S(1)} %maximum_select_fusion), channel_id=1, source_target_pairs={{0,2},{1,3},{2,0},{3,1},{4,6},{5,7},{6,4},{7,5},{8,10},{9,11},{10,... | collective-permute-start | bytes 786440 | tf_op jit(solution)/shard_map/ppermute | solution.py:436
  161.2 7.1 %collective-permute-done.30.refs_0_ = f32[128,1024]{1,0:T(8,128)S(1)} collective-permute-done((f32[128,1024]{1,0:T(8,128)S(1)}, f32[128,1024]{1,0:T(8,128)S(1)}, u32[]{:S(2)}, u32[]{:S(2)}) %collective-permute-start.30) | collective-permute-done | bytes 524320 | tf_op jit(solution)/shard_map/ppermute | solution.py:420
  168.5 3.7 %collective-permute-start.34 = (f32[128,1024]{1,0:T(8,128)S(1)}, f32[128,1024]{1,0:T(8,128)S(1)}, u32[]{:S(2)}, u32[]{:S(2)}) collective-permute-start(f32[128,1024]{1,0:T(8,128)S(1)} %get-tuple-element.125), channel_id=1, source_target_pairs={{0,8},{4,12},{8,0},{12,4},{16,24},{20,28},{24,16},{28,20},{1,9},{5... | collective-permute-start | bytes 1572872 | tf_op jit(solution)/shard_map/ppermute | solution.py:420
  172.2 0.9 collective-permute-start.35
  179.5 4.5 %collective-permute-done.34.refs_0_ = f32[128,1024]{1,0:T(8,128)S(1)} collective-permute-done((f32[128,1024]{1,0:T(8,128)S(1)}, f32[128,1024]{1,0:T(8,128)S(1)}, u32[]{:S(2)}, u32[]{:S(2)}) %collective-permute-start.34) | collective-permute-done | bytes 524320 | tf_op jit(solution)/shard_map/ppermute | solution.py:420
  184.0 1.1 exchange.16
  185.1 0.8 copy-done.11
  185.9 4.6 %collective-permute-start.39 = (f32[128,1024]{1,0:T(8,128)}, f32[128,1024]{1,0:T(8,128)}, u32[]{:S(2)}, u32[]{:S(2)}) collective-permute-start(f32[128,1024]{1,0:T(8,128)} %get-tuple-element.128), channel_id=1, source_target_pairs={{0,8},{4,12},{8,0},{12,4},{16,24},{20,28},{24,16},{28,20},{1,9},{5... | collective-permute-start | bytes 1572872 | tf_op jit(solution)/shard_map/ppermute | solution.py:420
  191.0 1.0 copy-done.2
  192.0 1.1 copy-done.4
  193.1 19.0 %update.2 = (f32[2048,2048]{1,0:T(8,128)}, f32[8,128]{1,0:T(8,128)S(1)}) custom-call(s32[6]{0:T(128)S(1)} %broadcast_select_fusion.4.place_ref, f32[128,1024]{1,0:T(8,128)} %get-tuple-element.109.refs_0_, f32[128,1024]{1,0:T(8,128)S(1)} %copy-done.2, f32[128,1280]{1,0:T(8,128)S(1)} %copy-done.4, f32[128,1280]{1,0:T(8,128)S(1)} %collective-permute-done.32.refs_5_.refs_3_, ...), custom_call_target="tpu_custom_call" | custom-call | flops 150994944 | bytes 360448 | tf_op jit(solution)/shard_map/update/pallas_call | solution.py:209
  212.1 1.1 exchange.17.refs_4_
  213.5 1.7 collective-permute-done.41.refs_5_
  215.2 18.6 %update.3 = (f32[2048,2048]{1,0:T(8,128)}, f32[8,128]{1,0:T(8,128)}) custom-call(s32[6]{0:T(128)S(1)} %broadcast_select_fusion.4.place_ref, f32[128,1024]{1,0:T(8,128)S(1)} %copy-done.6, f32[128,1024]{1,0:T(8,128)S(1)} %collective-permute-done.25.refs_9_.refs_1_, f32[128,1024]{1,0:T(8,128)S(1)} %copy-done.8, ...), custom_call_target="tpu_custom_call", output_to_operand_aliasing={{0}: (13, {})} | custom-call | flops 150994944 | bytes 360448 | tf_op jit(solution)/shard_map/update/pallas_call | solution.py:209
  (123 shorter events, 8.7 us)
Async XLA Ops:
  3.1 27.2 %collective-permute-start.5 = (f32[2048,128]{1,0:T(8,128)}, f32[2048,128]{1,0:T(8,128)}, u32[]{:S(2)}, u32[]{:S(2)}) collective-permute-start(f32[2048,128]{1,0:T(8,128)} %get-tuple-element.138.refs_0_), channel_id=1, source_target_pairs={{0,1},{1,0},{2,3},{3,2},{4,5},{5,4},{6,7},{7,6},{8,9},{9,8},{10,11... | collective-permute-start | bytes 3145736 | tf_op jit(solution)/shard_map/ppermute | solution.py:265
  6.0 26.4 %collective-permute-start = (f32[2048,128]{1,0:T(8,128)}, f32[2048,128]{1,0:T(8,128)}, u32[]{:S(2)}, u32[]{:S(2)}) collective-permute-start(f32[2048,128]{1,0:T(8,128)} %get-tuple-element.138.refs_0_), channel_id=1, source_target_pairs={{0,2},{1,3},{2,0},{3,1},{4,6},{5,7},{6,4},{7,5},{8,10},{9,11},{10,... | collective-permute-start | bytes 3145736 | tf_op jit(solution)/shard_map/ppermute | solution.py:265
  7.5 15.2 %copy-start.13 = (s32[3]{0:T(128)S(1)}, s32[3]{0:T(128)}, u32[]{:S(2)}) copy-start(s32[3]{0:T(128)} %param.14) | copy-start | bytes 40
  7.5 15.2 %copy-start.21 = (s32[4,2]{1,0:T(4,128)S(1)}, s32[4,2]{1,0:T(4,128)}, u32[]{:S(2)}) copy-start(s32[4,2]{1,0:T(4,128)} %constant.99.clone) | copy-start | bytes 100
  7.5 44.4 %collective-permute-start.2 = (f32[2048,128]{1,0:T(8,128)}, f32[2048,128]{1,0:T(8,128)}, u32[]{:S(2)}, u32[]{:S(2)}) collective-permute-start(f32[2048,128]{1,0:T(8,128)} %get-tuple-element.137.refs_1_), channel_id=1, source_target_pairs={{0,1},{1,0},{2,3},{3,2},{4,5},{5,4},{6,7},{7,6},{8,9},{9,8},{10,11... | collective-permute-start | bytes 3145736 | tf_op jit(solution)/shard_map/ppermute | solution.py:265
  8.1 54.0 %collective-permute-start.4 = (f32[2048,128]{1,0:T(8,128)}, f32[2048,128]{1,0:T(8,128)}, u32[]{:S(2)}, u32[]{:S(2)}) collective-permute-start(f32[2048,128]{1,0:T(8,128)} %get-tuple-element.137.refs_1_), channel_id=1, source_target_pairs={{0,2},{1,3},{2,0},{3,1},{4,6},{5,7},{6,4},{7,5},{8,10},{9,11},{10,... | collective-permute-start | bytes 3145736 | tf_op jit(solution)/shard_map/ppermute | solution.py:265
  40.5 4.8 %copy-start.14 = (s32[4,2]{1,0:T(4,128)S(1)}, s32[4,2]{1,0:T(4,128)}, u32[]{:S(2)}) copy-start(s32[4,2]{1,0:T(4,128)} %constant.101.clone) | copy-start | bytes 100
  40.5 4.8 %copy-start.15 = (s32[4,2]{1,0:T(4,128)S(1)}, s32[4,2]{1,0:T(4,128)}, u32[]{:S(2)}) copy-start(s32[4,2]{1,0:T(4,128)} %constant.100.clone) | copy-start | bytes 100
  40.5 4.9 %copy-start.20 = (s32[2,4]{1,0:T(2,128)S(1)}, s32[2,4]{1,0:T(2,128)}, u32[]{:S(2)}) copy-start(s32[2,4]{1,0:T(2,128)} %constant.104.clone) | copy-start | bytes 100
  40.5 6.1 %collective-permute-start.7 = (f32[128,512]{1,0:T(8,128)S(1)}, f32[128,512]{1,0:T(8,128)S(1)}, u32[]{:S(2)}, u32[]{:S(2)}) collective-permute-start(f32[128,512]{1,0:T(8,128)S(1)} %get-tuple-element.75), channel_id=1, source_target_pairs={{0,4},{4,0},{8,12},{12,8},{16,20},{20,16},{24,28},{28,24},{1,5},{5... | collective-permute-start | bytes 786440 | tf_op jit(solution)/shard_map/ppermute | solution.py:235
  44.5 2.1 collective-permute-start.6
  46.7 23.7 %collective-permute-start.10 = (f32[128,1024]{1,0:T(8,128)S(1)}, f32[128,1024]{1,0:T(8,128)S(1)}, u32[]{:S(2)}, u32[]{:S(2)}) collective-permute-start(f32[128,1024]{1,0:T(8,128)S(1)} %get-tuple-element.81), channel_id=1, source_target_pairs={{0,8},{4,12},{8,0},{12,4},{16,24},{20,28},{24,16},{28,20},{1,9},{5... | collective-permute-start | bytes 1572872 | tf_op jit(solution)/shard_map/ppermute | solution.py:420
  51.9 56.6 %collective-permute-start.3 = (f32[2048,128]{1,0:T(8,128)}, f32[2048,128]{1,0:T(8,128)S(1)}, u32[]{:S(2)}, u32[]{:S(2)}) collective-permute-start(f32[2048,128]{1,0:T(8,128)} %collective-permute-done.2.refs_3_.refs_1_.refs_2_), channel_id=1, source_target_pairs={{0,2},{1,3},{2,0},{3,1},{4,6},{5,7},{6,4},{7,5},{8,10},{9,11},{10,... | collective-permute-start | bytes 3145736 | tf_op jit(solution)/shard_map/ppermute | solution.py:265
  56.9 3.9 %copy-start.19 = (s32[2,4]{1,0:T(2,128)S(1)}, s32[2,4]{1,0:T(2,128)}, u32[]{:S(2)}) copy-start(s32[2,4]{1,0:T(2,128)} %constant.105.clone) | copy-start | bytes 100
  56.9 13.4 %collective-permute-start.9 = (f32[128,512]{1,0:T(8,128)S(1)}, f32[128,512]{1,0:T(8,128)S(1)}, u32[]{:S(2)}, u32[]{:S(2)}) collective-permute-start(f32[128,512]{1,0:T(8,128)S(1)} %get-tuple-element.80), channel_id=1, source_target_pairs={{0,4},{4,0},{8,12},{12,8},{16,20},{20,16},{24,28},{28,24},{1,5},{5... | collective-permute-start | bytes 786440 | tf_op jit(solution)/shard_map/ppermute | solution.py:235
  60.2 10.1 %collective-permute-start.8 = (f32[128,512]{1,0:T(8,128)S(1)}, f32[128,512]{1,0:T(8,128)S(1)}, u32[]{:S(2)}, u32[]{:S(2)}) collective-permute-start(f32[128,512]{1,0:T(8,128)S(1)} %get-tuple-element.78), channel_id=1, source_target_pairs={{0,4},{4,0},{8,12},{12,8},{16,20},{20,16},{24,28},{28,24},{1,5},{5... | collective-permute-start | bytes 786440 | tf_op jit(solution)/shard_map/ppermute | solution.py:235
  78.7 11.6 %collective-permute-start.12 = (f32[128,512]{1,0:T(8,128)S(1)}, f32[128,512]{1,0:T(8,128)S(1)}, u32[]{:S(2)}, u32[]{:S(2)}) collective-permute-start(f32[128,512]{1,0:T(8,128)S(1)} %get-tuple-element.87), channel_id=1, source_target_pairs={{0,4},{4,0},{8,12},{12,8},{16,20},{20,16},{24,28},{28,24},{1,5},{5... | collective-permute-start | bytes 786440 | tf_op jit(solution)/shard_map/ppermute | solution.py:235
  81.8 14.4 %collective-permute-start.14 = (f32[128,1024]{1,0:T(8,128)S(1)}, f32[128,1024]{1,0:T(8,128)S(1)}, u32[]{:S(2)}, u32[]{:S(2)}) collective-permute-start(f32[128,1024]{1,0:T(8,128)S(1)} %get-tuple-element.90), channel_id=1, source_target_pairs={{0,8},{4,12},{8,0},{12,4},{16,24},{20,28},{24,16},{28,20},{1,9},{5... | collective-permute-start | bytes 1572872 | tf_op jit(solution)/shard_map/ppermute | solution.py:420
  83.5 12.7 %collective-permute-start.15 = (f32[128,1024]{1,0:T(8,128)S(1)}, f32[128,1024]{1,0:T(8,128)S(1)}, u32[]{:S(2)}, u32[]{:S(2)}) collective-permute-start(f32[128,1024]{1,0:T(8,128)S(1)} %get-tuple-element.91.refs_8_), channel_id=1, source_target_pairs={{8,16},{12,20},{16,8},{20,12},{9,17},{13,21},{17,9},{21,13},{10,18... | collective-permute-start | bytes 1572872 | tf_op jit(solution)/shard_map/ppermute | solution.py:425
  84.2 1.4 collective-permute-start.13
  85.6 25.5 %collective-permute-start.1 = (f32[2048,128]{1,0:T(8,128)}, f32[2048,128]{1,0:T(8,128)S(1)}, u32[]{:S(2)}, u32[]{:S(2)}) collective-permute-start(f32[2048,128]{1,0:T(8,128)} %collective-permute-done.refs_3_.refs_4_.refs_2_), channel_id=1, source_target_pairs={{0,1},{1,0},{2,3},{3,2},{4,5},{5,4},{6,7},{7,6},{8,9},{9,8},{10,11... | collective-permute-start | bytes 3145736 | tf_op jit(solution)/shard_map/ppermute | solution.py:265
  90.3 1.6 collective-permute-start.11
  96.5 19.3 %collective-permute-start.18 = (f32[128,1280]{1,0:T(8,128)S(1)}, f32[128,1280]{1,0:T(8,128)S(1)}, u32[]{:S(2)}, u32[]{:S(2)}) collective-permute-start(f32[128,1280]{1,0:T(8,128)S(1)} %get-tuple-element.97), channel_id=1, source_target_pairs={{0,8},{4,12},{8,0},{12,4},{16,24},{20,28},{24,16},{28,20},{1,9},{5... | collective-permute-start | bytes 1966088 | tf_op jit(solution)/shard_map/ppermute | solution.py:420
  101.1 9.9 %collective-permute-start.19 = (f32[128,1024]{1,0:T(8,128)S(1)}, f32[128,1024]{1,0:T(8,128)S(1)}, u32[]{:S(2)}, u32[]{:S(2)}) collective-permute-start(f32[128,1024]{1,0:T(8,128)S(1)} %get-tuple-element.98.refs_6_), channel_id=1, source_target_pairs={{8,16},{12,20},{16,8},{20,12},{9,17},{13,21},{17,9},{21,13},{10,18... | collective-permute-start | bytes 1572872 | tf_op jit(solution)/shard_map/ppermute | solution.py:425
  105.2 5.8 %collective-permute-start.17 = (f32[128,512]{1,0:T(8,128)S(1)}, f32[128,512]{1,0:T(8,128)S(1)}, u32[]{:S(2)}, u32[]{:S(2)}) collective-permute-start(f32[128,512]{1,0:T(8,128)S(1)} %get-tuple-element.96), channel_id=1, source_target_pairs={{0,4},{4,0},{8,12},{12,8},{16,20},{20,16},{24,28},{28,24},{1,5},{5... | collective-permute-start | bytes 786440 | tf_op jit(solution)/shard_map/ppermute | solution.py:235
  108.6 2.5 %collective-permute-start.16 = (f32[128,512]{1,0:T(8,128)S(1)}, f32[128,512]{1,0:T(8,128)S(1)}, u32[]{:S(2)}, u32[]{:S(2)}) collective-permute-start(f32[128,512]{1,0:T(8,128)S(1)} %get-tuple-element.94), channel_id=1, source_target_pairs={{0,4},{4,0},{8,12},{12,8},{16,20},{20,16},{24,28},{28,24},{1,5},{5... | collective-permute-start | bytes 786440 | tf_op jit(solution)/shard_map/ppermute | solution.py:235
  117.0 0.8 copy-start.9
  117.8 16.6 %collective-permute-start.23 = (f32[128,1280]{1,0:T(8,128)}, f32[128,1280]{1,0:T(8,128)}, u32[]{:S(2)}, u32[]{:S(2)}) collective-permute-start(f32[128,1280]{1,0:T(8,128)} %get-tuple-element.107.refs_6_), channel_id=1, source_target_pairs={{8,16},{12,20},{16,8},{20,12},{9,17},{13,21},{17,9},{21,13},{10,18... | collective-permute-start | bytes 1966088 | tf_op jit(solution)/shard_map/ppermute | solution.py:425
  119.3 15.0 %collective-permute-start.22 = (f32[128,1024]{1,0:T(8,128)}, f32[128,1024]{1,0:T(8,128)}, u32[]{:S(2)}, u32[]{:S(2)}) collective-permute-start(f32[128,1024]{1,0:T(8,128)} %get-tuple-element.106), channel_id=1, source_target_pairs={{0,8},{4,12},{8,0},{12,4},{16,24},{20,28},{24,16},{28,20},{1,9},{5... | collective-permute-start | bytes 1572872 | tf_op jit(solution)/shard_map/ppermute | solution.py:420
  122.9 11.4 %collective-permute-start.24 = (f32[128,1024]{1,0:T(8,128)}, f32[128,1024]{1,0:T(8,128)S(1)}, u32[]{:S(2)}, u32[]{:S(2)}) collective-permute-start(f32[128,1024]{1,0:T(8,128)} %get-tuple-element.109.refs_0_), channel_id=1, source_target_pairs={{0,4},{4,0},{8,12},{12,8},{16,20},{20,16},{24,28},{28,24},{1,5},{5... | collective-permute-start | bytes 1572872 | tf_op jit(solution)/shard_map/ppermute | solution.py:235
  128.9 5.4 %copy-start.10 = (f32[128,1024]{1,0:T(8,128)S(1)}, f32[128,1024]{1,0:T(8,128)}, u32[]{:S(2)}) copy-start(f32[128,1024]{1,0:T(8,128)} %copy-done.9) | copy-start | bytes 1572868
  129.0 3.9 %collective-permute-start.21 = (f32[128,512]{1,0:T(8,128)S(1)}, f32[128,512]{1,0:T(8,128)S(1)}, u32[]{:S(2)}, u32[]{:S(2)}) collective-permute-start(f32[128,512]{1,0:T(8,128)S(1)} %get-tuple-element.105), channel_id=1, source_target_pairs={{0,4},{4,0},{8,12},{12,8},{16,20},{20,16},{24,28},{28,24},{1,5},{5... | collective-permute-start | bytes 786440 | tf_op jit(solution)/shard_map/ppermute | solution.py:235
  132.8 1.6 collective-permute-start.20
  134.4 2.0 copy-start.1
  136.3 6.6 %copy-start.5 = (f32[128,1024]{1,0:T(8,128)}, f32[128,1024]{1,0:T(8,128)S(1)}, u32[]{:S(2)}) copy-start(f32[128,1024]{1,0:T(8,128)S(1)} %get-tuple-element.110.refs_0_) | copy-start | bytes 1572868
  136.4 16.8 %collective-permute-start.28 = (f32[128,1280]{1,0:T(8,128)S(1)}, f32[128,1280]{1,0:T(8,128)S(1)}, u32[]{:S(2)}, u32[]{:S(2)}) collective-permute-start(f32[128,1280]{1,0:T(8,128)S(1)} %get-tuple-element.116), channel_id=1, source_target_pairs={{0,8},{4,12},{8,0},{12,4},{16,24},{20,28},{24,16},{28,20},{1,9},{5... | collective-permute-start | bytes 1966088 | tf_op jit(solution)/shard_map/ppermute | solution.py:420
  139.0 9.4 %collective-permute-start.25 = (f32[128,1024]{1,0:T(8,128)S(1)}, f32[128,1024]{1,0:T(8,128)S(1)}, u32[]{:S(2)}, u32[]{:S(2)}) collective-permute-start(f32[128,1024]{1,0:T(8,128)S(1)} %get-tuple-element.110.refs_0_), channel_id=1, source_target_pairs={{0,4},{4,0},{8,12},{12,8},{16,20},{20,16},{24,28},{28,24},{1,5},{5... | collective-permute-start | bytes 1572872 | tf_op jit(solution)/shard_map/ppermute | solution.py:235
  139.0 9.4 %collective-permute-start.29 = (f32[128,1024]{1,0:T(8,128)S(1)}, f32[128,1024]{1,0:T(8,128)S(1)}, u32[]{:S(2)}, u32[]{:S(2)}) collective-permute-start(f32[128,1024]{1,0:T(8,128)S(1)} %get-tuple-element.117.refs_6_), channel_id=1, source_target_pairs={{8,16},{12,20},{16,8},{20,12},{9,17},{13,21},{17,9},{21,13},{10,18... | collective-permute-start | bytes 1572872 | tf_op jit(solution)/shard_map/ppermute | solution.py:425
  143.0 3.9 %collective-permute-start.27 = (f32[128,512]{1,0:T(8,128)S(1)}, f32[128,512]{1,0:T(8,128)S(1)}, u32[]{:S(2)}, u32[]{:S(2)}) collective-permute-start(f32[128,512]{1,0:T(8,128)S(1)} %get-tuple-element.115), channel_id=1, source_target_pairs={{0,4},{4,0},{8,12},{12,8},{16,20},{20,16},{24,28},{28,24},{1,5},{5... | collective-permute-start | bytes 786440 | tf_op jit(solution)/shard_map/ppermute | solution.py:235
  146.8 1.6 collective-permute-start.26
  153.5 15.0 %copy-start.3 = (f32[128,1280]{1,0:T(8,128)}, f32[128,1280]{1,0:T(8,128)S(1)}, u32[]{:S(2)}) copy-start(f32[128,1280]{1,0:T(8,128)S(1)} %get-tuple-element.123.refs_2_) | copy-start | bytes 1966084
  153.5 3.0 %collective-permute-start.32 = (f32[128,1280]{1,0:T(8,128)S(1)}, f32[128,1280]{1,0:T(8,128)S(1)}, u32[]{:S(2)}, u32[]{:S(2)}) collective-permute-start(f32[128,1280]{1,0:T(8,128)S(1)} %get-tuple-element.123.refs_2_), channel_id=1, source_target_pairs={{0,4},{4,0},{8,12},{12,8},{16,20},{20,16},{24,28},{28,24},{1,5},{5... | collective-permute-start | bytes 1966088 | tf_op jit(solution)/shard_map/ppermute | solution.py:235
  153.6 14.7 %collective-permute-start.30 = (f32[128,1024]{1,0:T(8,128)S(1)}, f32[128,1024]{1,0:T(8,128)S(1)}, u32[]{:S(2)}, u32[]{:S(2)}) collective-permute-start(f32[128,1024]{1,0:T(8,128)S(1)} %get-tuple-element.119), channel_id=1, source_target_pairs={{0,8},{4,12},{8,0},{12,4},{16,24},{20,28},{24,16},{28,20},{1,9},{5... | collective-permute-start | bytes 1572872 | tf_op jit(solution)/shard_map/ppermute | solution.py:420
  155.8 12.5 %collective-permute-start.31 = (f32[128,1024]{1,0:T(8,128)S(1)}, f32[128,1024]{1,0:T(8,128)S(1)}, u32[]{:S(2)}, u32[]{:S(2)}) collective-permute-start(f32[128,1024]{1,0:T(8,128)S(1)} %get-tuple-element.121.refs_2_), channel_id=1, source_target_pairs={{8,16},{12,20},{16,8},{20,12},{9,17},{13,21},{17,9},{21,13},{10,18... | collective-permute-start | bytes 1572872 | tf_op jit(solution)/shard_map/ppermute | solution.py:425
  156.5 16.7 %copy-start.18 = (s32[2,3]{1,0:T(2,128)S(1)}, s32[2,3]{1,0:T(2,128)}, u32[]{:S(2)}) copy-start(s32[2,3]{1,0:T(2,128)} %constant.106.clone) | copy-start | bytes 76
  156.6 15.7 %collective-permute-start.38 = (f32[256,256]{1,0:T(8,128)S(1)}, f32[256,256]{1,0:T(8,128)S(1)}, u32[]{:S(2)}, u32[]{:S(2)}) collective-permute-start(f32[256,256]{1,0:T(8,128)S(1)} %maximum_select_fusion), channel_id=1, source_target_pairs={{0,3},{1,2},{2,1},{3,0},{4,7},{5,6},{6,5},{7,4},{8,11},{9,10},{10,... | collective-permute-start | bytes 786440 | tf_op jit(solution)/shard_map/ppermute | solution.py:436
  158.0 21.3 %collective-permute-start.37 = (f32[256,256]{1,0:T(8,128)S(1)}, f32[256,256]{1,0:T(8,128)S(1)}, u32[]{:S(2)}, u32[]{:S(2)}) collective-permute-start(f32[256,256]{1,0:T(8,128)S(1)} %maximum_select_fusion), channel_id=1, source_target_pairs={{0,2},{1,3},{2,0},{3,1},{4,6},{5,7},{6,4},{7,5},{8,10},{9,11},{10,... | collective-permute-start | bytes 786440 | tf_op jit(solution)/shard_map/ppermute | solution.py:436
  161.2 18.2 %collective-permute-start.36 = (f32[256,256]{1,0:T(8,128)S(1)}, f32[256,256]{1,0:T(8,128)S(1)}, u32[]{:S(2)}, u32[]{:S(2)}) collective-permute-start(f32[256,256]{1,0:T(8,128)S(1)} %maximum_select_fusion), channel_id=1, source_target_pairs={{0,1},{1,0},{2,3},{3,2},{4,5},{5,4},{6,7},{7,6},{8,9},{9,8},{10,11... | collective-permute-start | bytes 786440 | tf_op jit(solution)/shard_map/ppermute | solution.py:436
  168.5 15.5 %copy-start.7 = (f32[128,1024]{1,0:T(8,128)}, f32[128,1024]{1,0:T(8,128)S(1)}, u32[]{:S(2)}) copy-start(f32[128,1024]{1,0:T(8,128)S(1)} %get-tuple-element.124.refs_2_) | copy-start | bytes 1572868
  168.5 15.4 %collective-permute-start.34 = (f32[128,1024]{1,0:T(8,128)S(1)}, f32[128,1024]{1,0:T(8,128)S(1)}, u32[]{:S(2)}, u32[]{:S(2)}) collective-permute-start(f32[128,1024]{1,0:T(8,128)S(1)} %get-tuple-element.125), channel_id=1, source_target_pairs={{0,8},{4,12},{8,0},{12,4},{16,24},{20,28},{24,16},{28,20},{1,9},{5... | collective-permute-start | bytes 1572872 | tf_op jit(solution)/shard_map/ppermute | solution.py:420
  172.2 11.7 %collective-permute-start.33 = (f32[128,1024]{1,0:T(8,128)S(1)}, f32[128,1024]{1,0:T(8,128)S(1)}, u32[]{:S(2)}, u32[]{:S(2)}) collective-permute-start(f32[128,1024]{1,0:T(8,128)S(1)} %get-tuple-element.124.refs_2_), channel_id=1, source_target_pairs={{0,4},{4,0},{8,12},{12,8},{16,20},{20,16},{24,28},{28,24},{1,5},{5... | collective-permute-start | bytes 1572872 | tf_op jit(solution)/shard_map/ppermute | solution.py:235
  172.2 11.7 %collective-permute-start.35 = (f32[128,1024]{1,0:T(8,128)S(1)}, f32[128,1024]{1,0:T(8,128)S(1)}, u32[]{:S(2)}, u32[]{:S(2)}) collective-permute-start(f32[128,1024]{1,0:T(8,128)S(1)} %get-tuple-element.126.refs_1_), channel_id=1, source_target_pairs={{8,16},{12,20},{16,8},{20,12},{9,17},{13,21},{17,9},{21,13},{10,18... | collective-permute-start | bytes 1572872 | tf_op jit(solution)/shard_map/ppermute | solution.py:425
  179.5 11.0 %copy-start.16 = (s32[4,6]{1,0:T(4,128)S(1)}, s32[4,6]{1,0:T(4,128)}, u32[]{:S(2)}) copy-start(s32[4,6]{1,0:T(4,128)} %constant.103.clone) | copy-start | bytes 292
  179.5 11.0 %copy-start.17 = (s32[4,6]{1,0:T(4,128)S(1)}, s32[4,6]{1,0:T(4,128)}, u32[]{:S(2)}) copy-start(s32[4,6]{1,0:T(4,128)} %constant.102.clone) | copy-start | bytes 292
  179.5 11.5 %copy-start = (f32[3,256,256]{2,1,0:T(8,128)S(1)}, f32[3,256,256]{2,1,0:T(8,128)}, u32[]{:S(2)}) copy-start(f32[3,256,256]{2,1,0:T(8,128)} %refs_6_.3) | copy-start | bytes 2359300
  185.1 0.8 copy-start.11
  185.9 5.1 %collective-permute-start.40 = (f32[128,1024]{1,0:T(8,128)}, f32[128,1024]{1,0:T(8,128)}, u32[]{:S(2)}, u32[]{:S(2)}) collective-permute-start(f32[128,1024]{1,0:T(8,128)} %get-tuple-element.130.refs_4_), channel_id=1, source_target_pairs={{0,4},{4,0},{8,12},{12,8},{16,20},{20,16},{24,28},{28,24},{1,5},{5... | collective-permute-start | bytes 1572872 | tf_op jit(solution)/shard_map/ppermute | solution.py:235
  185.9 26.2 %collective-permute-start.39 = (f32[128,1024]{1,0:T(8,128)}, f32[128,1024]{1,0:T(8,128)}, u32[]{:S(2)}, u32[]{:S(2)}) collective-permute-start(f32[128,1024]{1,0:T(8,128)} %get-tuple-element.128), channel_id=1, source_target_pairs={{0,8},{4,12},{8,0},{12,4},{16,24},{20,28},{24,16},{28,20},{1,9},{5... | collective-permute-start | bytes 1572872 | tf_op jit(solution)/shard_map/ppermute | solution.py:420
  191.0 1.0 copy-start.2
  192.0 1.1 copy-start.4
  193.1 19.0 %copy-start.12 = (f32[128,1024]{1,0:T(8,128)S(1)}, f32[128,1024]{1,0:T(8,128)}, u32[]{:S(2)}) copy-start(f32[128,1024]{1,0:T(8,128)} %copy-done.11) | copy-start | bytes 1572868
  193.1 22.1 %copy-start.6 = (f32[128,1024]{1,0:T(8,128)S(1)}, f32[128,1024]{1,0:T(8,128)}, u32[]{:S(2)}) copy-start(f32[128,1024]{1,0:T(8,128)} %copy-done.5) | copy-start | bytes 1572868
  193.1 22.1 %copy-start.8 = (f32[128,1024]{1,0:T(8,128)S(1)}, f32[128,1024]{1,0:T(8,128)}, u32[]{:S(2)}) copy-start(f32[128,1024]{1,0:T(8,128)} %copy-done.7) | copy-start | bytes 1572868
  213.2 2.0 collective-permute-start.41
